TPU v7x, 32 devices: a whole 2x2x4 slice. The times are simulated.
32 devices in a mesh: groups: 2 (over y), dev: 4 (over z), view: 2 (over x), chip: 2 (over core).
Axes of the slice: x: 2, y: 2, z: 4, core: 2. Of those that a mesh axis runs over, the one named last changes fastest.
Arguments:
- params: float32 [58, 32768], P(None, ('groups', 'dev')), parts along dimension 1
- cameras: float32 [4, 2, 4], P(('groups', 'view')), parts along dimension 0
- view_basis: float32 [4, 16], P(('groups', 'view')), parts along dimension 0, may hold values from -0.6 to 0.6
- tile_lists: int32 [2, 8, 2, 16], P('view', ('groups', 'dev'), 'chip'), parts along dimension 1, may hold values from 0 to 127, as said below
- margin_blocks: int32 [2, 8, 2, 16, 256], P('view', ('groups', 'dev'), 'chip'), parts along dimension 1, may hold values from 0 to 3839, as said below
- depth_orders: int32 [2, 8, 2, 16, 256], P('view', ('groups', 'dev'), 'chip'), parts along dimension 1, may hold values from 0 to 255, as said below
- tile_counts: int32 [2, 8, 2, 16], P('view', ('groups', 'dev'), 'chip'), parts along dimension 1, may hold values from 0 to 256, as said below
- requests: int32 [2, 4, 2, 8, 960], P('view', None, 'chip', ('groups', 'dev')), parts along dimension 3, may hold values from 0 to 4095, as said below
- target: float32 [2, 8, 2, 16, 3, 256], P('view', ('groups', 'dev'), 'chip'), parts along dimension 1, may hold values from -3 to 3
Outputs:
- grads: float32 [58, 32768], P(None, ('groups', 'dev', 'view', 'chip')), parts along dimension 1
- images: float32 [2, 8, 2, 16, 3, 256], P('view', ('groups', 'dev'), 'chip'), parts along dimension 1
There are 2 independent parts, one for each index of `groups`. A program takes and returns all parts, laid end to end along the dimension named above; each array names one. Nothing has to cross between parts.
Inputs may be any that keep to these rules, and one draw needn't show every extreme that they name: `tile_lists`: each view's tiles are a permutation of 0 .. 127, 16 to a device. `margin_blocks`: every live entry names a slot that no other live entry of the same device names; a tile's live Gaussians lie near it on the image; dead entries hold 0. `depth_orders`: each row is a permutation of 0 .. 255 whose first tile_counts entries are the live entries of the block. `tile_counts`: live entries come first in depth order; some tile of every draw is full. `requests`: local Gaussian indices; slots that no live entry of the receiving device names hold 0; for some receiving device some shard fills all 960 slots.
All inputs are finite; a program needn't handle non-finite values.
Results may differ from a plain program's by a relative error of at most 0.0003.
Values sent between devices are 32-bit elements; how exact they have to be, the bound alone decides.
No kernel may reach another device: no remote copies, remote signals or barrier semaphores. Data moves between devices by JAX's collectives and lax.ppermute only.
A program may use at most 64 MiB of HBM per device.

v0:
```python
from functools import partial

import jax
import jax.numpy as jnp
from jax import lax
from jax.sharding import PartitionSpec as P

SIDE = 16
PIXELS = 256
TW = 16


dilation = 0.3


def project(columns, camera, basis):
    highest = lax.Precision.HIGHEST
    linear = camera[:, 0:3]
    means = jnp.dot(linear, columns[0:3], precision=highest) + camera[:, 3][:, None]
    diag_x = columns[3]
    cross_yx = columns[4]
    diag_y = columns[5]
    cross_zx = columns[6]
    cross_zy = columns[7]
    diag_z = columns[8]
    world_xx = diag_x * diag_x
    world_xy = diag_x * cross_yx
    world_xz = diag_x * cross_zx
    world_yy = cross_yx * cross_yx + diag_y * diag_y
    world_yz = cross_yx * cross_zx + diag_y * cross_zy
    world_zz = cross_zx * cross_zx + cross_zy * cross_zy + diag_z * diag_z
    world = jnp.stack(
        [
            jnp.stack([world_xx, world_xy, world_xz]),
            jnp.stack([world_xy, world_yy, world_yz]),
            jnp.stack([world_xz, world_yz, world_zz]),
        ]
    )
    halfway = jnp.einsum("ij,jkn->ikn", linear, world, precision=highest)
    screen = jnp.einsum("ikn,lk->iln", halfway, linear, precision=highest)
    upper = screen[0, 0] + dilation
    cross = screen[0, 1]
    lower = screen[1, 1] + dilation
    determinant = upper * lower - cross * cross
    opacity = jax.nn.sigmoid(columns[9])
    harmonics = columns[10:].reshape(3, basis.shape[0], columns.shape[1])
    colour = jnp.einsum("k,ckn->cn", basis, harmonics, precision=highest) + 0.5
    shape_rows = jnp.stack(
        [lower / determinant, -cross / determinant, upper / determinant, opacity]
    )
    return jnp.concatenate([means, shape_rows, colour], axis=0)


def tile_pixels(tile_id):
    within = jnp.arange(PIXELS, dtype=jnp.int32)
    column = tile_id % TW * SIDE + within % SIDE
    row_index = tile_id // TW * SIDE + within // SIDE
    return (column.astype(jnp.float32) + 0.5, row_index.astype(jnp.float32) + 0.5)


def render(values, live_mask, across, downward):
    offset_x = across[None, :] - values[0][:, None]
    offset_y = downward[None, :] - values[1][:, None]
    quadric = 0.5 * (
        values[2][:, None] * offset_x * offset_x
        + 2.0 * values[3][:, None] * offset_x * offset_y
        + values[4][:, None] * offset_y * offset_y
    )
    alpha = (live_mask * values[5])[:, None] * jnp.exp(-quadric)
    logs = jnp.log1p(-alpha)
    before = jnp.exp(jnp.cumsum(logs, axis=0) - logs)
    return jnp.dot(values[6:9], before * alpha, precision=lax.Precision.HIGHEST)


def tile_step(features_all, slot_ids, ordering, live_count, tile_id, target_tile):
    ordered = jnp.take(slot_ids, ordering)
    live_mask = (jnp.arange(ordering.shape[0], dtype=jnp.int32) < live_count).astype(jnp.float32)
    gathered = jnp.take(features_all, ordered, axis=1)
    across, downward = tile_pixels(tile_id)
    image, pullback = jax.vjp(lambda values: render(values, live_mask, across, downward), gathered)
    cotangent = pullback(image - target_tile)[0]
    return (image, cotangent, ordered)


def local(
    params,
    cameras,
    view_basis,
    tile_lists,
    margin_blocks,
    depth_orders,
    tile_counts,
    requests,
    target,
):
    camera = cameras[0]
    basis = view_basis[0]
    wanted = requests[0, :, 0, 0, :].reshape(-1)
    slot_total = wanted.shape[0]
    picked = jnp.take(params, wanted, axis=1)
    arrived = lax.all_to_all(picked, "dev", split_axis=1, concat_axis=1, tiled=True)
    features_all = project(arrived, camera, basis)
    tiles_here = tile_lists.shape[3]
    entries = margin_blocks.shape[4]
    halves = tiles_here // 2
    grouped = (
        margin_blocks[0, 0, 0].reshape(halves, 2, entries),
        depth_orders[0, 0, 0].reshape(halves, 2, entries),
        tile_counts[0, 0, 0].reshape(halves, 2),
        tile_lists[0, 0, 0].reshape(halves, 2),
        target[0, 0, 0].reshape(halves, 2, 3, target.shape[5]),
    )

    def two_tiles(inputs):
        return jax.vmap(partial(tile_step, features_all))(*inputs)

    images, cotangents, ordered = lax.map(two_tiles, grouped)
    flat_grads = jnp.swapaxes(cotangents.reshape(tiles_here, 9, entries), 1, 2).reshape(
        tiles_here * entries, 9
    )
    slot_grad = jax.ops.segment_sum(flat_grads, ordered.reshape(tiles_here * entries), slot_total).T
    shard_width = params.shape[1]
    pullback = jax.vjp(lambda columns: project(columns, camera, basis), arrived)[1]
    row_grad = lax.all_to_all(
        pullback(slot_grad)[0], "dev", split_axis=1, concat_axis=1, tiled=True
    )
    local_grad = jax.ops.segment_sum(row_grad.T, wanted, shard_width).T
    grads = lax.psum_scatter(local_grad, ("view", "chip"), scatter_dimension=1, tiled=True)
    return (grads, images.reshape(target.shape))


def solution(mesh):
    return jax.shard_map(
        local,
        mesh=mesh,
        in_specs=(
            P(None, ("groups", "dev")),
            P(("groups", "view"), None, None),
            P(("groups", "view"), None),
            P("view", ("groups", "dev"), "chip", None),
            P("view", ("groups", "dev"), "chip", None, None),
            P("view", ("groups", "dev"), "chip", None, None),
            P("view", ("groups", "dev"), "chip", None),
            P("view", None, "chip", ("groups", "dev"), None),
            P("view", ("groups", "dev"), "chip", None, None, None),
        ),
        out_specs=(
            P(None, ("groups", "dev", "view", "chip")),
            P("view", ("groups", "dev"), "chip", None, None, None),
        ),
        check_vma=False,
    )
```

profile of v0, /device:TPU:0, one launch (start us, length us, event | category | flops | bytes accessed | tf_op | source)
XLA Modules:
  0.0 370.5 jit_solution(5595678414629761168)
XLA Ops:
  8.8 1.9 copy.108
  10.7 7.9 %gather_fusion.2 = f32[3840,58]{1,0:T(8,128)} fusion(f32[58,4096]{0,1:T(8,128)S(1)} %copy.108, s32[4096]{0:T(1024)S(1)} %pad_clamp_fusion.1), kind=kCustom, calls=%fused_computation.2 | custom fusion | bytes 1797120 | tf_op jit(solution)/shard_map/jit(_take)/gather | solution.py:100
  18.6 2.2 copy.109
  20.8 1.1 broadcast_select_fusion
  21.9 6.3 %all-to-all-start = ((f32[58,4,960]{2,0,1:T(8,128)}), f32[58,4,960]{2,0,1:T(8,128)S(1)}, u32[]{:S(2)}, u32[]{:S(2)}) async-start(f32[58,4,960]{2,0,1:T(8,128)} %broadcast_select_fusion), calls=%async_computation | async-start | bytes 2097152 | tf_op jit(solution)/shard_map/all_to_all | solution.py:101
  30.6 23.4 %all-to-all-done = f32[58,4,960]{2,0,1:T(8,128)S(1)} async-done(((f32[58,4,960]{2,0,1:T(8,128)}), f32[58,4,960]{2,0,1:T(8,128)S(1)}, u32[]{:S(2)}, u32[]{:S(2)}) %all-to-all-start) | async-done | bytes 890912 | tf_op jit(solution)/shard_map/all_to_all | solution.py:101
  59.0 1.9 copy.116
  60.9 184.4 %while.17 = (s32[]{:T(128)}, f32[8,2,3,256]{3,2,1,0:T(4,128)S(1)}, f32[8,2,9,256]{3,2,1,0:T(8,128)S(1)}, s32[8,2,256]{2,1,0:T(2,128)S(1)}, s32[8,2,256]{2,1,0:T(...) while((s32[]{:T(128)}, f32[8,2,3,256]{3,2,1,0:T(4,128)S(1)}, ...), condition=%wide.region_11.12_spmd, body=%wide.region_0.11_spmd.sunk | while | flops 64161844 | bytes 16846108 | solution.py:117
  61.0 4.8 %gather_fusion = s32[512]{0:T(512)S(1)} fusion(s32[2,256]{1,0:T(2,128)S(1)} %dynamic-slice_bitcast_fusion.2, s32[512]{0:T(512)S(1)} %bitcast.290), kind=kCustom, calls=%fused_computation.1.clone.1 | custom fusion | bytes 8192 | tf_op jit(solution)/shard_map/while/body/eval_jaxpr/vmap(jit(_take))/gather | solution.py:76
  66.2 2.6 gather_fusion.1
  69.9 1.9 fusion.141
  72.9 1.1 bitcast_dynamic-update-slice_fusion.4
  75.1 1.3 fusion.142
  76.4 4.6 %fusion.143 = f32[2,256,2,128]{1,2,3,0:T(2,128)S(1)} fusion(f32[2,256,2,128]{1,3,2,0:T(8,128)S(1)} %bitcast.291), kind=kOutput, calls=%fused_computation.68.clone.1 | output fusion | flops 16646144 | bytes 1048576 | tf_op jit(solution)/shard_map/reduce-window.18
  84.1 4.8 %gather_fusion = s32[512]{0:T(512)S(1)} fusion(s32[2,256]{1,0:T(2,128)S(1)} %dynamic-slice_bitcast_fusion.2, s32[512]{0:T(512)S(1)} %bitcast.290), kind=kCustom, calls=%fused_computation.1.clone.1 | custom fusion | bytes 8192 | tf_op jit(solution)/shard_map/while/body/eval_jaxpr/vmap(jit(_take))/gather | solution.py:76
  89.2 2.6 gather_fusion.1
  92.9 1.9 fusion.141
  95.9 1.1 bitcast_dynamic-update-slice_fusion.4
  98.1 1.3 fusion.142
  99.4 4.6 %fusion.143 = f32[2,256,2,128]{1,2,3,0:T(2,128)S(1)} fusion(f32[2,256,2,128]{1,3,2,0:T(8,128)S(1)} %bitcast.291), kind=kOutput, calls=%fused_computation.68.clone.1 | output fusion | flops 16646144 | bytes 1048576 | tf_op jit(solution)/shard_map/reduce-window.18
  107.1 4.8 %gather_fusion = s32[512]{0:T(512)S(1)} fusion(s32[2,256]{1,0:T(2,128)S(1)} %dynamic-slice_bitcast_fusion.2, s32[512]{0:T(512)S(1)} %bitcast.290), kind=kCustom, calls=%fused_computation.1.clone.1 | custom fusion | bytes 8192 | tf_op jit(solution)/shard_map/while/body/eval_jaxpr/vmap(jit(_take))/gather | solution.py:76
  112.2 2.6 gather_fusion.1
  116.0 1.9 fusion.141
  118.9 1.1 bitcast_dynamic-update-slice_fusion.4
  121.1 1.3 fusion.142
  122.4 4.6 %fusion.143 = f32[2,256,2,128]{1,2,3,0:T(2,128)S(1)} fusion(f32[2,256,2,128]{1,3,2,0:T(8,128)S(1)} %bitcast.291), kind=kOutput, calls=%fused_computation.68.clone.1 | output fusion | flops 16646144 | bytes 1048576 | tf_op jit(solution)/shard_map/reduce-window.18
  130.1 4.8 %gather_fusion = s32[512]{0:T(512)S(1)} fusion(s32[2,256]{1,0:T(2,128)S(1)} %dynamic-slice_bitcast_fusion.2, s32[512]{0:T(512)S(1)} %bitcast.290), kind=kCustom, calls=%fused_computation.1.clone.1 | custom fusion | bytes 8192 | tf_op jit(solution)/shard_map/while/body/eval_jaxpr/vmap(jit(_take))/gather | solution.py:76
  135.2 2.6 gather_fusion.1
  139.0 1.9 fusion.141
  141.9 1.1 bitcast_dynamic-update-slice_fusion.4
  144.1 1.3 fusion.142
  145.4 4.6 %fusion.143 = f32[2,256,2,128]{1,2,3,0:T(2,128)S(1)} fusion(f32[2,256,2,128]{1,3,2,0:T(8,128)S(1)} %bitcast.291), kind=kOutput, calls=%fused_computation.68.clone.1 | output fusion | flops 16646144 | bytes 1048576 | tf_op jit(solution)/shard_map/reduce-window.18
  153.1 4.8 %gather_fusion = s32[512]{0:T(512)S(1)} fusion(s32[2,256]{1,0:T(2,128)S(1)} %dynamic-slice_bitcast_fusion.2, s32[512]{0:T(512)S(1)} %bitcast.290), kind=kCustom, calls=%fused_computation.1.clone.1 | custom fusion | bytes 8192 | tf_op jit(solution)/shard_map/while/body/eval_jaxpr/vmap(jit(_take))/gather | solution.py:76
  158.2 2.6 gather_fusion.1
  162.0 1.9 fusion.141
  165.0 1.1 bitcast_dynamic-update-slice_fusion.4
  167.2 1.3 fusion.142
  168.4 4.6 %fusion.143 = f32[2,256,2,128]{1,2,3,0:T(2,128)S(1)} fusion(f32[2,256,2,128]{1,3,2,0:T(8,128)S(1)} %bitcast.291), kind=kOutput, calls=%fused_computation.68.clone.1 | output fusion | flops 16646144 | bytes 1048576 | tf_op jit(solution)/shard_map/reduce-window.18
  176.1 4.8 %gather_fusion = s32[512]{0:T(512)S(1)} fusion(s32[2,256]{1,0:T(2,128)S(1)} %dynamic-slice_bitcast_fusion.2, s32[512]{0:T(512)S(1)} %bitcast.290), kind=kCustom, calls=%fused_computation.1.clone.1 | custom fusion | bytes 8192 | tf_op jit(solution)/shard_map/while/body/eval_jaxpr/vmap(jit(_take))/gather | solution.py:76
  181.3 2.6 gather_fusion.1
  185.0 1.9 fusion.141
  188.0 1.1 bitcast_dynamic-update-slice_fusion.4
  190.2 1.3 fusion.142
  191.5 4.6 %fusion.143 = f32[2,256,2,128]{1,2,3,0:T(2,128)S(1)} fusion(f32[2,256,2,128]{1,3,2,0:T(8,128)S(1)} %bitcast.291), kind=kOutput, calls=%fused_computation.68.clone.1 | output fusion | flops 16646144 | bytes 1048576 | tf_op jit(solution)/shard_map/reduce-window.18
  199.2 4.8 %gather_fusion = s32[512]{0:T(512)S(1)} fusion(s32[2,256]{1,0:T(2,128)S(1)} %dynamic-slice_bitcast_fusion.2, s32[512]{0:T(512)S(1)} %bitcast.290), kind=kCustom, calls=%fused_computation.1.clone.1 | custom fusion | bytes 8192 | tf_op jit(solution)/shard_map/while/body/eval_jaxpr/vmap(jit(_take))/gather | solution.py:76
  204.3 2.6 gather_fusion.1
  208.0 1.9 fusion.141
  211.0 1.1 bitcast_dynamic-update-slice_fusion.4
  213.2 1.3 fusion.142
  214.5 4.6 %fusion.143 = f32[2,256,2,128]{1,2,3,0:T(2,128)S(1)} fusion(f32[2,256,2,128]{1,3,2,0:T(8,128)S(1)} %bitcast.291), kind=kOutput, calls=%fused_computation.68.clone.1 | output fusion | flops 16646144 | bytes 1048576 | tf_op jit(solution)/shard_map/reduce-window.18
  222.2 4.8 %gather_fusion = s32[512]{0:T(512)S(1)} fusion(s32[2,256]{1,0:T(2,128)S(1)} %dynamic-slice_bitcast_fusion.2, s32[512]{0:T(512)S(1)} %bitcast.290), kind=kCustom, calls=%fused_computation.1.clone.1 | custom fusion | bytes 8192 | tf_op jit(solution)/shard_map/while/body/eval_jaxpr/vmap(jit(_take))/gather | solution.py:76
  227.3 2.6 gather_fusion.1
  231.1 1.9 fusion.141
  234.0 1.1 bitcast_dynamic-update-slice_fusion.4
  236.2 1.3 fusion.142
  237.5 4.6 %fusion.143 = f32[2,256,2,128]{1,2,3,0:T(2,128)S(1)} fusion(f32[2,256,2,128]{1,3,2,0:T(8,128)S(1)} %bitcast.291), kind=kOutput, calls=%fused_computation.68.clone.1 | output fusion | flops 16646144 | bytes 1048576 | tf_op jit(solution)/shard_map/reduce-window.18
  245.3 2.0 copy.117
  247.3 23.5 %scatter_custom_fusion = f32[3840,9]{1,0:T(8,128)S(1)} fusion(s32[4096]{0:T(1024)S(1)} %bitcast.326, f32[4096,9]{1,0:T(8,128)} %bitcast.297, f32[]{:T(128)} %constant.216.clone.1), kind=kCustom, calls=%fused_computation.153 | custom fusion | flops 36864 | bytes 138752 | tf_op jit(solution)/shard_map/scatter-add | solution.py:121
  274.5 1.5 copy.120
  276.0 3.5 all-to-all-start.1
  279.7 25.1 %all-to-all-done.1 = f32[58,4,960]{2,0,1:T(8,128)S(1)} async-done(((f32[58,4,960]{2,0,1:T(8,128)}), f32[58,4,960]{2,0,1:T(8,128)S(1)}, u32[]{:S(2)}, u32[]{:S(2)}) %all-to-all-start.1) | async-done | bytes 890912 | tf_op jit(solution)/shard_map/all_to_all | solution.py:124
  306.9 24.1 %scatter_custom_fusion.1 = f32[4096,58]{1,0:T(8,128)} fusion(s32[3840]{0:T(1024)S(1)} %reshape.1196, f32[3840,58]{1,0:T(8,128)S(1)} %copy.122, f32[]{:T(128)} %constant.216.clone.1), kind=kCustom, calls=%fused_computation.150 | custom fusion | flops 222720 | bytes 950276 | tf_op jit(solution)/shard_map/scatter-add | solution.py:127
  331.6 30.1 %reduce-scatter.2.cloned.1.call-done = f32[58,1024]{0,1:T(8,128)} async-done(((f32[58,4096]{0,1:T(8,128)}), f32[58,1024]{0,1:T(8,128)}) %reduce-scatter.2.cloned.1.call-update) | async-done | bytes 237584 | tf_op jit(solution)/shard_map/reduce_scatter | solution.py:128
  361.7 1.9 copy.124
  (551 shorter events, 67.0 us)
Async XLA Ops:
  20.8 8.0 %copy-start.5 = (s32[1,1,1,16]{3,2,1,0:T(1,128)S(1)}, s32[1,1,1,16]{3,2,1,0:T(1,128)}, u32[]{:S(2)}) copy-start(s32[1,1,1,16]{3,2,1,0:T(1,128)} %param.14) | copy-start | bytes 196
  20.8 8.7 %copy-start.6 = (s32[1,1,1,16]{3,2,1,0:T(1,128)S(1)}, s32[1,1,1,16]{3,2,1,0:T(1,128)}, u32[]{:S(2)}) copy-start(s32[1,1,1,16]{3,2,1,0:T(1,128)} %param.17) | copy-start | bytes 196
  20.8 9.5 %copy-start.2 = (s32[1,1,1,16,256]{4,3,2,1,0:T(8,128)S(1)}, s32[1,1,1,16,256]{4,3,2,1,0:T(8,128)}, u32[]{:S(2)}) copy-start(s32[1,1,1,16,256]{4,3,2,1,0:T(8,128)} %param.15) | copy-start | bytes 49156
  20.8 9.5 %copy-start.3 = (s32[1,1,1,16,256]{4,3,2,1,0:T(8,128)S(1)}, s32[1,1,1,16,256]{4,3,2,1,0:T(8,128)}, u32[]{:S(2)}) copy-start(s32[1,1,1,16,256]{4,3,2,1,0:T(8,128)} %param.16) | copy-start | bytes 49156
  20.8 9.5 %copy-start = (f32[1,1,1,16,3,256]{5,3,4,2,1,0:T(8,128)S(1)}, f32[1,1,1,16,3,256]{5,3,4,2,1,0:T(8,128)}, u32[]{:S(2)}) copy-start(f32[1,1,1,16,3,256]{5,3,4,2,1,0:T(8,128)} %param.19) | copy-start | bytes 147460
  20.8 9.6 %copy-start.1 = (f32[1,2,4]{2,1,0:T(2,128)S(1)}, f32[1,2,4]{2,1,0:T(2,128)}, u32[]{:S(2)}) copy-start(f32[1,2,4]{2,1,0:T(2,128)} %param.12) | copy-start | bytes 100
  21.9 32.0 %all-to-all-start = ((f32[58,4,960]{2,0,1:T(8,128)}), f32[58,4,960]{2,0,1:T(8,128)S(1)}, u32[]{:S(2)}, u32[]{:S(2)}) async-start(f32[58,4,960]{2,0,1:T(8,128)} %broadcast_select_fusion), calls=%async_computation | async-start | bytes 2097152 | tf_op jit(solution)/shard_map/all_to_all | solution.py:101
  54.2 2.3 copy-start.4
  276.0 28.8 %all-to-all-start.1 = ((f32[58,4,960]{2,0,1:T(8,128)}), f32[58,4,960]{2,0,1:T(8,128)S(1)}, u32[]{:S(2)}, u32[]{:S(2)}) async-start(f32[58,4,960]{2,0,1:T(8,128)} %copy.120), calls=%async_computation.1 | async-start | bytes 2097152 | tf_op jit(solution)/shard_map/all_to_all | solution.py:124
  279.5 82.2 %reduce-scatter.2.cloned.1.call-start = ((), (), s32[]{:S(2)}) async-start(), calls=%async_computation.3 | async-start | bytes 2621440 | tf_op jit(solution)/shard_map/reduce_scatter | solution.py:128
Sparse Core Ops, SparseCore 0:
  331.1 30.5 reduce-scatter.1
where the time goes:
time: 371 us; the launch traced here: 370 us
  other arithmetic  125 us (34%)
  local copies, waits for them, and re-layouts  111 us (30%)
  waiting for transfers between devices  78.6 us (21%)
  matrix products  28.9 us (8%)
  between operations  14.4 us (4%)
  starting transfers between devices  9.87 us (3%)
    another operation x48, other arithmetic  55.4 us
    gather x32, local copies, waits for them, and re-layouts, tile_step(): ordered = jnp.take(slot_ids, ordering)  39.1 us
    reduce_scatter x1, waiting for transfers between devices, local(): lax.psum_scatter(local_grad, ('view', 'chip'), scatter_dimension=1, tiled...  30.1 us
    dot_general x24, matrix products, render(): return jnp.dot(values[6:9], before * alpha, precision=lax.Precision.HIGHEST)  26.1 us
    all_to_all x1, waiting for transfers between devices, local(): lax.all_to_all(pullback(slot_grad)[0], 'dev', split_axis=1, concat_axis=1...  25.1 us
    scatter-add x1, other arithmetic, local(): local_grad = jax.ops.segment_sum(row_grad.T, wanted, shard_width).T  24.1 us
    scatter-add x1, other arithmetic, local(): jax.ops.segment_sum(flat_grads, ordered.reshape(tiles_here * entries), sl...  23.5 us
    all_to_all x1, waiting for transfers between devices, local(): lax.all_to_all(picked, 'dev', split_axis=1, concat_axis=1, tiled=True)  23.4 us
  transfers between devices with their start and end apart: 3, of which 3 were waited for; matrix products, arithmetic and copies ran while one was open for 1% of the time, Pallas kernels for 0%

commit v1 on v0

v1 whole, which is shorter than its diff:
```python
from functools import partial

import jax
import jax.numpy as jnp
from jax import lax
from jax.experimental import pallas as pl
from jax.experimental.pallas import tpu as pltpu
from jax.sharding import PartitionSpec as P

SIDE = 16
TW = 16
LANES = 128
LOG2E = 1.4426950408889634
LN2 = 0.6931471805599453
DILATION = 0.3
DEAD = -1e30
F32 = jnp.float32
BF16 = jnp.bfloat16
FEATS = 9


def lane_take(row, index):
    return jnp.take_along_axis(row, index, axis=1, mode="promise_in_bounds")


def split2(x):
    hi = x.astype(BF16)
    return hi, (x - hi.astype(F32)).astype(BF16)


def dot(a, b, ca, cb):
    return lax.dot_general(a, b, (((ca,), (cb,)), ((), ())), preferred_element_type=F32)


def send_kernel(me_ref, cam_ref, basis_ref, params_ref, req_ref, *refs, nd, cap, rows):
    outs = refs[:nd]
    idx_out, w_out, feat, w_scr = refs[nd:]
    me = me_ref[0]
    width = params_ref.shape[1]
    coefs = basis_ref.shape[-1]
    idx_out[...] = jnp.zeros_like(idx_out)
    for j in range(nd):
        dest = lax.rem(me + j, nd)
        for i in range(rows):
            size = min(LANES, cap - i * LANES)
            idx_out[j * rows + i : j * rows + i + 1, 0:size] = req_ref[
                0, dest, 0, 0:1, i * LANES : i * LANES + size
            ]
    w_scr[...] = jnp.zeros_like(w_scr)
    w_scr[0:2, 0:4] = cam_ref[0]
    w_scr[2:3, 0:coefs] = basis_ref[...]
    packed = w_scr[...]
    lane8 = lax.broadcasted_iota(jnp.int32, (8, LANES), 1)
    row8 = lax.broadcasted_iota(jnp.int32, (8, LANES), 0)
    basis_row = jnp.broadcast_to(packed[2:3, :], (8, LANES))
    camera_row = jnp.where((row8 < 2), packed, 0.0)
    at10 = pltpu.roll(basis_row, 10, 1)
    w_out[...] = camera_row + jnp.where(row8 == 0, at10, 0.0)
    weights = jnp.where(lane8 < 3, camera_row, 0.0)
    weights = weights + jnp.where(row8 == 2, at10, 0.0)
    weights = weights + jnp.where(row8 == 3, pltpu.roll(basis_row, 10 + coefs, 1), 0.0)
    weights = weights + jnp.where(row8 == 4, pltpu.roll(basis_row, 10 + 2 * coefs, 1), 0.0)
    w_scr[...] = weights
    linear = lax.dot_general(
        w_scr[:, 0 : params_ref.shape[0]],
        params_ref[...],
        (((1,), (0,)), ((), ())),
        precision=lax.Precision.HIGHEST,
        preferred_element_type=F32,
    )

    def cam(i, j):
        return cam_ref[0, i : i + 1, j : j + 1]

    def row(i):
        return params_ref[i : i + 1, :]

    lx, lyx, ly, lzx, lzy, lz = [row(i) for i in range(3, 9)]
    m = []
    for i in range(2):
        a0, a1, a2 = cam(i, 0), cam(i, 1), cam(i, 2)
        m.append((a0 * lx + a1 * lyx + a2 * lzx, a1 * ly + a2 * lzy, a2 * lz))
    upper = m[0][0] * m[0][0] + m[0][1] * m[0][1] + m[0][2] * m[0][2] + DILATION
    cross = m[0][0] * m[1][0] + m[0][1] * m[1][1] + m[0][2] * m[1][2]
    lower = m[1][0] * m[1][0] + m[1][1] * m[1][1] + m[1][2] * m[1][2] + DILATION
    inverse = 1.0 / (upper * lower - cross * cross)
    logit = row(9)
    log_opacity = jnp.minimum(logit, 0.0) * LOG2E - LOG2E * jnp.log(1.0 + jnp.exp(-jnp.abs(logit)))
    feat[0:1, :] = linear[0:1, :] + cam(0, 3)
    feat[1:2, :] = linear[1:2, :] + cam(1, 3)
    feat[2:3, :] = lower * inverse * (0.5 * LOG2E)
    feat[3:4, :] = -cross * inverse * LOG2E
    feat[4:5, :] = upper * inverse * (0.5 * LOG2E)
    feat[5:6, :] = log_opacity
    for c in range(3):
        feat[6 + c : 7 + c, :] = linear[2 + c : 3 + c, :] + 0.5

    total = nd * rows
    step = 8 if total % 8 == 0 else total
    source_rows = width // LANES
    for first in range(0, total, step):
        index = idx_out[first : first + step, :]
        low = index & (LANES - 1)
        high = index >> 7
        acc = [jnp.zeros((step, LANES), F32) for _ in range(FEATS)]
        for r in range(source_rows):
            here = high == r
            for f in range(FEATS):
                source = jnp.broadcast_to(feat[f : f + 1, r * LANES : (r + 1) * LANES], (step, LANES))
                acc[f] = jnp.where(here, lane_take(source, low), acc[f])
        for f in range(FEATS):
            for n in range(step):
                j, i = divmod(first + n, rows)
                if rows % step == 0:
                    if n == 0:
                        outs[j][f, i : i + step, :] = acc[f]
                else:
                    outs[j][f, i : i + 1, :] = acc[f][n : n + 1, :]


def vmem_spec():
    return pl.BlockSpec(memory_space=pltpu.VMEM)


def smem_spec():
    return pl.BlockSpec(memory_space=pltpu.SMEM)


def send(me, cameras, basis, params, requests, nd, cap, rows):
    return pl.pallas_call(
        partial(send_kernel, nd=nd, cap=cap, rows=rows),
        in_specs=[smem_spec()] + [vmem_spec()] * 4,
        out_specs=[vmem_spec()] * (nd + 2),
        out_shape=[jax.ShapeDtypeStruct((FEATS, rows, LANES), F32)] * nd
        + [
            jax.ShapeDtypeStruct((nd * rows, LANES), jnp.int32),
            jax.ShapeDtypeStruct((8, LANES), F32),
        ],
        scratch_shapes=[pltpu.VMEM((16, params.shape[1]), F32), pltpu.VMEM((8, LANES), F32)],
        compiler_params=pltpu.CompilerParams(vmem_limit_bytes=40 * 1024 * 1024),
        name="project_gather",
    )(me, cameras, basis, params, requests)


def scatter_products(value_rows, index_rows, spread, hot, out_rows):
    width = value_rows[0][0].shape[1]
    for n, (values, (high, low)) in enumerate(zip(value_rows, index_rows)):
        columns = slice(n * width, (n + 1) * width)
        high_iota = lax.broadcasted_iota(jnp.int32, (out_rows, width), 0)
        low_iota = lax.broadcasted_iota(jnp.int32, (LANES, width), 0)
        here = high_iota == high
        hot[:, columns] = jnp.where(low_iota == low, 1.0, 0.0).astype(BF16)
        for f in range(FEATS):
            hi, lo = split2(values[f])
            hi, lo = hi.astype(F32), lo.astype(F32)
            spread[f * out_rows : (f + 1) * out_rows, columns] = jnp.where(here, hi, 0.0).astype(BF16)
            base = (FEATS + f) * out_rows
            spread[base : base + out_rows, columns] = jnp.where(here, lo, 0.0).astype(BF16)


def render_kernel(me_ref, *refs, nd, cap, rows, tiles, entries):
    recv = refs[:nd]
    blocks_ref, orders_ref, counts_ref, ids_ref, target_ref = refs[nd : nd + 5]
    outs = refs[nd + 5 : 2 * nd + 5]
    (images_ref, coef, a_scr, t_scr, q_scr, whi_scr, wlo_scr, ghi_scr, glo_scr, g_rows, mom, spread, hot) = refs[
        2 * nd + 5 :
    ]
    me = me_ref[0]
    pixels = SIDE * SIDE
    chunk = entries // 8
    halves = entries // LANES
    table_rows = nd * rows

    place = lax.broadcasted_iota(jnp.int32, (tiles, entries), 1)
    rank = (place & 7) * chunk + (place >> 3)

    def take_wide(source, index):
        parts = []
        for c in range(halves):
            wanted = index[:, c * LANES : (c + 1) * LANES]
            low = wanted & (LANES - 1)
            high = wanted >> 7
            value = lane_take(source[:, 0:LANES], low)
            for h in range(1, halves):
                value = jnp.where(high == h, lane_take(source[:, h * LANES : (h + 1) * LANES], low), value)
            parts.append(value)
        return jnp.concatenate(parts, axis=1)

    def put(ref, at, value):
        for h in range(halves):
            ref[h, at : at + value.shape[0], :] = value[:, h * LANES : (h + 1) * LANES]

    def column(ref):
        square = jnp.broadcast_to(ref[0, 0].astype(F32), (tiles, tiles))
        diagonal = lax.broadcasted_iota(jnp.int32, (tiles, tiles), 0) == lax.broadcasted_iota(
            jnp.int32, (tiles, tiles), 1
        )
        return jnp.sum(jnp.where(diagonal, square, 0.0), axis=1, keepdims=True).astype(jnp.int32)

    order = take_wide(orders_ref[0, 0, 0], rank)
    slot = take_wide(blocks_ref[0, 0, 0], order)
    shard = jnp.zeros_like(slot)
    for i in range(1, nd):
        shard = shard + (slot >= i * cap).astype(jnp.int32)
    offset = slot - shard * cap
    hop = me - shard
    hop = jnp.where(hop < 0, hop + nd, hop)
    slot_row = hop * rows + (offset >> 7)
    slot_lane = offset & (LANES - 1)
    live = rank < column(counts_ref)
    tile_id = column(ids_ref)
    centre_x = ((tile_id % TW) * SIDE).astype(F32) + 0.5 * SIDE
    centre_y = ((tile_id // TW) * SIDE).astype(F32) + 0.5 * SIDE

    pieces = [[None] * halves for _ in range(FEATS)]
    for c in range(halves):
        low = slot_lane[:, c * LANES : (c + 1) * LANES]
        high = slot_row[:, c * LANES : (c + 1) * LANES]
        acc = [jnp.zeros((tiles, LANES), F32) for _ in range(FEATS)]
        for n in range(table_rows):
            here = high == n
            for f in range(FEATS):
                source = jnp.broadcast_to(recv[n // rows][f, n % rows : n % rows + 1, :], (tiles, LANES))
                acc[f] = jnp.where(here, lane_take(source, low), acc[f])
        for f in range(FEATS):
            pieces[f][c] = acc[f]
    mean_x, mean_y, con_a, con_b, con_c, log_op, red, green, blue = [jnp.concatenate(p, axis=1) for p in pieces]
    mean_x = mean_x - centre_x
    mean_y = mean_y - centre_y
    bx = con_a * mean_x
    by = con_c * mean_y
    constant = log_op - (bx * mean_x + con_b * mean_x * mean_y + by * mean_y)
    constant = jnp.where(live, constant, DEAD)
    poly = [constant, 2.0 * bx + con_b * mean_y, 2.0 * by + con_b * mean_x, -con_a, -con_b, -con_c]
    for i, value in enumerate(poly):
        rest = value
        for part in range(3):
            piece = rest.astype(BF16).astype(F32)
            rest = rest - piece
            at = (6 * part + i) * tiles
            put(coef, at, piece)
    for i, value in enumerate((red, green, blue)):
        first = value.astype(BF16).astype(F32)
        second = (value - first).astype(BF16).astype(F32)
        for block, piece in enumerate((first, first, second, second)):
            at = (18 + 3 * block + i) * tiles
            put(coef, at, piece)
    coef[:, 30 * tiles : 32 * tiles, :] = jnp.zeros((halves, 2 * tiles, LANES), F32)

    pixel = lax.broadcasted_iota(jnp.int32, (1, pixels), 1)
    px = (pixel & (SIDE - 1)).astype(F32) + (0.5 - 0.5 * SIDE)
    py = (pixel >> 4).astype(F32) + (0.5 - 0.5 * SIDE)
    one = jnp.ones((1, pixels), F32)
    monomials = [one, px, py, px * px, px * py, py * py]
    zero = jnp.zeros((1, pixels), F32)
    basis_scr = g_rows
    for part in range(3):
        for i in range(6):
            basis_scr[6 * part + i : 6 * part + i + 1, :] = monomials[i]
    basis_scr[18:32, :] = jnp.zeros((14, pixels), F32)
    basis = basis_scr[...].astype(BF16)
    moment_basis = jnp.concatenate(monomials + [zero, zero], axis=0).astype(BF16)
    g_rows[0:18, :] = jnp.zeros((18, pixels), F32)

    sub_e = lax.broadcasted_iota(jnp.int32, (8, entries), 0)
    own_chunk = jnp.where(sub_e == (lax.broadcasted_iota(jnp.int32, (8, entries), 1) & 7), 1.0, 0.0)
    sub_p = lax.broadcasted_iota(jnp.int32, (8, pixels), 0)

    def down(x, by, fill):
        return jnp.where(sub_p >= by, pltpu.roll(x, by, 0), fill)

    def up(x, by, fill):
        return jnp.where(sub_p < 8 - by, pltpu.roll(x, 8 - by, 0), fill)

    def tile(t, carry):
        table = [coef[h, pl.ds(t, 32, stride=tiles), :] for h in range(halves)]
        table = jnp.concatenate(table, axis=1)
        lhs = table.T.astype(BF16)
        a_scr[...] = jnp.exp2(jnp.minimum(dot(lhs, basis, 1, 0), 0.0))
        trans = jnp.ones((8, pixels), F32)
        for jj in range(entries // 16):
            w = []
            for h in range(2):
                at = slice(16 * jj + 8 * h, 16 * jj + 8 * h + 8)
                t_scr[at, :] = trans
                value = trans * a_scr[at, :]
                trans = trans - value
                w.append(value)
            at = slice(16 * jj, 16 * jj + 16)
            whi_scr[at, :], wlo_scr[at, :] = split2(jnp.concatenate(w, axis=0))
        colour = [own_chunk * table[18 + i : 19 + i, :] for i in range(3)]
        colour = colour + [own_chunk * table[24 + i : 25 + i, :] for i in range(3)]
        colour = jnp.concatenate(colour, axis=0).astype(BF16)
        local = dot(colour, whi_scr[...], 1, 0) + dot(colour, wlo_scr[...], 1, 0)
        local = [local[8 * i : 8 * i + 8, :] + local[24 + 8 * i : 32 + 8 * i, :] for i in range(3)]
        before = down(trans, 1, 1.0)
        for by in (1, 2, 4):
            before = before * down(before, by, 1.0)
        tinted = []
        inner = jnp.zeros((8, pixels), F32)
        for i in range(3):
            image = jnp.sum(before * local[i], axis=0, keepdims=True)
            images_ref[0, 0, 0, t, i : i + 1, :] = image
            residual = image - target_ref[0, 0, 0, t, i : i + 1, :]
            first = residual.astype(BF16).astype(F32)
            second = (residual - first).astype(BF16).astype(F32)
            g_rows[18 + i : 19 + i, :] = first
            g_rows[21 + i : 22 + i, :] = second
            g_rows[24 + i : 25 + i, :] = first
            g_rows[27 + i : 28 + i, :] = second
            tinted.append(before * residual)
            inner = inner + residual * local[i]
        q_scr[...] = dot(lhs, g_rows[...].astype(BF16), 1, 0)
        tinted_hi, tinted_lo = split2(jnp.concatenate(tinted, axis=0))
        tinted = jnp.concatenate([tinted_hi.astype(F32), tinted_lo.astype(F32)], axis=0).astype(BF16)
        colour_grad = dot(tinted, whi_scr[...], 1, 1) + dot(tinted, wlo_scr[...], 1, 1)
        rows_out = []
        for i in range(3):
            both = colour_grad[8 * i : 8 * i + 8, :] + colour_grad[24 + 8 * i : 32 + 8 * i, :]
            rows_out.append(jnp.sum(own_chunk * both, axis=0, keepdims=True))
        add = up(inner, 1, 0.0)
        scale = up(trans, 1, 0.0)
        for by in (1, 2, 4):
            add = add + scale * up(add, by, 0.0)
            scale = scale * up(scale, by, 0.0)
        behind = add
        for jj in reversed(range(entries // 16)):
            g = [None, None]
            for h in (1, 0):
                at = slice(16 * jj + 8 * h, 16 * jj + 8 * h + 8)
                moved = a_scr[at, :] * (q_scr[at, :] - behind)
                behind = behind + moved
                g[h] = (t_scr[at, :] * before) * moved
            at = slice(16 * jj, 16 * jj + 16)
            ghi_scr[at, :], glo_scr[at, :] = split2(jnp.concatenate(g, axis=0))
        moments = dot(moment_basis, ghi_scr[...], 1, 1) + dot(moment_basis, glo_scr[...], 1, 1)
        for h in range(halves):
            columns = slice(h * LANES, (h + 1) * LANES)
            mom[h, pl.ds(t, 8, stride=tiles), :] = moments[:, columns]
            for i in range(3):
                mom[h, pl.ds((8 + i) * tiles + t, 1), :] = rows_out[i][:, columns]
        return carry

    lax.fori_loop(0, tiles, tile, 0)

    def got(i):
        return jnp.concatenate([mom[h, i * tiles : (i + 1) * tiles, :] for h in range(halves)], axis=1)

    m0, m1, m2, m3, m4, m5 = [got(i) for i in range(6)]
    su = m1 - mean_x * m0
    sv = m2 - mean_y * m0
    suu = m3 - mean_x * (m1 + su)
    suv = m4 - mean_x * m2 - mean_y * su
    svv = m5 - mean_y * (m2 + sv)
    grads = [
        LN2 * (2.0 * con_a * su + con_b * sv),
        LN2 * (con_b * su + 2.0 * con_c * sv),
        -0.5 * suu,
        -suv,
        -0.5 * svv,
        m0,
    ] + [got(8 + i) for i in range(3)]
    value_rows = [[g[t : t + 1, :] for g in grads] for t in range(tiles)]
    index_rows = [(slot_row[t : t + 1, :], slot_lane[t : t + 1, :]) for t in range(tiles)]
    scatter_products(value_rows, index_rows, spread, hot, table_rows)
    summed = dot(spread[...], hot[...], 1, 1)
    for f in range(FEATS):
        both = (
            summed[f * table_rows : (f + 1) * table_rows, :]
            + summed[(FEATS + f) * table_rows : (FEATS + f + 1) * table_rows, :]
        )
        for j in range(nd):
            outs[j][f] = both[j * rows : (j + 1) * rows, :]


def render(me, received, blocks, orders, counts, ids, target, nd, cap, rows):
    tiles, entries = blocks.shape[3:]
    pixels = SIDE * SIDE
    return pl.pallas_call(
        partial(render_kernel, nd=nd, cap=cap, rows=rows, tiles=tiles, entries=entries),
        in_specs=[smem_spec()] + [vmem_spec()] * (nd + 5),
        out_specs=[vmem_spec()] * (nd + 1),
        out_shape=[jax.ShapeDtypeStruct((FEATS, rows, LANES), F32)] * nd
        + [jax.ShapeDtypeStruct(target.shape, F32)],
        scratch_shapes=[
            pltpu.VMEM((entries // LANES, 32 * tiles, LANES), F32),
            pltpu.VMEM((entries, pixels), F32),
            pltpu.VMEM((entries, pixels), F32),
            pltpu.VMEM((entries, pixels), F32),
            pltpu.VMEM((entries, pixels), BF16),
            pltpu.VMEM((entries, pixels), BF16),
            pltpu.VMEM((entries, pixels), BF16),
            pltpu.VMEM((entries, pixels), BF16),
            pltpu.VMEM((32, pixels), F32),
            pltpu.VMEM((entries // LANES, 11 * tiles, LANES), F32),
            pltpu.VMEM((2 * FEATS * nd * rows, tiles * entries), BF16),
            pltpu.VMEM((LANES, tiles * entries), BF16),
        ],
        compiler_params=pltpu.CompilerParams(vmem_limit_bytes=48 * 1024 * 1024),
        name="render_tiles",
    )(me, *received, blocks, orders, counts, ids, target)


def owner_kernel(me_ref, *refs, nd, rows, parts, nv, nc, out_rows):
    recv = refs[:nd]
    idx_ref, w_ref = refs[nd : nd + 2]
    outs = refs[nd + 2 : nd + 2 + parts]
    spread, hot, summed = refs[nd + 2 + parts :]
    my_view = me_ref[1]
    my_chip = me_ref[2]
    value_rows = []
    index_rows = []
    for n in range(nd * rows):
        value_rows.append([recv[n // rows][f, n % rows : n % rows + 1, :] for f in range(FEATS)])
        index = idx_ref[n : n + 1, :]
        index_rows.append((index >> 7, index & (LANES - 1)))
    scatter_products(value_rows, index_rows, spread, hot, out_rows)
    result = dot(spread[...], hot[...], 1, 1)
    share = out_rows // parts
    for f in range(FEATS):
        both = (
            result[f * out_rows : (f + 1) * out_rows, :]
            + result[(FEATS + f) * out_rows : (FEATS + f + 1) * out_rows, :]
        )
        for p in range(parts):
            summed[p, f] = both[p * share : (p + 1) * share, :]
    for p in range(parts):
        summed[p, FEATS] = w_ref[0:share, :]
    for dv in range(nv):
        for dc in range(nc):
            where = lax.rem(my_view + dv, nv) * nc + lax.rem(my_chip + dc, nc)
            outs[dv * nc + dc][...] = summed[where]


def owner_sums(me, received, index, weights, nd, rows, nv, nc, width):
    parts = nv * nc
    out_rows = width // LANES
    share = out_rows // parts
    return pl.pallas_call(
        partial(owner_kernel, nd=nd, rows=rows, parts=parts, nv=nv, nc=nc, out_rows=out_rows),
        in_specs=[smem_spec()] + [vmem_spec()] * (nd + 2),
        out_specs=[vmem_spec()] * parts,
        out_shape=[jax.ShapeDtypeStruct((FEATS + 1, share, LANES), F32)] * parts,
        scratch_shapes=[
            pltpu.VMEM((2 * FEATS * out_rows, nd * rows * LANES), BF16),
            pltpu.VMEM((LANES, nd * rows * LANES), BF16),
            pltpu.VMEM((parts, FEATS + 1, share, LANES), F32),
        ],
        compiler_params=pltpu.CompilerParams(vmem_limit_bytes=48 * 1024 * 1024),
        name="owner_sums",
    )(me, *received, index, weights)


def pullback_kernel(at_ref, params_ref, *refs, nv, nc, coefs):
    recv = refs[: nv * nc]
    out_ref, flat = refs[nv * nc :]
    share = recv[0].shape[1]
    columns = share * LANES

    def row(i):
        return params_ref[i : i + 1, :]

    lx, lyx, ly, lzx, lzy, lz = [row(i) for i in range(3, 9)]
    total = [jnp.zeros((1, columns), F32) for _ in range(10)]
    harmonics = [jnp.zeros((coefs, columns), F32) for _ in range(3)]
    square = lax.broadcasted_iota(jnp.int32, (coefs, LANES), 1) == lax.broadcasted_iota(
        jnp.int32, (coefs, LANES), 0
    ) + 10
    for v in range(nv):
        packed = recv[v * nc][FEATS]
        for i in range(share):
            block = recv[v * nc][0:FEATS, i, :]
            for c in range(1, nc):
                block = block + recv[v * nc + c][0:FEATS, i, :]
            flat[0:FEATS, i * LANES : (i + 1) * LANES] = block
        gx, gy, g0, g1, g2, gh, gr, gg, gb = [flat[f : f + 1, :] for f in range(FEATS)]
        cam = [[packed[i : i + 1, j : j + 1] for j in range(3)] for i in range(2)]
        for j in range(3):
            total[j] = total[j] + cam[0][j] * gx + cam[1][j] * gy
        m = []
        for i in range(2):
            a0, a1, a2 = cam[i]
            m.append((a0 * lx + a1 * lyx + a2 * lzx, a1 * ly + a2 * lzy, a2 * lz))
        upper = m[0][0] * m[0][0] + m[0][1] * m[0][1] + m[0][2] * m[0][2] + DILATION
        cross = m[0][0] * m[1][0] + m[0][1] * m[1][1] + m[0][2] * m[1][2]
        lower = m[1][0] * m[1][0] + m[1][1] * m[1][1] + m[1][2] * m[1][2] + DILATION
        inverse = 1.0 / (upper * lower - cross * cross)
        c0, c1, c2 = lower * inverse, -cross * inverse, upper * inverse
        h1 = 0.5 * g1
        k00, k01 = g0 * c0 + h1 * c1, g0 * c1 + h1 * c2
        k10, k11 = h1 * c0 + g2 * c1, h1 * c1 + g2 * c2
        s00 = -(c0 * k00 + c1 * k10)
        s01 = -(c0 * k01 + c1 * k11)
        s11 = -(c1 * k01 + c2 * k11)
        gm = [[2.0 * (s00 * m[0][k] + s01 * m[1][k]) for k in range(3)]]
        gm.append([2.0 * (s01 * m[0][k] + s11 * m[1][k]) for k in range(3)])
        at = 3
        for i in range(3):
            for k in range(i + 1):
                total[at] = total[at] + cam[0][i] * gm[0][k] + cam[1][i] * gm[1][k]
                at += 1
        total[9] = total[9] + gh
        basis = jnp.sum(jnp.where(square, packed[0:1, :], 0.0), axis=1, keepdims=True)
        for c, g in enumerate((gr, gg, gb)):
            harmonics[c] = harmonics[c] + basis * g
    logit = row(9)
    total[9] = total[9] / (1.0 + jnp.exp(logit))
    for i in range(10):
        out_ref[i : i + 1, :] = total[i]
    for c in range(3):
        out_ref[10 + c * coefs : 10 + (c + 1) * coefs, :] = harmonics[c]


def pull_back(at, params, received, nv, nc, coefs):
    parts = nv * nc
    columns = params.shape[1] // parts
    block = received[0].shape
    return pl.pallas_call(
        partial(pullback_kernel, nv=nv, nc=nc, coefs=coefs),
        grid_spec=pltpu.PrefetchScalarGridSpec(
            num_scalar_prefetch=1,
            grid=(1,),
            in_specs=[pl.BlockSpec((params.shape[0], columns), lambda i, at_ref: (0, at_ref[0]))]
            + [pl.BlockSpec(block, lambda i, at_ref: (0, 0, 0))] * parts,
            out_specs=pl.BlockSpec((params.shape[0], columns), lambda i, at_ref: (0, 0)),
            scratch_shapes=[pltpu.VMEM((16, columns), F32)],
        ),
        out_shape=jax.ShapeDtypeStruct((params.shape[0], columns), F32),
        compiler_params=pltpu.CompilerParams(vmem_limit_bytes=40 * 1024 * 1024),
        name="pull_back",
    )(at, params, *received)


def local(
    params,
    cameras,
    view_basis,
    tile_lists,
    margin_blocks,
    depth_orders,
    tile_counts,
    requests,
    target,
    *,
    nd,
    nv,
    nc,
):
    cap = requests.shape[4]
    rows = -(-cap // LANES)
    my_view = lax.axis_index("view")
    my_chip = lax.axis_index("chip")
    me = jnp.stack([lax.axis_index("dev"), my_view, my_chip]).astype(jnp.int32)
    at = (my_view * nc + my_chip).astype(jnp.int32).reshape(1)

    *packets, index, weights = send(me, cameras, view_basis, params, requests, nd, cap, rows)
    received = [packets[0]]
    for j in range(1, nd):
        received.append(lax.ppermute(packets[j], "dev", [(i, (i + j) % nd) for i in range(nd)]))
    *returns, images = render(
        me, received, margin_blocks, depth_orders, tile_counts, tile_lists, target, nd, cap, rows
    )
    back = [returns[0]]
    for j in range(1, nd):
        back.append(lax.ppermute(returns[j], "dev", [((i + j) % nd, i) for i in range(nd)]))
    shares = owner_sums(me, back, index, weights, nd, rows, nv, nc, params.shape[1])
    arrived = []
    for dv in range(nv):
        for dc in range(nc):
            pairs = [
                (v * nc + c, (v + dv) % nv * nc + (c + dc) % nc) for v in range(nv) for c in range(nc)
            ]
            piece = shares[dv * nc + dc]
            arrived.append(piece if dv + dc == 0 else lax.ppermute(piece, ("view", "chip"), pairs))
    grads = pull_back(at, params, arrived, nv, nc, view_basis.shape[1])
    return (grads, images)


def solution(mesh):
    return jax.shard_map(
        partial(local, nd=mesh.shape["dev"], nv=mesh.shape["view"], nc=mesh.shape["chip"]),
        mesh=mesh,
        in_specs=(
            P(None, ("groups", "dev")),
            P(("groups", "view"), None, None),
            P(("groups", "view"), None),
            P("view", ("groups", "dev"), "chip", None),
            P("view", ("groups", "dev"), "chip", None, None),
            P("view", ("groups", "dev"), "chip", None, None),
            P("view", ("groups", "dev"), "chip", None),
            P("view", None, "chip", ("groups", "dev"), None),
            P("view", ("groups", "dev"), "chip", None, None, None),
        ),
        out_specs=(
            P(None, ("groups", "dev", "view", "chip")),
            P("view", ("groups", "dev"), "chip", None, None, None),
        ),
        check_vma=False,
    )
```

time: 371 us -> 53.5 us (0.14)
  other arithmetic: 125 us -> 0.08 us
  local copies, waits for them, and re-layouts: 111 us -> 3.33 us
  waiting for transfers between devices: 78.6 us -> 9.44 us
  matrix products: 28.9 us -> 0 us
  Pallas kernels: 0 us -> 26.9 us
  between operations: 14.4 us -> 0.74 us
    gather x50 -> x0, local copies, waits for them, and re-layouts: 70.6 us -> none  [the longest x32 39.1 us: tile_step(): ordered = jnp.take(slot_ids, ordering)]
    another operation x49 -> x1, other arithmetic: 55.6 us -> 0.08 us  [local(): me = jnp.stack([lax.axis_index('dev'), my_view, my_chip]).astype(jnp.int32)]
    all_to_all x2 -> x0, waiting for transfers between devices: 48.5 us -> none  [the longest x1 25.1 us: local(): lax.all_to_all(pullback(slot_grad)[0], 'dev', split_axis=1, concat_axis=1...]
    scatter-add x2 -> x0, other arithmetic: 47.5 us -> none  [the longest x1 24.1 us: local(): local_grad = jax.ops.segment_sum(row_grad.T, wanted, shard_width).T]
    reduce_scatter x1 -> x0, waiting for transfers between devices: 30.1 us -> none  [local(): lax.psum_scatter(local_grad, ('view', 'chip'), scatter_dimension=1, tiled...]
    dot_general x31 -> x0, matrix products: 28.9 us -> none  [the longest x24 26.1 us: render(): return jnp.dot(values[6:9], before * alpha, precision=lax.Precision.HIGHEST)]
    pallas_call x0 -> x4, Pallas kernels: none -> 26.9 us  [the longest x1 20.6 us: render(): pl.pallas_call(partial(render_kernel, nd=nd, cap=cap, rows=rows, tiles=ti...]
    another operation x81 -> x0, local copies, waits for them, and re-layouts: 15.1 us -> none
  transfers between devices with their start and end apart: 3 -> 9, of which waited for: 3 -> 7; matrix products, arithmetic and copies ran while one was open for 1% -> 3% of each run, Pallas kernels for 0% -> 0%
where the time goes in v1:
time: 53.5 us; the launch traced here: 53.2 us
  Pallas kernels  26.9 us (50%)
  starting transfers between devices  12.8 us (24%)
  waiting for transfers between devices  9.44 us (18%)
  local copies, waits for them, and re-layouts  3.33 us (6%)
  between operations  0.74 us (1%)
    pallas_call x1, Pallas kernels, render(): pl.pallas_call(partial(render_kernel, nd=nd, cap=cap, rows=rows, tiles=ti...  20.6 us
    ppermute x3, starting transfers between devices, local(): lax.ppermute(packets[j], 'dev', [(i, (i + j) % nd) for i in range(nd)])  7.01 us
    ppermute x3, waiting for transfers between devices, local(): lax.ppermute(returns[j], 'dev', [((i + j) % nd, i) for i in range(nd)])  5.12 us
    ppermute x3, starting transfers between devices, local(): lax.ppermute(returns[j], 'dev', [((i + j) % nd, i) for i in range(nd)])  3.84 us
    unnamed x20, local copies, waits for them, and re-layouts  3.33 us
    pallas_call x1, Pallas kernels, owner_sums(): pl.pallas_call(partial(owner_kernel, nd=nd, rows=rows, parts=parts, nv=nv...  2.79 us
    ppermute x3, waiting for transfers between devices, local(): lax.ppermute(piece, ('view', 'chip'), pairs)  2.59 us
    pallas_call x1, Pallas kernels, send(): pl.pallas_call(partial(send_kernel, nd=nd, cap=cap, rows=rows), in_specs=...  2.25 us
  transfers between devices with their start and end apart: 9, of which 7 were waited for; matrix products, arithmetic and copies ran while one was open for 3% of the time, Pallas kernels for 0%

profile of v1, /device:TPU:0, one launch (start us, length us, event | category | flops | bytes accessed | tf_op | source)
XLA Modules:
  0.0 53.2 jit_solution(15987657170355570808)
XLA Ops:
  0.6 0.0 copy-start.2
  0.6 0.0 copy-start.5
  0.7 0.0 copy-start.6
  0.7 0.1 pad_add_fusion.me_ref
  0.7 0.6 %copy-done.2 = s32[1,4,1,1,960]{4,3,2,1,0:T(1,128)S(1)} copy-done((s32[1,4,1,1,960]{4,3,2,1,0:T(1,128)S(1)}, s32[1,4,1,1,960]{4,3,2,1,0:T(1,128)}, u32[]{:S(2)}) %copy-start.2) | copy-done | bytes 15384
  1.3 0.0 copy-done.5
  1.4 0.0 copy-done.6
  1.4 0.0 copy-start
  1.4 1.2 %copy-done = f32[58,4096]{1,0:T(8,128)S(1)} copy-done((f32[58,4096]{1,0:T(8,128)S(1)}, f32[58,4096]{1,0:T(8,128)}, u32[]{:S(2)}) %copy-start) | copy-done | bytes 950296
  2.6 0.0 copy-start.1
  2.6 2.3 %project_gather.1 = (f32[9,8,128]{2,1,0:T(8,128)S(1)}, f32[9,8,128]{2,1,0:T(8,128)S(1)}, f32[9,8,128]{2,1,0:T(8,128)S(1)}, f32[9,8,128]{2,1,0:T(8,128)S(1)}, s32...) custom-call(s32[3]{0:T(128)S(1)} %pad_add_fusion.me_ref, f32[1,2,4]{2,1,0:T(2,128)S(1)} %copy-done.5, f32[1,16]{1,0:T(1,128)S(1)} %copy-done.6, ...), custom_call_target="tpu_custom_call" | custom-call | tf_op jit(solution)/shard_map/project_gather/pallas_call | solution.py:130
  4.8 3.1 %collective-permute-start = (f32[9,8,128]{2,1,0:T(8,128)S(1)}, f32[9,8,128]{2,1,0:T(8,128)S(1)}, u32[]{:S(2)}, u32[]{:S(2)}) collective-permute-start(f32[9,8,128]{2,1,0:T(8,128)S(1)} %get-tuple-element.18), channel_id=1, source_target_pairs={{0,4},{4,8},{8,12},{12,0},{1,5},{5,9},{9,13},{13,1},{2,6},{6,10},{... | collective-permute-start | bytes 110600 | tf_op jit(solution)/shard_map/ppermute | solution.py:559
  7.9 2.6 %collective-permute-start.1 = (f32[9,8,128]{2,1,0:T(8,128)S(1)}, f32[9,8,128]{2,1,0:T(8,128)S(1)}, u32[]{:S(2)}, u32[]{:S(2)}) collective-permute-start(f32[9,8,128]{2,1,0:T(8,128)S(1)} %get-tuple-element.19), channel_id=1, source_target_pairs={{0,8},{4,12},{8,0},{12,4},{1,9},{5,13},{9,1},{13,5},{2,10},{6,14},... | collective-permute-start | bytes 110600 | tf_op jit(solution)/shard_map/ppermute | solution.py:559
  10.5 0.0 copy-start.3
  10.5 0.0 copy-start.4
  10.5 1.3 %collective-permute-start.2 = (f32[9,8,128]{2,1,0:T(8,128)S(1)}, f32[9,8,128]{2,1,0:T(8,128)S(1)}, u32[]{:S(2)}, u32[]{:S(2)}) collective-permute-start(f32[9,8,128]{2,1,0:T(8,128)S(1)} %get-tuple-element.20), channel_id=1, source_target_pairs={{0,12},{4,0},{8,4},{12,8},{1,13},{5,1},{9,5},{13,9},{2,14},{6,2},{... | collective-permute-start | bytes 110600 | tf_op jit(solution)/shard_map/ppermute | solution.py:559
  11.9 0.8 %copy.11.refs_8_ = f32[1,1,1,16,3,256]{5,4,3,2,1,0:T(4,128)S(1)} copy(f32[1,1,1,16,3,256]{5,3,4,2,1,0:T(8,128)} %param.17) | data formatting | bytes 98304 | tf_op args[8]
  12.7 0.0 copy-start.7
  12.7 0.0 copy-start.8
  12.7 0.0 collective-permute-done.refs_1_
  12.7 0.4 collective-permute-done.1.refs_2_
  13.2 1.3 %collective-permute-done.2.refs_3_ = f32[9,8,128]{2,1,0:T(8,128)S(1)} collective-permute-done((f32[9,8,128]{2,1,0:T(8,128)S(1)}, f32[9,8,128]{2,1,0:T(8,128)S(1)}, u32[]{:S(2)}, u32[]{:S(2)}) %collective-permute-start.2) | collective-permute-done | bytes 36896 | tf_op jit(solution)/shard_map/ppermute | solution.py:559
  14.5 0.0 copy-done.3
  14.5 0.0 copy-done.4
  14.5 0.0 copy-done.7
  14.5 0.0 copy-done.8
  14.5 20.6 %render_tiles.1 = (f32[9,8,128]{2,1,0:T(8,128)S(1)}, f32[9,8,128]{2,1,0:T(8,128)S(1)}, f32[9,8,128]{2,1,0:T(8,128)S(1)}, f32[9,8,128]{2,1,0:T(8,128)S(1)}, f32[1,1,1,16,3,256]{5,4,3,2,1,0:T(4,128)S(1)}) custom-call(s32[3]{0:T(128)S(1)} %pad_add_fusion.me_ref, f32[9,8,128]{2,1,0:T(8,128)S(1)} %get-tuple-element.17.refs_0_, ...), custom_call_target="tpu_custom_call" | custom-call | tf_op jit(solution)/shard_map/render_tiles/pallas_call | solution.py:379
  35.1 3.2 %collective-permute-start.3 = (f32[9,8,128]{2,1,0:T(8,128)S(1)}, f32[9,8,128]{2,1,0:T(8,128)S(1)}, u32[]{:S(2)}, u32[]{:S(2)}) collective-permute-start(f32[9,8,128]{2,1,0:T(8,128)S(1)} %get-tuple-element.22), channel_id=1, source_target_pairs={{4,0},{8,4},{12,8},{0,12},{5,1},{9,5},{13,9},{1,13},{6,2},{10,6},{... | collective-permute-start | bytes 110600 | tf_op jit(solution)/shard_map/ppermute | solution.py:565
  38.3 0.0 collective-permute-start.4
  38.3 0.6 %collective-permute-start.5 = (f32[9,8,128]{2,1,0:T(8,128)S(1)}, f32[9,8,128]{2,1,0:T(8,128)S(1)}, u32[]{:S(2)}, u32[]{:S(2)}) collective-permute-start(f32[9,8,128]{2,1,0:T(8,128)S(1)} %get-tuple-element.24), channel_id=1, source_target_pairs={{12,0},{0,4},{4,8},{8,12},{13,1},{1,5},{5,9},{9,13},{14,2},{2,6},{... | collective-permute-start | bytes 110600 | tf_op jit(solution)/shard_map/ppermute | solution.py:565
  39.0 1.0 %collective-permute-done.3.refs_1_ = f32[9,8,128]{2,1,0:T(8,128)S(1)} collective-permute-done((f32[9,8,128]{2,1,0:T(8,128)S(1)}, f32[9,8,128]{2,1,0:T(8,128)S(1)}, u32[]{:S(2)}, u32[]{:S(2)}) %collective-permute-start.3) | collective-permute-done | bytes 36896 | tf_op jit(solution)/shard_map/ppermute | solution.py:565
  40.0 3.2 %collective-permute-done.4.refs_2_ = f32[9,8,128]{2,1,0:T(8,128)S(1)} collective-permute-done((f32[9,8,128]{2,1,0:T(8,128)S(1)}, f32[9,8,128]{2,1,0:T(8,128)S(1)}, u32[]{:S(2)}, u32[]{:S(2)}) %collective-permute-start.4) | collective-permute-done | bytes 36896 | tf_op jit(solution)/shard_map/ppermute | solution.py:565
  43.2 0.9 %collective-permute-done.5.refs_3_ = f32[9,8,128]{2,1,0:T(8,128)S(1)} collective-permute-done((f32[9,8,128]{2,1,0:T(8,128)S(1)}, f32[9,8,128]{2,1,0:T(8,128)S(1)}, u32[]{:S(2)}, u32[]{:S(2)}) %collective-permute-start.5) | collective-permute-done | bytes 36896 | tf_op jit(solution)/shard_map/ppermute | solution.py:565
  44.1 2.8 %owner_sums.1 = (f32[10,8,128]{2,1,0:T(8,128)S(1)}, f32[10,8,128]{2,1,0:T(8,128)S(1)}, f32[10,8,128]{2,1,0:T(8,128)S(1)}, f32[10,8,128]{2,1,0:T(8,128)S(1)}) custom-call(s32[3]{0:T(128)S(1)} %pad_add_fusion.me_ref, f32[9,8,128]{2,1,0:T(8,128)S(1)} %get-tuple-element.21.refs_0_, f32[9,8,128]{2,1,0:T(8,128)S(1)} %collective-permute-done.3.refs_1_, ...), custom_call_target="tpu_custom_call" | custom-call | tf_op jit(solution)/shard_map/owner_sums/pallas_call | solution.py:439
  46.9 0.1 collective-permute-start.6
  47.0 1.6 %collective-permute-start.7 = (f32[10,8,128]{2,1,0:T(8,128)S(1)}, f32[10,8,128]{2,1,0:T(8,128)S(1)}, u32[]{:S(2)}, u32[]{:S(2)}) collective-permute-start(f32[10,8,128]{2,1,0:T(8,128)S(1)} %get-tuple-element.29), channel_id=1, source_target_pairs={{0,2},{1,3},{2,0},{3,1},{4,6},{5,7},{6,4},{7,5},{8,10},{9,11},{10,... | collective-permute-start | bytes 122888 | tf_op jit(solution)/shard_map/ppermute | solution.py:574
  48.5 0.3 collective-permute-start.8
  48.8 0.6 %copy.12 = f32[1,1,1,16,3,256]{5,3,4,2,1,0:T(8,128)} copy(f32[1,1,1,16,3,256]{5,4,3,2,1,0:T(4,128)S(1)} %get-tuple-element.33) | data formatting | bytes 98304
  49.5 0.0 collective-permute-done.6.refs_1_
  49.5 1.6 %collective-permute-done.7.refs_2_ = f32[10,8,128]{2,1,0:T(8,128)S(1)} collective-permute-done((f32[10,8,128]{2,1,0:T(8,128)S(1)}, f32[10,8,128]{2,1,0:T(8,128)S(1)}, u32[]{:S(2)}, u32[]{:S(2)}) %collective-permute-start.7) | collective-permute-done | bytes 40992 | tf_op jit(solution)/shard_map/ppermute | solution.py:574
  51.0 1.0 %collective-permute-done.8.refs_3_ = f32[10,8,128]{2,1,0:T(8,128)S(1)} collective-permute-done((f32[10,8,128]{2,1,0:T(8,128)S(1)}, f32[10,8,128]{2,1,0:T(8,128)S(1)}, u32[]{:S(2)}, u32[]{:S(2)}) %collective-permute-start.8) | collective-permute-done | bytes 40992 | tf_op jit(solution)/shard_map/ppermute | solution.py:574
  52.0 0.0 copy-done.1
  52.0 1.2 %pull_back.1 = f32[58,1024]{1,0:T(8,128)} custom-call(s32[1]{0:T(128)} %bitcast.at_ref, f32[58,4096]{1,0:T(8,128)S(1)} %copy-done.1, f32[10,8,128]{2,1,0:T(8,128)S(1)} %get-tuple-element.27.refs_0_, f32[10,8,128]{2,1,0:T(8,128)S(1)} %collective-permute-done.6.refs_1_, f32[10,8,128]{2,1,0:T(8,128)S(1)} %collective-permute-done.7.refs_2_, ...), custom_call_target="tpu_custom_call" | custom-call | tf_op jit(solution)/shard_map/pull_back/pallas_call | solution.py:518
Async XLA Ops:
  0.6 0.7 %copy-start.2 = (s32[1,4,1,1,960]{4,3,2,1,0:T(1,128)S(1)}, s32[1,4,1,1,960]{4,3,2,1,0:T(1,128)}, u32[]{:S(2)}) copy-start(s32[1,4,1,1,960]{4,3,2,1,0:T(1,128)} %req_ref.1) | copy-start | bytes 46084
  0.6 0.7 %copy-start.5 = (f32[1,2,4]{2,1,0:T(2,128)S(1)}, f32[1,2,4]{2,1,0:T(2,128)}, u32[]{:S(2)}) copy-start(f32[1,2,4]{2,1,0:T(2,128)} %cam_ref.1) | copy-start | bytes 100
  0.7 0.7 %copy-start.6 = (f32[1,16]{1,0:T(1,128)S(1)}, f32[1,16]{1,0:T(1,128)}, u32[]{:S(2)}) copy-start(f32[1,16]{1,0:T(1,128)} %basis_ref.1) | copy-start | bytes 196
  1.4 1.2 %copy-start = (f32[58,4096]{1,0:T(8,128)S(1)}, f32[58,4096]{1,0:T(8,128)}, u32[]{:S(2)}) copy-start(f32[58,4096]{1,0:T(8,128)} %params_ref.3) | copy-start | bytes 2850820
  2.6 49.5 %copy-start.1 = (f32[58,4096]{1,0:T(8,128)S(1)}, f32[58,4096]{1,0:T(8,128)}, u32[]{:S(2)}) copy-start(f32[58,4096]{1,0:T(8,128)} %params_ref.3) | copy-start | bytes 2850820
  4.8 7.9 %collective-permute-start = (f32[9,8,128]{2,1,0:T(8,128)S(1)}, f32[9,8,128]{2,1,0:T(8,128)S(1)}, u32[]{:S(2)}, u32[]{:S(2)}) collective-permute-start(f32[9,8,128]{2,1,0:T(8,128)S(1)} %get-tuple-element.18), channel_id=1, source_target_pairs={{0,4},{4,8},{8,12},{12,0},{1,5},{5,9},{9,13},{13,1},{2,6},{6,10},{... | collective-permute-start | bytes 110600 | tf_op jit(solution)/shard_map/ppermute | solution.py:559
  7.9 5.3 %collective-permute-start.1 = (f32[9,8,128]{2,1,0:T(8,128)S(1)}, f32[9,8,128]{2,1,0:T(8,128)S(1)}, u32[]{:S(2)}, u32[]{:S(2)}) collective-permute-start(f32[9,8,128]{2,1,0:T(8,128)S(1)} %get-tuple-element.19), channel_id=1, source_target_pairs={{0,8},{4,12},{8,0},{12,4},{1,9},{5,13},{9,1},{13,5},{2,10},{6,14},... | collective-permute-start | bytes 110600 | tf_op jit(solution)/shard_map/ppermute | solution.py:559
  10.5 4.0 %copy-start.3 = (s32[1,1,1,16,256]{4,3,2,1,0:T(8,128)S(1)}, s32[1,1,1,16,256]{4,3,2,1,0:T(8,128)}, u32[]{:S(2)}) copy-start(s32[1,1,1,16,256]{4,3,2,1,0:T(8,128)} %refs_4_.1) | copy-start | bytes 49156
  10.5 4.0 %copy-start.4 = (s32[1,1,1,16,256]{4,3,2,1,0:T(8,128)S(1)}, s32[1,1,1,16,256]{4,3,2,1,0:T(8,128)}, u32[]{:S(2)}) copy-start(s32[1,1,1,16,256]{4,3,2,1,0:T(8,128)} %refs_5_.1) | copy-start | bytes 49156
  10.5 4.0 %collective-permute-start.2 = (f32[9,8,128]{2,1,0:T(8,128)S(1)}, f32[9,8,128]{2,1,0:T(8,128)S(1)}, u32[]{:S(2)}, u32[]{:S(2)}) collective-permute-start(f32[9,8,128]{2,1,0:T(8,128)S(1)} %get-tuple-element.20), channel_id=1, source_target_pairs={{0,12},{4,0},{8,4},{12,8},{1,13},{5,1},{9,5},{13,9},{2,14},{6,2},{... | collective-permute-start | bytes 110600 | tf_op jit(solution)/shard_map/ppermute | solution.py:559
  12.7 1.8 %copy-start.7 = (s32[1,1,1,16]{3,2,1,0:T(1,128)S(1)}, s32[1,1,1,16]{3,2,1,0:T(1,128)}, u32[]{:S(2)}) copy-start(s32[1,1,1,16]{3,2,1,0:T(1,128)} %refs_6_.1) | copy-start | bytes 196
  12.7 1.8 %copy-start.8 = (s32[1,1,1,16]{3,2,1,0:T(1,128)S(1)}, s32[1,1,1,16]{3,2,1,0:T(1,128)}, u32[]{:S(2)}) copy-start(s32[1,1,1,16]{3,2,1,0:T(1,128)} %refs_7_.1) | copy-start | bytes 196
  35.1 4.8 %collective-permute-start.3 = (f32[9,8,128]{2,1,0:T(8,128)S(1)}, f32[9,8,128]{2,1,0:T(8,128)S(1)}, u32[]{:S(2)}, u32[]{:S(2)}) collective-permute-start(f32[9,8,128]{2,1,0:T(8,128)S(1)} %get-tuple-element.22), channel_id=1, source_target_pairs={{4,0},{8,4},{12,8},{0,12},{5,1},{9,5},{13,9},{1,13},{6,2},{10,6},{... | collective-permute-start | bytes 110600 | tf_op jit(solution)/shard_map/ppermute | solution.py:565
  38.3 4.9 %collective-permute-start.4 = (f32[9,8,128]{2,1,0:T(8,128)S(1)}, f32[9,8,128]{2,1,0:T(8,128)S(1)}, u32[]{:S(2)}, u32[]{:S(2)}) collective-permute-start(f32[9,8,128]{2,1,0:T(8,128)S(1)} %get-tuple-element.23), channel_id=1, source_target_pairs={{8,0},{12,4},{0,8},{4,12},{9,1},{13,5},{1,9},{5,13},{10,2},{14,6},... | collective-permute-start | bytes 110600 | tf_op jit(solution)/shard_map/ppermute | solution.py:565
  38.3 5.8 %collective-permute-start.5 = (f32[9,8,128]{2,1,0:T(8,128)S(1)}, f32[9,8,128]{2,1,0:T(8,128)S(1)}, u32[]{:S(2)}, u32[]{:S(2)}) collective-permute-start(f32[9,8,128]{2,1,0:T(8,128)S(1)} %get-tuple-element.24), channel_id=1, source_target_pairs={{12,0},{0,4},{4,8},{8,12},{13,1},{1,5},{5,9},{9,13},{14,2},{2,6},{... | collective-permute-start | bytes 110600 | tf_op jit(solution)/shard_map/ppermute | solution.py:565
  46.9 2.6 %collective-permute-start.6 = (f32[10,8,128]{2,1,0:T(8,128)S(1)}, f32[10,8,128]{2,1,0:T(8,128)S(1)}, u32[]{:S(2)}, u32[]{:S(2)}) collective-permute-start(f32[10,8,128]{2,1,0:T(8,128)S(1)} %get-tuple-element.28), channel_id=1, source_target_pairs={{0,1},{1,0},{2,3},{3,2},{4,5},{5,4},{6,7},{7,6},{8,9},{9,8},{10,11... | collective-permute-start | bytes 122888 | tf_op jit(solution)/shard_map/ppermute | solution.py:574
  47.0 4.1 %collective-permute-start.7 = (f32[10,8,128]{2,1,0:T(8,128)S(1)}, f32[10,8,128]{2,1,0:T(8,128)S(1)}, u32[]{:S(2)}, u32[]{:S(2)}) collective-permute-start(f32[10,8,128]{2,1,0:T(8,128)S(1)} %get-tuple-element.29), channel_id=1, source_target_pairs={{0,2},{1,3},{2,0},{3,1},{4,6},{5,7},{6,4},{7,5},{8,10},{9,11},{10,... | collective-permute-start | bytes 122888 | tf_op jit(solution)/shard_map/ppermute | solution.py:574
  48.5 3.5 %collective-permute-start.8 = (f32[10,8,128]{2,1,0:T(8,128)S(1)}, f32[10,8,128]{2,1,0:T(8,128)S(1)}, u32[]{:S(2)}, u32[]{:S(2)}) collective-permute-start(f32[10,8,128]{2,1,0:T(8,128)S(1)} %get-tuple-element.30), channel_id=1, source_target_pairs={{0,3},{1,2},{2,1},{3,0},{4,7},{5,6},{6,5},{7,4},{8,11},{9,10},{10,... | collective-permute-start | bytes 122888 | tf_op jit(solution)/shard_map/ppermute | solution.py:574

commit v2 on v1

--- a/solution.py
+++ b/solution.py
@@ -17,6 +17,7 @@
 F32 = jnp.float32
 BF16 = jnp.bfloat16
 FEATS = 9
+GROUP = 16
 
 
 def lane_take(row, index):
@@ -253,14 +254,14 @@
     one = jnp.ones((1, pixels), F32)
     monomials = [one, px, py, px * px, px * py, py * py]
     zero = jnp.zeros((1, pixels), F32)
-    basis_scr = g_rows
+    basis_scr = g_rows.at[0]
     for part in range(3):
         for i in range(6):
             basis_scr[6 * part + i : 6 * part + i + 1, :] = monomials[i]
     basis_scr[18:32, :] = jnp.zeros((14, pixels), F32)
     basis = basis_scr[...].astype(BF16)
     moment_basis = jnp.concatenate(monomials + [zero, zero], axis=0).astype(BF16)
-    g_rows[0:18, :] = jnp.zeros((18, pixels), F32)
+    g_rows[...] = jnp.zeros_like(g_rows)
 
     sub_e = lax.broadcasted_iota(jnp.int32, (8, entries), 0)
     own_chunk = jnp.where(sub_e == (lax.broadcasted_iota(jnp.int32, (8, entries), 1) & 7), 1.0, 0.0)
@@ -272,76 +273,88 @@
     def up(x, by, fill):
         return jnp.where(sub_p < 8 - by, pltpu.roll(x, 8 - by, 0), fill)
 
-    def tile(t, carry):
-        table = [coef[h, pl.ds(t, 32, stride=tiles), :] for h in range(halves)]
-        table = jnp.concatenate(table, axis=1)
-        lhs = table.T.astype(BF16)
-        a_scr[...] = jnp.exp2(jnp.minimum(dot(lhs, basis, 1, 0), 0.0))
-        trans = jnp.ones((8, pixels), F32)
+    def group(step, carry):
+        lanes = range(GROUP)
+        ts = [step * GROUP + u for u in lanes]
+        tables, lhs = [], []
+        for u in lanes:
+            table = [coef[h, pl.ds(ts[u], 32, stride=tiles), :] for h in range(halves)]
+            tables.append(jnp.concatenate(table, axis=1))
+            lhs.append(tables[u].T.astype(BF16))
+            a_scr[u] = jnp.exp2(jnp.minimum(dot(lhs[u], basis, 1, 0), 0.0))
+        trans = [jnp.ones((8, pixels), F32) for _ in lanes]
         for jj in range(entries // 16):
-            w = []
-            for h in range(2):
-                at = slice(16 * jj + 8 * h, 16 * jj + 8 * h + 8)
-                t_scr[at, :] = trans
-                value = trans * a_scr[at, :]
-                trans = trans - value
-                w.append(value)
-            at = slice(16 * jj, 16 * jj + 16)
-            whi_scr[at, :], wlo_scr[at, :] = split2(jnp.concatenate(w, axis=0))
-        colour = [own_chunk * table[18 + i : 19 + i, :] for i in range(3)]
-        colour = colour + [own_chunk * table[24 + i : 25 + i, :] for i in range(3)]
-        colour = jnp.concatenate(colour, axis=0).astype(BF16)
-        local = dot(colour, whi_scr[...], 1, 0) + dot(colour, wlo_scr[...], 1, 0)
-        local = [local[8 * i : 8 * i + 8, :] + local[24 + 8 * i : 32 + 8 * i, :] for i in range(3)]
-        before = down(trans, 1, 1.0)
-        for by in (1, 2, 4):
-            before = before * down(before, by, 1.0)
-        tinted = []
-        inner = jnp.zeros((8, pixels), F32)
-        for i in range(3):
-            image = jnp.sum(before * local[i], axis=0, keepdims=True)
-            images_ref[0, 0, 0, t, i : i + 1, :] = image
-            residual = image - target_ref[0, 0, 0, t, i : i + 1, :]
-            first = residual.astype(BF16).astype(F32)
-            second = (residual - first).astype(BF16).astype(F32)
-            g_rows[18 + i : 19 + i, :] = first
-            g_rows[21 + i : 22 + i, :] = second
-            g_rows[24 + i : 25 + i, :] = first
-            g_rows[27 + i : 28 + i, :] = second
-            tinted.append(before * residual)
-            inner = inner + residual * local[i]
-        q_scr[...] = dot(lhs, g_rows[...].astype(BF16), 1, 0)
-        tinted_hi, tinted_lo = split2(jnp.concatenate(tinted, axis=0))
-        tinted = jnp.concatenate([tinted_hi.astype(F32), tinted_lo.astype(F32)], axis=0).astype(BF16)
-        colour_grad = dot(tinted, whi_scr[...], 1, 1) + dot(tinted, wlo_scr[...], 1, 1)
+            for u in lanes:
+                w = []
+                for h in range(2):
+                    at = slice(16 * jj + 8 * h, 16 * jj + 8 * h + 8)
+                    t_scr[u, at, :] = trans[u]
+                    value = trans[u] * a_scr[u, at, :]
+                    trans[u] = trans[u] - value
+                    w.append(value)
+                at = slice(16 * jj, 16 * jj + 16)
+                whi_scr[u, at, :], wlo_scr[u, at, :] = split2(jnp.concatenate(w, axis=0))
+        befores, tints, behinds = [], [], []
+        for u in lanes:
+            table, t = tables[u], ts[u]
+            colour = [own_chunk * table[18 + i : 19 + i, :] for i in range(3)]
+            colour = colour + [own_chunk * table[24 + i : 25 + i, :] for i in range(3)]
+            colour = jnp.concatenate(colour, axis=0).astype(BF16)
+            local = dot(colour, whi_scr[u], 1, 0) + dot(colour, wlo_scr[u], 1, 0)
+            local = [local[8 * i : 8 * i + 8, :] + local[24 + 8 * i : 32 + 8 * i, :] for i in range(3)]
+            before = down(trans[u], 1, 1.0)
+            for by in (1, 2, 4):
+                before = before * down(before, by, 1.0)
+            tinted = []
+            inner = jnp.zeros((8, pixels), F32)
+            for i in range(3):
+                image = jnp.sum(before * local[i], axis=0, keepdims=True)
+                images_ref[0, 0, 0, t, i : i + 1, :] = image
+                residual = image - target_ref[0, 0, 0, t, i : i + 1, :]
+                first = residual.astype(BF16).astype(F32)
+                second = (residual - first).astype(BF16).astype(F32)
+                g_rows[u, 18 + i : 19 + i, :] = first
+                g_rows[u, 21 + i : 22 + i, :] = second
+                g_rows[u, 24 + i : 25 + i, :] = first
+                g_rows[u, 27 + i : 28 + i, :] = second
+                tinted.append(before * residual)
+                inner = inner + residual * local[i]
+            q_scr[u] = dot(lhs[u], g_rows[u].astype(BF16), 1, 0)
+            tinted_hi, tinted_lo = split2(jnp.concatenate(tinted, axis=0))
+            tints.append(jnp.concatenate([tinted_hi.astype(F32), tinted_lo.astype(F32)], axis=0).astype(BF16))
+            add = up(inner, 1, 0.0)
+            scale = up(trans[u], 1, 0.0)
+            for by in (1, 2, 4):
+                add = add + scale * up(add, by, 0.0)
+                scale = scale * up(scale, by, 0.0)
+            behinds.append(add)
+            befores.append(before)
         rows_out = []
-        for i in range(3):
-            both = colour_grad[8 * i : 8 * i + 8, :] + colour_grad[24 + 8 * i : 32 + 8 * i, :]
-            rows_out.append(jnp.sum(own_chunk * both, axis=0, keepdims=True))
-        add = up(inner, 1, 0.0)
-        scale = up(trans, 1, 0.0)
-        for by in (1, 2, 4):
-            add = add + scale * up(add, by, 0.0)
-            scale = scale * up(scale, by, 0.0)
-        behind = add
+        for u in lanes:
+            colour_grad = dot(tints[u], whi_scr[u], 1, 1) + dot(tints[u], wlo_scr[u], 1, 1)
+            for i in range(3):
+                both = colour_grad[8 * i : 8 * i + 8, :] + colour_grad[24 + 8 * i : 32 + 8 * i, :]
+                rows_out.append(jnp.sum(own_chunk * both, axis=0, keepdims=True))
         for jj in reversed(range(entries // 16)):
-            g = [None, None]
-            for h in (1, 0):
-                at = slice(16 * jj + 8 * h, 16 * jj + 8 * h + 8)
-                moved = a_scr[at, :] * (q_scr[at, :] - behind)
-                behind = behind + moved
-                g[h] = (t_scr[at, :] * before) * moved
-            at = slice(16 * jj, 16 * jj + 16)
-            ghi_scr[at, :], glo_scr[at, :] = split2(jnp.concatenate(g, axis=0))
-        moments = dot(moment_basis, ghi_scr[...], 1, 1) + dot(moment_basis, glo_scr[...], 1, 1)
-        for h in range(halves):
-            columns = slice(h * LANES, (h + 1) * LANES)
-            mom[h, pl.ds(t, 8, stride=tiles), :] = moments[:, columns]
-            for i in range(3):
-                mom[h, pl.ds((8 + i) * tiles + t, 1), :] = rows_out[i][:, columns]
+            for u in lanes:
+                g = [None, None]
+                for h in (1, 0):
+                    at = slice(16 * jj + 8 * h, 16 * jj + 8 * h + 8)
+                    moved = a_scr[u, at, :] * (q_scr[u, at, :] - behinds[u])
+                    behinds[u] = behinds[u] + moved
+                    g[h] = (t_scr[u, at, :] * befores[u]) * moved
+                at = slice(16 * jj, 16 * jj + 16)
+                ghi_scr[u, at, :], glo_scr[u, at, :] = split2(jnp.concatenate(g, axis=0))
+        for u in lanes:
+            moments = dot(moment_basis, ghi_scr[u], 1, 1) + dot(moment_basis, glo_scr[u], 1, 1)
+            for h in range(halves):
+                columns = slice(h * LANES, (h + 1) * LANES)
+                mom[h, pl.ds(ts[u], 8, stride=tiles), :] = moments[:, columns]
+                for i in range(3):
+                    mom[h, pl.ds((8 + i) * tiles + ts[u], 1), :] = rows_out[3 * u + i][:, columns]
         return carry
 
-    lax.fori_loop(0, tiles, tile, 0)
+    lax.fori_loop(0, tiles // GROUP, group, 0)
 
     def got(i):
         return jnp.concatenate([mom[h, i * tiles : (i + 1) * tiles, :] for h in range(halves)], axis=1)
@@ -384,14 +397,14 @@
         + [jax.ShapeDtypeStruct(target.shape, F32)],
         scratch_shapes=[
             pltpu.VMEM((entries // LANES, 32 * tiles, LANES), F32),
-            pltpu.VMEM((entries, pixels), F32),
-            pltpu.VMEM((entries, pixels), F32),
-            pltpu.VMEM((entries, pixels), F32),
-            pltpu.VMEM((entries, pixels), BF16),
-            pltpu.VMEM((entries, pixels), BF16),
-            pltpu.VMEM((entries, pixels), BF16),
-            pltpu.VMEM((entries, pixels), BF16),
-            pltpu.VMEM((32, pixels), F32),
+            pltpu.VMEM((GROUP, entries, pixels), F32),
+            pltpu.VMEM((GROUP, entries, pixels), F32),
+            pltpu.VMEM((GROUP, entries, pixels), F32),
+            pltpu.VMEM((GROUP, entries, pixels), BF16),
+            pltpu.VMEM((GROUP, entries, pixels), BF16),
+            pltpu.VMEM((GROUP, entries, pixels), BF16),
+            pltpu.VMEM((GROUP, entries, pixels), BF16),
+            pltpu.VMEM((GROUP, 32, pixels), F32),
             pltpu.VMEM((entries // LANES, 11 * tiles, LANES), F32),
             pltpu.VMEM((2 * FEATS * nd * rows, tiles * entries), BF16),
             pltpu.VMEM((LANES, tiles * entries), BF16),

time: 53.5 us -> 41.9 us (0.78)
  Pallas kernels: 26.9 us -> 15.3 us
    pallas_call x1, Pallas kernels: 20.6 us -> 9.03 us  [render(): pl.pallas_call(partial(render_kernel, nd=nd, cap=cap, rows=rows, tiles=ti...]
  transfers between devices with their start and end apart: 9 -> 9, of which waited for: 7 -> 7; matrix products, arithmetic and copies ran while one was open for 3% -> 4% of each run, Pallas kernels for 0% -> 0%
where the time goes in v2:
time: 41.9 us; the launch traced here: 41.6 us
  Pallas kernels  15.3 us (37%)
  starting transfers between devices  12.8 us (31%)
  waiting for transfers between devices  9.44 us (23%)
  local copies, waits for them, and re-layouts  3.33 us (8%)
  between operations  0.73 us (2%)
    pallas_call x1, Pallas kernels, render(): pl.pallas_call(partial(render_kernel, nd=nd, cap=cap, rows=rows, tiles=ti...  9.03 us
    ppermute x3, starting transfers between devices, local(): lax.ppermute(packets[j], 'dev', [(i, (i + j) % nd) for i in range(nd)])  7.01 us
    ppermute x3, waiting for transfers between devices, local(): lax.ppermute(returns[j], 'dev', [((i + j) % nd, i) for i in range(nd)])  5.12 us
    ppermute x3, starting transfers between devices, local(): lax.ppermute(returns[j], 'dev', [((i + j) % nd, i) for i in range(nd)])  3.84 us
    unnamed x20, local copies, waits for them, and re-layouts  3.33 us
    pallas_call x1, Pallas kernels, owner_sums(): pl.pallas_call(partial(owner_kernel, nd=nd, rows=rows, parts=parts, nv=nv...  2.79 us
    ppermute x3, waiting for transfers between devices, local(): lax.ppermute(piece, ('view', 'chip'), pairs)  2.58 us
    pallas_call x1, Pallas kernels, send(): pl.pallas_call(partial(send_kernel, nd=nd, cap=cap, rows=rows), in_specs=...  2.25 us
  transfers between devices with their start and end apart: 9, of which 7 were waited for; matrix products, arithmetic and copies ran while one was open for 4% of the time, Pallas kernels for 0%

profile of v2, /device:TPU:0, one launch (start us, length us, event | category | flops | bytes accessed | tf_op | source)
XLA Modules:
  0.0 41.6 jit_solution(4453433458373543652)
XLA Ops:
  0.6 0.0 copy-start.2
  0.6 0.0 copy-start.5
  0.7 0.0 copy-start.6
  0.7 0.1 pad_add_fusion.me_ref
  0.7 0.6 %copy-done.2 = s32[1,4,1,1,960]{4,3,2,1,0:T(1,128)S(1)} copy-done((s32[1,4,1,1,960]{4,3,2,1,0:T(1,128)S(1)}, s32[1,4,1,1,960]{4,3,2,1,0:T(1,128)}, u32[]{:S(2)}) %copy-start.2) | copy-done | bytes 15384
  1.3 0.0 copy-done.5
  1.4 0.0 copy-done.6
  1.4 0.0 copy-start
  1.4 1.2 %copy-done = f32[58,4096]{1,0:T(8,128)S(1)} copy-done((f32[58,4096]{1,0:T(8,128)S(1)}, f32[58,4096]{1,0:T(8,128)}, u32[]{:S(2)}) %copy-start) | copy-done | bytes 950296
  2.6 0.0 copy-start.1
  2.6 2.3 %project_gather.1 = (f32[9,8,128]{2,1,0:T(8,128)S(1)}, f32[9,8,128]{2,1,0:T(8,128)S(1)}, f32[9,8,128]{2,1,0:T(8,128)S(1)}, f32[9,8,128]{2,1,0:T(8,128)S(1)}, s32...) custom-call(s32[3]{0:T(128)S(1)} %pad_add_fusion.me_ref, f32[1,2,4]{2,1,0:T(2,128)S(1)} %copy-done.5, f32[1,16]{1,0:T(1,128)S(1)} %copy-done.6, ...), custom_call_target="tpu_custom_call" | custom-call | tf_op jit(solution)/shard_map/project_gather/pallas_call | solution.py:131
  4.8 3.1 %collective-permute-start = (f32[9,8,128]{2,1,0:T(8,128)S(1)}, f32[9,8,128]{2,1,0:T(8,128)S(1)}, u32[]{:S(2)}, u32[]{:S(2)}) collective-permute-start(f32[9,8,128]{2,1,0:T(8,128)S(1)} %get-tuple-element.18), channel_id=1, source_target_pairs={{0,4},{4,8},{8,12},{12,0},{1,5},{5,9},{9,13},{13,1},{2,6},{6,10},{... | collective-permute-start | bytes 110600 | tf_op jit(solution)/shard_map/ppermute | solution.py:572
  7.9 2.6 %collective-permute-start.1 = (f32[9,8,128]{2,1,0:T(8,128)S(1)}, f32[9,8,128]{2,1,0:T(8,128)S(1)}, u32[]{:S(2)}, u32[]{:S(2)}) collective-permute-start(f32[9,8,128]{2,1,0:T(8,128)S(1)} %get-tuple-element.19), channel_id=1, source_target_pairs={{0,8},{4,12},{8,0},{12,4},{1,9},{5,13},{9,1},{13,5},{2,10},{6,14},... | collective-permute-start | bytes 110600 | tf_op jit(solution)/shard_map/ppermute | solution.py:572
  10.5 0.0 copy-start.3
  10.5 0.0 copy-start.4
  10.5 1.3 %collective-permute-start.2 = (f32[9,8,128]{2,1,0:T(8,128)S(1)}, f32[9,8,128]{2,1,0:T(8,128)S(1)}, u32[]{:S(2)}, u32[]{:S(2)}) collective-permute-start(f32[9,8,128]{2,1,0:T(8,128)S(1)} %get-tuple-element.20), channel_id=1, source_target_pairs={{0,12},{4,0},{8,4},{12,8},{1,13},{5,1},{9,5},{13,9},{2,14},{6,2},{... | collective-permute-start | bytes 110600 | tf_op jit(solution)/shard_map/ppermute | solution.py:572
  11.9 0.8 %copy.11.refs_8_ = f32[1,1,1,16,3,256]{5,4,3,2,1,0:T(4,128)S(1)} copy(f32[1,1,1,16,3,256]{5,3,4,2,1,0:T(8,128)} %param.17) | data formatting | bytes 98304 | tf_op args[8]
  12.7 0.0 copy-start.7
  12.7 0.0 copy-start.8
  12.7 0.0 collective-permute-done.refs_1_
  12.7 0.4 %collective-permute-done.1.refs_2_ = f32[9,8,128]{2,1,0:T(8,128)S(1)} collective-permute-done((f32[9,8,128]{2,1,0:T(8,128)S(1)}, f32[9,8,128]{2,1,0:T(8,128)S(1)}, u32[]{:S(2)}, u32[]{:S(2)}) %collective-permute-start.1) | collective-permute-done | bytes 36896 | tf_op jit(solution)/shard_map/ppermute | solution.py:572
  13.2 1.3 %collective-permute-done.2.refs_3_ = f32[9,8,128]{2,1,0:T(8,128)S(1)} collective-permute-done((f32[9,8,128]{2,1,0:T(8,128)S(1)}, f32[9,8,128]{2,1,0:T(8,128)S(1)}, u32[]{:S(2)}, u32[]{:S(2)}) %collective-permute-start.2) | collective-permute-done | bytes 36896 | tf_op jit(solution)/shard_map/ppermute | solution.py:572
  14.5 0.0 copy-done.3
  14.5 0.0 copy-done.4
  14.5 0.0 copy-done.7
  14.5 0.0 copy-done.8
  14.5 9.0 %render_tiles.1 = (f32[9,8,128]{2,1,0:T(8,128)S(1)}, f32[9,8,128]{2,1,0:T(8,128)S(1)}, f32[9,8,128]{2,1,0:T(8,128)S(1)}, f32[9,8,128]{2,1,0:T(8,128)S(1)}, f32[1,1,1,16,3,256]{5,4,3,2,1,0:T(4,128)S(1)}) custom-call(s32[3]{0:T(128)S(1)} %pad_add_fusion.me_ref, f32[9,8,128]{2,1,0:T(8,128)S(1)} %get-tuple-element.17.refs_0_, ...), custom_call_target="tpu_custom_call" | custom-call | tf_op jit(solution)/shard_map/render_tiles/pallas_call | solution.py:392
  23.5 3.2 %collective-permute-start.3 = (f32[9,8,128]{2,1,0:T(8,128)S(1)}, f32[9,8,128]{2,1,0:T(8,128)S(1)}, u32[]{:S(2)}, u32[]{:S(2)}) collective-permute-start(f32[9,8,128]{2,1,0:T(8,128)S(1)} %get-tuple-element.22), channel_id=1, source_target_pairs={{4,0},{8,4},{12,8},{0,12},{5,1},{9,5},{13,9},{1,13},{6,2},{10,6},{... | collective-permute-start | bytes 110600 | tf_op jit(solution)/shard_map/ppermute | solution.py:578
  26.7 0.0 collective-permute-start.4
  26.7 0.6 %collective-permute-start.5 = (f32[9,8,128]{2,1,0:T(8,128)S(1)}, f32[9,8,128]{2,1,0:T(8,128)S(1)}, u32[]{:S(2)}, u32[]{:S(2)}) collective-permute-start(f32[9,8,128]{2,1,0:T(8,128)S(1)} %get-tuple-element.24), channel_id=1, source_target_pairs={{12,0},{0,4},{4,8},{8,12},{13,1},{1,5},{5,9},{9,13},{14,2},{2,6},{... | collective-permute-start | bytes 110600 | tf_op jit(solution)/shard_map/ppermute | solution.py:578
  27.4 1.0 %collective-permute-done.3.refs_1_ = f32[9,8,128]{2,1,0:T(8,128)S(1)} collective-permute-done((f32[9,8,128]{2,1,0:T(8,128)S(1)}, f32[9,8,128]{2,1,0:T(8,128)S(1)}, u32[]{:S(2)}, u32[]{:S(2)}) %collective-permute-start.3) | collective-permute-done | bytes 36896 | tf_op jit(solution)/shard_map/ppermute | solution.py:578
  28.4 3.2 %collective-permute-done.4.refs_2_ = f32[9,8,128]{2,1,0:T(8,128)S(1)} collective-permute-done((f32[9,8,128]{2,1,0:T(8,128)S(1)}, f32[9,8,128]{2,1,0:T(8,128)S(1)}, u32[]{:S(2)}, u32[]{:S(2)}) %collective-permute-start.4) | collective-permute-done | bytes 36896 | tf_op jit(solution)/shard_map/ppermute | solution.py:578
  31.6 0.9 %collective-permute-done.5.refs_3_ = f32[9,8,128]{2,1,0:T(8,128)S(1)} collective-permute-done((f32[9,8,128]{2,1,0:T(8,128)S(1)}, f32[9,8,128]{2,1,0:T(8,128)S(1)}, u32[]{:S(2)}, u32[]{:S(2)}) %collective-permute-start.5) | collective-permute-done | bytes 36896 | tf_op jit(solution)/shard_map/ppermute | solution.py:578
  32.5 2.8 %owner_sums.1 = (f32[10,8,128]{2,1,0:T(8,128)S(1)}, f32[10,8,128]{2,1,0:T(8,128)S(1)}, f32[10,8,128]{2,1,0:T(8,128)S(1)}, f32[10,8,128]{2,1,0:T(8,128)S(1)}) custom-call(s32[3]{0:T(128)S(1)} %pad_add_fusion.me_ref, f32[9,8,128]{2,1,0:T(8,128)S(1)} %get-tuple-element.21.refs_0_, f32[9,8,128]{2,1,0:T(8,128)S(1)} %collective-permute-done.3.refs_1_, ...), custom_call_target="tpu_custom_call" | custom-call | tf_op jit(solution)/shard_map/owner_sums/pallas_call | solution.py:452
  35.3 0.1 collective-permute-start.6
  35.4 1.6 %collective-permute-start.7 = (f32[10,8,128]{2,1,0:T(8,128)S(1)}, f32[10,8,128]{2,1,0:T(8,128)S(1)}, u32[]{:S(2)}, u32[]{:S(2)}) collective-permute-start(f32[10,8,128]{2,1,0:T(8,128)S(1)} %get-tuple-element.29), channel_id=1, source_target_pairs={{0,2},{1,3},{2,0},{3,1},{4,6},{5,7},{6,4},{7,5},{8,10},{9,11},{10,... | collective-permute-start | bytes 122888 | tf_op jit(solution)/shard_map/ppermute | solution.py:587
  36.9 0.3 collective-permute-start.8
  37.2 0.6 %copy.12 = f32[1,1,1,16,3,256]{5,3,4,2,1,0:T(8,128)} copy(f32[1,1,1,16,3,256]{5,4,3,2,1,0:T(4,128)S(1)} %get-tuple-element.33) | data formatting | bytes 98304
  37.9 0.0 collective-permute-done.6.refs_1_
  37.9 1.6 %collective-permute-done.7.refs_2_ = f32[10,8,128]{2,1,0:T(8,128)S(1)} collective-permute-done((f32[10,8,128]{2,1,0:T(8,128)S(1)}, f32[10,8,128]{2,1,0:T(8,128)S(1)}, u32[]{:S(2)}, u32[]{:S(2)}) %collective-permute-start.7) | collective-permute-done | bytes 40992 | tf_op jit(solution)/shard_map/ppermute | solution.py:587
  39.4 1.0 %collective-permute-done.8.refs_3_ = f32[10,8,128]{2,1,0:T(8,128)S(1)} collective-permute-done((f32[10,8,128]{2,1,0:T(8,128)S(1)}, f32[10,8,128]{2,1,0:T(8,128)S(1)}, u32[]{:S(2)}, u32[]{:S(2)}) %collective-permute-start.8) | collective-permute-done | bytes 40992 | tf_op jit(solution)/shard_map/ppermute | solution.py:587
  40.4 0.0 copy-done.1
  40.4 1.2 %pull_back.1 = f32[58,1024]{1,0:T(8,128)} custom-call(s32[1]{0:T(128)} %bitcast.at_ref, f32[58,4096]{1,0:T(8,128)S(1)} %copy-done.1, f32[10,8,128]{2,1,0:T(8,128)S(1)} %get-tuple-element.27.refs_0_, f32[10,8,128]{2,1,0:T(8,128)S(1)} %collective-permute-done.6.refs_1_, f32[10,8,128]{2,1,0:T(8,128)S(1)} %collective-permute-done.7.refs_2_, ...), custom_call_target="tpu_custom_call" | custom-call | tf_op jit(solution)/shard_map/pull_back/pallas_call | solution.py:531
Async XLA Ops:
  0.6 0.7 %copy-start.2 = (s32[1,4,1,1,960]{4,3,2,1,0:T(1,128)S(1)}, s32[1,4,1,1,960]{4,3,2,1,0:T(1,128)}, u32[]{:S(2)}) copy-start(s32[1,4,1,1,960]{4,3,2,1,0:T(1,128)} %req_ref.1) | copy-start | bytes 46084
  0.6 0.7 %copy-start.5 = (f32[1,2,4]{2,1,0:T(2,128)S(1)}, f32[1,2,4]{2,1,0:T(2,128)}, u32[]{:S(2)}) copy-start(f32[1,2,4]{2,1,0:T(2,128)} %cam_ref.1) | copy-start | bytes 100
  0.7 0.7 %copy-start.6 = (f32[1,16]{1,0:T(1,128)S(1)}, f32[1,16]{1,0:T(1,128)}, u32[]{:S(2)}) copy-start(f32[1,16]{1,0:T(1,128)} %basis_ref.1) | copy-start | bytes 196
  1.4 1.2 %copy-start = (f32[58,4096]{1,0:T(8,128)S(1)}, f32[58,4096]{1,0:T(8,128)}, u32[]{:S(2)}) copy-start(f32[58,4096]{1,0:T(8,128)} %params_ref.3) | copy-start | bytes 2850820
  2.6 37.9 %copy-start.1 = (f32[58,4096]{1,0:T(8,128)S(1)}, f32[58,4096]{1,0:T(8,128)}, u32[]{:S(2)}) copy-start(f32[58,4096]{1,0:T(8,128)} %params_ref.3) | copy-start | bytes 2850820
  4.8 7.9 %collective-permute-start = (f32[9,8,128]{2,1,0:T(8,128)S(1)}, f32[9,8,128]{2,1,0:T(8,128)S(1)}, u32[]{:S(2)}, u32[]{:S(2)}) collective-permute-start(f32[9,8,128]{2,1,0:T(8,128)S(1)} %get-tuple-element.18), channel_id=1, source_target_pairs={{0,4},{4,8},{8,12},{12,0},{1,5},{5,9},{9,13},{13,1},{2,6},{6,10},{... | collective-permute-start | bytes 110600 | tf_op jit(solution)/shard_map/ppermute | solution.py:572
  7.9 5.3 %collective-permute-start.1 = (f32[9,8,128]{2,1,0:T(8,128)S(1)}, f32[9,8,128]{2,1,0:T(8,128)S(1)}, u32[]{:S(2)}, u32[]{:S(2)}) collective-permute-start(f32[9,8,128]{2,1,0:T(8,128)S(1)} %get-tuple-element.19), channel_id=1, source_target_pairs={{0,8},{4,12},{8,0},{12,4},{1,9},{5,13},{9,1},{13,5},{2,10},{6,14},... | collective-permute-start | bytes 110600 | tf_op jit(solution)/shard_map/ppermute | solution.py:572
  10.5 4.0 %copy-start.3 = (s32[1,1,1,16,256]{4,3,2,1,0:T(8,128)S(1)}, s32[1,1,1,16,256]{4,3,2,1,0:T(8,128)}, u32[]{:S(2)}) copy-start(s32[1,1,1,16,256]{4,3,2,1,0:T(8,128)} %refs_4_.1) | copy-start | bytes 49156
  10.5 4.0 %copy-start.4 = (s32[1,1,1,16,256]{4,3,2,1,0:T(8,128)S(1)}, s32[1,1,1,16,256]{4,3,2,1,0:T(8,128)}, u32[]{:S(2)}) copy-start(s32[1,1,1,16,256]{4,3,2,1,0:T(8,128)} %refs_5_.1) | copy-start | bytes 49156
  10.5 4.0 %collective-permute-start.2 = (f32[9,8,128]{2,1,0:T(8,128)S(1)}, f32[9,8,128]{2,1,0:T(8,128)S(1)}, u32[]{:S(2)}, u32[]{:S(2)}) collective-permute-start(f32[9,8,128]{2,1,0:T(8,128)S(1)} %get-tuple-element.20), channel_id=1, source_target_pairs={{0,12},{4,0},{8,4},{12,8},{1,13},{5,1},{9,5},{13,9},{2,14},{6,2},{... | collective-permute-start | bytes 110600 | tf_op jit(solution)/shard_map/ppermute | solution.py:572
  12.7 1.8 %copy-start.7 = (s32[1,1,1,16]{3,2,1,0:T(1,128)S(1)}, s32[1,1,1,16]{3,2,1,0:T(1,128)}, u32[]{:S(2)}) copy-start(s32[1,1,1,16]{3,2,1,0:T(1,128)} %refs_6_.1) | copy-start | bytes 196
  12.7 1.8 %copy-start.8 = (s32[1,1,1,16]{3,2,1,0:T(1,128)S(1)}, s32[1,1,1,16]{3,2,1,0:T(1,128)}, u32[]{:S(2)}) copy-start(s32[1,1,1,16]{3,2,1,0:T(1,128)} %refs_7_.1) | copy-start | bytes 196
  23.5 4.8 %collective-permute-start.3 = (f32[9,8,128]{2,1,0:T(8,128)S(1)}, f32[9,8,128]{2,1,0:T(8,128)S(1)}, u32[]{:S(2)}, u32[]{:S(2)}) collective-permute-start(f32[9,8,128]{2,1,0:T(8,128)S(1)} %get-tuple-element.22), channel_id=1, source_target_pairs={{4,0},{8,4},{12,8},{0,12},{5,1},{9,5},{13,9},{1,13},{6,2},{10,6},{... | collective-permute-start | bytes 110600 | tf_op jit(solution)/shard_map/ppermute | solution.py:578
  26.7 4.9 %collective-permute-start.4 = (f32[9,8,128]{2,1,0:T(8,128)S(1)}, f32[9,8,128]{2,1,0:T(8,128)S(1)}, u32[]{:S(2)}, u32[]{:S(2)}) collective-permute-start(f32[9,8,128]{2,1,0:T(8,128)S(1)} %get-tuple-element.23), channel_id=1, source_target_pairs={{8,0},{12,4},{0,8},{4,12},{9,1},{13,5},{1,9},{5,13},{10,2},{14,6},... | collective-permute-start | bytes 110600 | tf_op jit(solution)/shard_map/ppermute | solution.py:578
  26.7 5.8 %collective-permute-start.5 = (f32[9,8,128]{2,1,0:T(8,128)S(1)}, f32[9,8,128]{2,1,0:T(8,128)S(1)}, u32[]{:S(2)}, u32[]{:S(2)}) collective-permute-start(f32[9,8,128]{2,1,0:T(8,128)S(1)} %get-tuple-element.24), channel_id=1, source_target_pairs={{12,0},{0,4},{4,8},{8,12},{13,1},{1,5},{5,9},{9,13},{14,2},{2,6},{... | collective-permute-start | bytes 110600 | tf_op jit(solution)/shard_map/ppermute | solution.py:578
  35.3 2.6 %collective-permute-start.6 = (f32[10,8,128]{2,1,0:T(8,128)S(1)}, f32[10,8,128]{2,1,0:T(8,128)S(1)}, u32[]{:S(2)}, u32[]{:S(2)}) collective-permute-start(f32[10,8,128]{2,1,0:T(8,128)S(1)} %get-tuple-element.28), channel_id=1, source_target_pairs={{0,1},{1,0},{2,3},{3,2},{4,5},{5,4},{6,7},{7,6},{8,9},{9,8},{10,11... | collective-permute-start | bytes 122888 | tf_op jit(solution)/shard_map/ppermute | solution.py:587
  35.4 4.1 %collective-permute-start.7 = (f32[10,8,128]{2,1,0:T(8,128)S(1)}, f32[10,8,128]{2,1,0:T(8,128)S(1)}, u32[]{:S(2)}, u32[]{:S(2)}) collective-permute-start(f32[10,8,128]{2,1,0:T(8,128)S(1)} %get-tuple-element.29), channel_id=1, source_target_pairs={{0,2},{1,3},{2,0},{3,1},{4,6},{5,7},{6,4},{7,5},{8,10},{9,11},{10,... | collective-permute-start | bytes 122888 | tf_op jit(solution)/shard_map/ppermute | solution.py:587
  36.9 3.5 %collective-permute-start.8 = (f32[10,8,128]{2,1,0:T(8,128)S(1)}, f32[10,8,128]{2,1,0:T(8,128)S(1)}, u32[]{:S(2)}, u32[]{:S(2)}) collective-permute-start(f32[10,8,128]{2,1,0:T(8,128)S(1)} %get-tuple-element.30), channel_id=1, source_target_pairs={{0,3},{1,2},{2,1},{3,0},{4,7},{5,6},{6,5},{7,4},{8,11},{9,10},{10,... | collective-permute-start | bytes 122888 | tf_op jit(solution)/shard_map/ppermute | solution.py:587

commit v3 on v2

--- a/solution.py
+++ b/solution.py
@@ -17,6 +17,8 @@
 F32 = jnp.float32
 BF16 = jnp.bfloat16
 FEATS = 9
+FORTH = (1, 2, 3)
+BACK = (1, 2, 3)
 GROUP = 16
 
 
@@ -33,15 +35,32 @@
     return lax.dot_general(a, b, (((ca,), (cb,)), ((), ())), preferred_element_type=F32)
 
 
-def send_kernel(me_ref, cam_ref, basis_ref, params_ref, req_ref, *refs, nd, cap, rows):
-    outs = refs[:nd]
-    idx_out, w_out, feat, w_scr = refs[nd:]
-    me = me_ref[0]
+def send_kernel(cam_hbm, basis_hbm, params_hbm, req_hbm, *refs, later, nd, nc, cap, rows):
+    later_hbm = refs[:later]
+    outs = refs[later : later + nd]
+    idx_out, w_out, own_out = refs[later + nd : later + nd + 3]
+    later_out = refs[later + nd + 3 : 2 * later + nd + 3]
+    feat, w_scr, cam_ref, basis_ref, params_ref, req_ref, sems = refs[2 * later + nd + 3 :]
+    me = lax.axis_index("dev")
+    share = own_out.shape[1]
+    owned = pl.multiple_of((lax.axis_index("view") * nc + lax.axis_index("chip")) * share, LANES)
+    copies = [
+        (params_hbm, params_ref),
+        (cam_hbm, cam_ref),
+        (basis_hbm, basis_ref),
+        (req_hbm, req_ref),
+        (params_hbm.at[:, pl.ds(owned, share)], own_out),
+    ] + list(zip(later_hbm, later_out))
+    copies = [pltpu.make_async_copy(source, target, sems.at[i]) for i, (source, target) in enumerate(copies)]
+    for copy in copies:
+        copy.start()
+    for copy in copies[1:4]:
+        copy.wait()
     width = params_ref.shape[1]
     coefs = basis_ref.shape[-1]
     idx_out[...] = jnp.zeros_like(idx_out)
     for j in range(nd):
-        dest = lax.rem(me + j, nd)
+        dest = me ^ j
         for i in range(rows):
             size = min(LANES, cap - i * LANES)
             idx_out[j * rows + i : j * rows + i + 1, 0:size] = req_ref[
@@ -62,6 +81,7 @@
     weights = weights + jnp.where(row8 == 3, pltpu.roll(basis_row, 10 + coefs, 1), 0.0)
     weights = weights + jnp.where(row8 == 4, pltpu.roll(basis_row, 10 + 2 * coefs, 1), 0.0)
     w_scr[...] = weights
+    copies[0].wait()
     linear = lax.dot_general(
         w_scr[:, 0 : params_ref.shape[0]],
         params_ref[...],
@@ -117,6 +137,8 @@
                         outs[j][f, i : i + step, :] = acc[f]
                 else:
                     outs[j][f, i : i + 1, :] = acc[f][n : n + 1, :]
+    for copy in copies[4:]:
+        copy.wait()
 
 
 def vmem_spec():
@@ -127,50 +149,84 @@
     return pl.BlockSpec(memory_space=pltpu.SMEM)
 
 
-def send(me, cameras, basis, params, requests, nd, cap, rows):
+def send(cameras, basis, params, requests, later, nd, nv, nc, cap, rows):
+    count, width = params.shape
+    first = (cameras, basis, params, requests)
+    out_shape = [jax.ShapeDtypeStruct((FEATS, rows, LANES), F32)] * nd
+    out_shape += [
+        jax.ShapeDtypeStruct((nd * rows, LANES), jnp.int32),
+        jax.ShapeDtypeStruct((8, LANES), F32),
+        jax.ShapeDtypeStruct((count, width // (nv * nc)), F32),
+    ]
+    out_shape += [jax.ShapeDtypeStruct(x.shape, x.dtype) for x in later]
     return pl.pallas_call(
-        partial(send_kernel, nd=nd, cap=cap, rows=rows),
-        in_specs=[smem_spec()] + [vmem_spec()] * 4,
-        out_specs=[vmem_spec()] * (nd + 2),
-        out_shape=[jax.ShapeDtypeStruct((FEATS, rows, LANES), F32)] * nd
-        + [
-            jax.ShapeDtypeStruct((nd * rows, LANES), jnp.int32),
-            jax.ShapeDtypeStruct((8, LANES), F32),
-        ],
-        scratch_shapes=[pltpu.VMEM((16, params.shape[1]), F32), pltpu.VMEM((8, LANES), F32)],
-        compiler_params=pltpu.CompilerParams(vmem_limit_bytes=40 * 1024 * 1024),
+        partial(send_kernel, later=len(later), nd=nd, nc=nc, cap=cap, rows=rows),
+        in_specs=[pl.BlockSpec(memory_space=pl.ANY)] * (4 + len(later)),
+        out_specs=[vmem_spec()] * len(out_shape),
+        out_shape=out_shape,
+        scratch_shapes=[pltpu.VMEM((16, width), F32), pltpu.VMEM((8, LANES), F32)]
+        + [pltpu.VMEM(x.shape, x.dtype) for x in first]
+        + [pltpu.SemaphoreType.DMA((5 + len(later),))],
+        compiler_params=pltpu.CompilerParams(vmem_limit_bytes=60 * 1024 * 1024),
         name="project_gather",
-    )(me, cameras, basis, params, requests)
-
-
-def scatter_products(value_rows, index_rows, spread, hot, out_rows):
-    width = value_rows[0][0].shape[1]
-    for n, (values, (high, low)) in enumerate(zip(value_rows, index_rows)):
-        columns = slice(n * width, (n + 1) * width)
-        high_iota = lax.broadcasted_iota(jnp.int32, (out_rows, width), 0)
-        low_iota = lax.broadcasted_iota(jnp.int32, (LANES, width), 0)
-        here = high_iota == high
-        hot[:, columns] = jnp.where(low_iota == low, 1.0, 0.0).astype(BF16)
+    )(*first, *later)
+
+
+def fold_of(block):
+    return 2 if block % 2 == 0 else 1
+
+
+def fold(row, lane, block):
+    wide = fold_of(block)
+    height = block // wide
+    inside = lax.rem(row, block)
+    return lax.div(row, block) * height + lax.rem(inside, height), lax.div(inside, height) * LANES + lane
+
+
+def place_hot(hot, at, column, wide):
+    size = column.shape[0]
+    lane = lax.broadcasted_iota(jnp.int32, (size, wide * LANES), 1)
+    hot[at : at + size, :] = jnp.where(lane == column, 1.0, 0.0).astype(BF16)
+
+
+def place_mask(mask, at, row):
+    size = row.shape[1]
+    high = lax.broadcasted_iota(jnp.int32, (mask.shape[0], size), 0)
+    mask[:, at : at + size] = jnp.where(high == row, 1.0, 0.0).astype(BF16)
+
+
+def place_values(spread, at, mask, values):
+    height, size = mask.shape
+    for f, pair in enumerate(values):
+        for part, row in enumerate(pair):
+            base = (part * FEATS + f) * height
+            wide_row = jnp.broadcast_to(row, (height, size)).astype(BF16)
+            spread[base : base + height, at : at + size] = mask * wide_row
+
+
+def exact_parts(x):
+    hi = x.astype(BF16).astype(F32)
+    return hi, (x - hi).astype(BF16).astype(F32)
+
+
+def take_rows(source, high, low, first_row, count, start):
+    acc = list(start)
+    for n in range(first_row, first_row + count):
+        here = high == n
         for f in range(FEATS):
-            hi, lo = split2(values[f])
-            hi, lo = hi.astype(F32), lo.astype(F32)
-            spread[f * out_rows : (f + 1) * out_rows, columns] = jnp.where(here, hi, 0.0).astype(BF16)
-            base = (FEATS + f) * out_rows
-            spread[base : base + out_rows, columns] = jnp.where(here, lo, 0.0).astype(BF16)
-
-
-def render_kernel(me_ref, *refs, nd, cap, rows, tiles, entries):
-    recv = refs[:nd]
-    blocks_ref, orders_ref, counts_ref, ids_ref, target_ref = refs[nd : nd + 5]
-    outs = refs[nd + 5 : 2 * nd + 5]
-    (images_ref, coef, a_scr, t_scr, q_scr, whi_scr, wlo_scr, ghi_scr, glo_scr, g_rows, mom, spread, hot) = refs[
-        2 * nd + 5 :
-    ]
-    me = me_ref[0]
-    pixels = SIDE * SIDE
+            value = jnp.broadcast_to(source(f, n), low.shape)
+            acc[f] = jnp.where(here, lane_take(value, low), acc[f])
+    return acc
+
+
+def index_kernel(
+    own_ref, blocks_ref, orders_ref, counts_ref, high_out, low_out, live_out, part_out, mask_out, hot_out, *, nd, cap
+):
+    me = lax.axis_index("dev")
+    rows = own_ref.shape[1]
+    tiles, entries = blocks_ref.shape[3:]
     chunk = entries // 8
     halves = entries // LANES
-    table_rows = nd * rows
 
     place = lax.broadcasted_iota(jnp.int32, (tiles, entries), 1)
     rank = (place & 7) * chunk + (place >> 3)
@@ -187,44 +243,92 @@
             parts.append(value)
         return jnp.concatenate(parts, axis=1)
 
-    def put(ref, at, value):
-        for h in range(halves):
-            ref[h, at : at + value.shape[0], :] = value[:, h * LANES : (h + 1) * LANES]
-
-    def column(ref):
-        square = jnp.broadcast_to(ref[0, 0].astype(F32), (tiles, tiles))
-        diagonal = lax.broadcasted_iota(jnp.int32, (tiles, tiles), 0) == lax.broadcasted_iota(
-            jnp.int32, (tiles, tiles), 1
-        )
-        return jnp.sum(jnp.where(diagonal, square, 0.0), axis=1, keepdims=True).astype(jnp.int32)
-
     order = take_wide(orders_ref[0, 0, 0], rank)
     slot = take_wide(blocks_ref[0, 0, 0], order)
     shard = jnp.zeros_like(slot)
     for i in range(1, nd):
         shard = shard + (slot >= i * cap).astype(jnp.int32)
     offset = slot - shard * cap
-    hop = me - shard
-    hop = jnp.where(hop < 0, hop + nd, hop)
-    slot_row = hop * rows + (offset >> 7)
+    slot_row = (shard ^ me) * rows + (offset >> 7)
     slot_lane = offset & (LANES - 1)
-    live = rank < column(counts_ref)
-    tile_id = column(ids_ref)
+    high_out[...] = slot_row
+    low_out[...] = slot_lane
+    live_out[...] = jnp.where(rank < column_of(counts_ref, tiles), 1.0, 0.0)
+    for c in range(halves):
+        columns = slice(c * LANES, (c + 1) * LANES)
+        for first in range(0, tiles, 8):
+            low = slot_lane[first : first + 8, columns]
+            high = slot_row[first : first + 8, columns]
+            start = [jnp.zeros((8, LANES), F32)] * FEATS
+            acc = take_rows(lambda f, n: own_ref[f, n : n + 1, :], high, low, 0, rows, start)
+            for f in range(FEATS):
+                part_out[f, first : first + 8, columns] = acc[f]
+    wide = fold_of(rows)
+    key_high, key_low = fold(slot_row, slot_lane, rows)
+    key_columns = key_low.astype(F32).T.astype(jnp.int32)
+    for t in range(tiles):
+        place_mask(mask_out, t * entries, key_high[t : t + 1, :])
+        place_hot(hot_out, t * entries, key_columns[:, t : t + 1], wide)
+
+
+def tile_indices(own, blocks, orders, counts, nd, cap):
+    rows = own.shape[1]
+    tiles, entries = blocks.shape[3:]
+    wide = fold_of(rows)
+    return pl.pallas_call(
+        partial(index_kernel, nd=nd, cap=cap),
+        in_specs=[vmem_spec()] * 4,
+        out_specs=[vmem_spec()] * 6,
+        out_shape=[
+            jax.ShapeDtypeStruct((tiles, entries), jnp.int32),
+            jax.ShapeDtypeStruct((tiles, entries), jnp.int32),
+            jax.ShapeDtypeStruct((tiles, entries), F32),
+            jax.ShapeDtypeStruct((FEATS, tiles, entries), F32),
+            jax.ShapeDtypeStruct((nd * rows // wide, tiles * entries), BF16),
+            jax.ShapeDtypeStruct((tiles * entries, wide * LANES), BF16),
+        ],
+        compiler_params=pltpu.CompilerParams(vmem_limit_bytes=40 * 1024 * 1024),
+        name="prep_tiles",
+    )(own, blocks, orders, counts)
+
+
+def column_of(ref, tiles):
+    square = jnp.broadcast_to(ref[0, 0].astype(F32), (tiles, tiles))
+    diagonal = lax.broadcasted_iota(jnp.int32, (tiles, tiles), 0) == lax.broadcasted_iota(jnp.int32, (tiles, tiles), 1)
+    return jnp.sum(jnp.where(diagonal, square, 0.0), axis=1, keepdims=True).astype(jnp.int32)
+
+
+def render_kernel(*refs, nd, rows, tiles, entries):
+    recv = refs[: nd - 1]
+    high_ref, low_ref, live_ref, part_ref, mask_ref, hot_ref, ids_ref, target_ref = refs[nd - 1 : nd + 7]
+    outs = refs[nd + 7 : 2 * nd + 7]
+    (images_ref, coef, a_scr, t_scr, q_scr, whi_scr, wlo_scr, ghi_scr, glo_scr, g_rows, mom, spread) = refs[2 * nd + 7 :]
+    pixels = SIDE * SIDE
+    halves = entries // LANES
+    table_rows = nd * rows
+
+    def put(ref, at, value):
+        for h in range(halves):
+            ref[h, at : at + value.shape[0], :] = value[:, h * LANES : (h + 1) * LANES]
+
+    tile_id = column_of(ids_ref, tiles)
     centre_x = ((tile_id % TW) * SIDE).astype(F32) + 0.5 * SIDE
     centre_y = ((tile_id // TW) * SIDE).astype(F32) + 0.5 * SIDE
-
-    pieces = [[None] * halves for _ in range(FEATS)]
+    live = live_ref[...] > 0.5
+
+    pieces = [[[] for _ in range(halves)] for _ in range(FEATS)]
     for c in range(halves):
-        low = slot_lane[:, c * LANES : (c + 1) * LANES]
-        high = slot_row[:, c * LANES : (c + 1) * LANES]
-        acc = [jnp.zeros((tiles, LANES), F32) for _ in range(FEATS)]
-        for n in range(table_rows):
-            here = high == n
+        columns = slice(c * LANES, (c + 1) * LANES)
+        for first in range(0, tiles, 8):
+            low = low_ref[first : first + 8, columns]
+            high = high_ref[first : first + 8, columns]
+            start = [part_ref[f, first : first + 8, columns] for f in range(FEATS)]
+            acc = take_rows(
+                lambda f, n: recv[n // rows - 1][f, n % rows : n % rows + 1, :], high, low, rows, table_rows - rows, start
+            )
             for f in range(FEATS):
-                source = jnp.broadcast_to(recv[n // rows][f, n % rows : n % rows + 1, :], (tiles, LANES))
-                acc[f] = jnp.where(here, lane_take(source, low), acc[f])
-        for f in range(FEATS):
-            pieces[f][c] = acc[f]
+                pieces[f][c].append(acc[f])
+    pieces = [[jnp.concatenate(p, axis=0) for p in both] for both in pieces]
     mean_x, mean_y, con_a, con_b, con_c, log_op, red, green, blue = [jnp.concatenate(p, axis=1) for p in pieces]
     mean_x = mean_x - centre_x
     mean_y = mean_y - centre_y
@@ -309,8 +413,8 @@
             inner = jnp.zeros((8, pixels), F32)
             for i in range(3):
                 image = jnp.sum(before * local[i], axis=0, keepdims=True)
-                images_ref[0, 0, 0, t, i : i + 1, :] = image
-                residual = image - target_ref[0, 0, 0, t, i : i + 1, :]
+                images_ref[0, 0, 0, i, pl.ds(t, 1), :] = image
+                residual = image - target_ref[0, 0, 0, i, pl.ds(t, 1), :]
                 first = residual.astype(BF16).astype(F32)
                 second = (residual - first).astype(BF16).astype(F32)
                 g_rows[u, 18 + i : 19 + i, :] = first
@@ -354,7 +458,10 @@
                     mom[h, pl.ds((8 + i) * tiles + ts[u], 1), :] = rows_out[3 * u + i][:, columns]
         return carry
 
-    lax.fori_loop(0, tiles // GROUP, group, 0)
+    if tiles == GROUP:
+        group(0, 0)
+    else:
+        lax.fori_loop(0, tiles // GROUP, group, 0)
 
     def got(i):
         return jnp.concatenate([mom[h, i * tiles : (i + 1) * tiles, :] for h in range(halves)], axis=1)
@@ -373,25 +480,29 @@
         -0.5 * svv,
         m0,
     ] + [got(8 + i) for i in range(3)]
-    value_rows = [[g[t : t + 1, :] for g in grads] for t in range(tiles)]
-    index_rows = [(slot_row[t : t + 1, :], slot_lane[t : t + 1, :]) for t in range(tiles)]
-    scatter_products(value_rows, index_rows, spread, hot, table_rows)
-    summed = dot(spread[...], hot[...], 1, 1)
+    parts = [exact_parts(g) for g in grads]
+    for t in range(tiles):
+        at = t * entries
+        values = [[x[t : t + 1, :] for x in pair] for pair in parts]
+        place_values(spread, at, mask_ref[:, at : at + entries], values)
+    summed = dot(spread[...], hot_ref[...], 1, 0)
+    wide = fold_of(rows)
+    height = rows // wide
+    total = table_rows // wide
     for f in range(FEATS):
-        both = (
-            summed[f * table_rows : (f + 1) * table_rows, :]
-            + summed[(FEATS + f) * table_rows : (FEATS + f + 1) * table_rows, :]
-        )
+        both = summed[f * total : (f + 1) * total, :] + summed[(FEATS + f) * total : (FEATS + f + 1) * total, :]
         for j in range(nd):
-            outs[j][f] = both[j * rows : (j + 1) * rows, :]
-
-
-def render(me, received, blocks, orders, counts, ids, target, nd, cap, rows):
-    tiles, entries = blocks.shape[3:]
+            for h in range(wide):
+                outs[j][f, h * height : (h + 1) * height, :] = both[
+                    j * height : (j + 1) * height, h * LANES : (h + 1) * LANES
+                ]
+
+
+def render(received, prepared, ids, target, nd, rows, tiles, entries):
     pixels = SIDE * SIDE
     return pl.pallas_call(
-        partial(render_kernel, nd=nd, cap=cap, rows=rows, tiles=tiles, entries=entries),
-        in_specs=[smem_spec()] + [vmem_spec()] * (nd + 5),
+        partial(render_kernel, nd=nd, rows=rows, tiles=tiles, entries=entries),
+        in_specs=[vmem_spec()] * (nd + 7),
         out_specs=[vmem_spec()] * (nd + 1),
         out_shape=[jax.ShapeDtypeStruct((FEATS, rows, LANES), F32)] * nd
         + [jax.ShapeDtypeStruct(target.shape, F32)],
@@ -406,37 +517,74 @@
             pltpu.VMEM((GROUP, entries, pixels), BF16),
             pltpu.VMEM((GROUP, 32, pixels), F32),
             pltpu.VMEM((entries // LANES, 11 * tiles, LANES), F32),
-            pltpu.VMEM((2 * FEATS * nd * rows, tiles * entries), BF16),
-            pltpu.VMEM((LANES, tiles * entries), BF16),
+            pltpu.VMEM((2 * FEATS * nd * rows // fold_of(rows), tiles * entries), BF16),
         ],
         compiler_params=pltpu.CompilerParams(vmem_limit_bytes=48 * 1024 * 1024),
         name="render_tiles",
-    )(me, *received, blocks, orders, counts, ids, target)
-
-
-def owner_kernel(me_ref, *refs, nd, rows, parts, nv, nc, out_rows):
-    recv = refs[:nd]
-    idx_ref, w_ref = refs[nd : nd + 2]
-    outs = refs[nd + 2 : nd + 2 + parts]
-    spread, hot, summed = refs[nd + 2 + parts :]
-    my_view = me_ref[1]
-    my_chip = me_ref[2]
-    value_rows = []
-    index_rows = []
-    for n in range(nd * rows):
-        value_rows.append([recv[n // rows][f, n % rows : n % rows + 1, :] for f in range(FEATS)])
-        index = idx_ref[n : n + 1, :]
-        index_rows.append((index >> 7, index & (LANES - 1)))
-    scatter_products(value_rows, index_rows, spread, hot, out_rows)
-    result = dot(spread[...], hot[...], 1, 1)
-    share = out_rows // parts
+    )(*received, *prepared, ids, target)
+
+
+def owner_index_kernel(own_ref, idx_ref, mask_out, hot_out, sum_out, spread, *, share):
+    rows = own_ref.shape[1]
+    index = idx_ref[...]
+    key_high, key_low = fold(index >> 7, index & (LANES - 1), share)
+    key_columns = key_low.astype(F32).T.astype(jnp.int32)
+    wide = fold_of(share)
+    for n in range(idx_ref.shape[0]):
+        place_mask(mask_out, n * LANES, key_high[n : n + 1, :])
+        place_hot(hot_out, n * LANES, key_columns[:, n : n + 1], wide)
+    parts = [exact_parts(own_ref[f]) for f in range(FEATS)]
+    for n in range(rows):
+        values = [[x[n : n + 1, :] for x in pair] for pair in parts]
+        place_values(spread, n * LANES, mask_out[:, n * LANES : (n + 1) * LANES], values)
+    sum_out[...] = dot(spread[...], hot_out[0 : rows * LANES, :], 1, 0)
+
+
+def owner_indices(own, index, share, width):
+    rows = own.shape[1]
+    wide = fold_of(share)
+    height = width // LANES // wide
+    slots = index.shape[0] * LANES
+    return pl.pallas_call(
+        partial(owner_index_kernel, share=share),
+        in_specs=[vmem_spec()] * 2,
+        out_specs=[vmem_spec()] * 3,
+        out_shape=[
+            jax.ShapeDtypeStruct((height, slots), BF16),
+            jax.ShapeDtypeStruct((slots, wide * LANES), BF16),
+            jax.ShapeDtypeStruct((2 * FEATS * height, wide * LANES), F32),
+        ],
+        scratch_shapes=[pltpu.VMEM((2 * FEATS * height, rows * LANES), BF16)],
+        compiler_params=pltpu.CompilerParams(vmem_limit_bytes=40 * 1024 * 1024),
+        name="prep_owner",
+    )(own, index)
+
+
+def owner_kernel(*refs, nd, rows, parts, nv, nc, share):
+    recv = refs[: nd - 1]
+    mask_ref, hot_ref, sum_ref, w_ref = refs[nd - 1 : nd + 3]
+    outs = refs[nd + 3 : nd + 3 + parts]
+    spread, summed = refs[nd + 3 + parts :]
+    my_view = lax.axis_index("view")
+    my_chip = lax.axis_index("chip")
+    skip = rows * LANES
+    for j in range(nd - 1):
+        pairs = [exact_parts(recv[j][f]) for f in range(FEATS)]
+        for i in range(rows):
+            at = (j * rows + i) * LANES
+            values = [[x[i : i + 1, :] for x in pair] for pair in pairs]
+            place_values(spread, at, mask_ref[:, skip + at : skip + at + LANES], values)
+    result = sum_ref[...] + dot(spread[...], hot_ref[skip:, :], 1, 0)
+    wide = fold_of(share)
+    height = share // wide
+    total = parts * height
     for f in range(FEATS):
-        both = (
-            result[f * out_rows : (f + 1) * out_rows, :]
-            + result[(FEATS + f) * out_rows : (FEATS + f + 1) * out_rows, :]
-        )
+        both = result[f * total : (f + 1) * total, :] + result[(FEATS + f) * total : (FEATS + f + 1) * total, :]
         for p in range(parts):
-            summed[p, f] = both[p * share : (p + 1) * share, :]
+            for h in range(wide):
+                summed[p, f, h * height : (h + 1) * height, :] = both[
+                    p * height : (p + 1) * height, h * LANES : (h + 1) * LANES
+                ]
     for p in range(parts):
         summed[p, FEATS] = w_ref[0:share, :]
     for dv in range(nv):
@@ -445,26 +593,24 @@
             outs[dv * nc + dc][...] = summed[where]
 
 
-def owner_sums(me, received, index, weights, nd, rows, nv, nc, width):
+def owner_sums(received, prepared, weights, nd, rows, nv, nc, share):
     parts = nv * nc
-    out_rows = width // LANES
-    share = out_rows // parts
+    height, slots = prepared[0].shape
     return pl.pallas_call(
-        partial(owner_kernel, nd=nd, rows=rows, parts=parts, nv=nv, nc=nc, out_rows=out_rows),
-        in_specs=[smem_spec()] + [vmem_spec()] * (nd + 2),
+        partial(owner_kernel, nd=nd, rows=rows, parts=parts, nv=nv, nc=nc, share=share),
+        in_specs=[vmem_spec()] * (nd + 3),
         out_specs=[vmem_spec()] * parts,
         out_shape=[jax.ShapeDtypeStruct((FEATS + 1, share, LANES), F32)] * parts,
         scratch_shapes=[
-            pltpu.VMEM((2 * FEATS * out_rows, nd * rows * LANES), BF16),
-            pltpu.VMEM((LANES, nd * rows * LANES), BF16),
+            pltpu.VMEM((2 * FEATS * height, slots - rows * LANES), BF16),
             pltpu.VMEM((parts, FEATS + 1, share, LANES), F32),
         ],
-        compiler_params=pltpu.CompilerParams(vmem_limit_bytes=48 * 1024 * 1024),
+        compiler_params=pltpu.CompilerParams(vmem_limit_bytes=40 * 1024 * 1024),
         name="owner_sums",
-    )(me, *received, index, weights)
-
-
-def pullback_kernel(at_ref, params_ref, *refs, nv, nc, coefs):
+    )(*received, *prepared, weights)
+
+
+def pullback_kernel(params_ref, *refs, nv, nc, coefs):
     recv = refs[: nv * nc]
     out_ref, flat = refs[nv * nc :]
     share = recv[0].shape[1]
@@ -524,24 +670,20 @@
         out_ref[10 + c * coefs : 10 + (c + 1) * coefs, :] = harmonics[c]
 
 
-def pull_back(at, params, received, nv, nc, coefs):
-    parts = nv * nc
-    columns = params.shape[1] // parts
-    block = received[0].shape
+def pull_back(params, received, nv, nc, coefs):
     return pl.pallas_call(
         partial(pullback_kernel, nv=nv, nc=nc, coefs=coefs),
-        grid_spec=pltpu.PrefetchScalarGridSpec(
-            num_scalar_prefetch=1,
-            grid=(1,),
-            in_specs=[pl.BlockSpec((params.shape[0], columns), lambda i, at_ref: (0, at_ref[0]))]
-            + [pl.BlockSpec(block, lambda i, at_ref: (0, 0, 0))] * parts,
-            out_specs=pl.BlockSpec((params.shape[0], columns), lambda i, at_ref: (0, 0)),
-            scratch_shapes=[pltpu.VMEM((16, columns), F32)],
-        ),
-        out_shape=jax.ShapeDtypeStruct((params.shape[0], columns), F32),
+        in_specs=[vmem_spec()] * (1 + nv * nc),
+        out_specs=vmem_spec(),
+        out_shape=jax.ShapeDtypeStruct(params.shape, F32),
+        scratch_shapes=[pltpu.VMEM((16, params.shape[1]), F32)],
         compiler_params=pltpu.CompilerParams(vmem_limit_bytes=40 * 1024 * 1024),
         name="pull_back",
-    )(at, params, *received)
+    )(params, *received)
+
+
+def hop_order(nd, first):
+    return [j for j in first if j < nd] + [j for j in range(1, nd) if j not in first]
 
 
 def local(
@@ -561,22 +703,22 @@
 ):
     cap = requests.shape[4]
     rows = -(-cap // LANES)
-    my_view = lax.axis_index("view")
-    my_chip = lax.axis_index("chip")
-    me = jnp.stack([lax.axis_index("dev"), my_view, my_chip]).astype(jnp.int32)
-    at = (my_view * nc + my_chip).astype(jnp.int32).reshape(1)
-
-    *packets, index, weights = send(me, cameras, view_basis, params, requests, nd, cap, rows)
-    received = [packets[0]]
-    for j in range(1, nd):
-        received.append(lax.ppermute(packets[j], "dev", [(i, (i + j) % nd) for i in range(nd)]))
-    *returns, images = render(
-        me, received, margin_blocks, depth_orders, tile_counts, tile_lists, target, nd, cap, rows
-    )
-    back = [returns[0]]
-    for j in range(1, nd):
-        back.append(lax.ppermute(returns[j], "dev", [((i + j) % nd, i) for i in range(nd)]))
-    shares = owner_sums(me, back, index, weights, nd, rows, nv, nc, params.shape[1])
+    later = (margin_blocks, depth_orders, tile_counts, tile_lists, jnp.swapaxes(target, 3, 4))
+    outs = send(cameras, view_basis, params, requests, later, nd, nv, nc, cap, rows)
+    packets = outs[:nd]
+    index, weights, owned, blocks, orders, counts, ids, swapped = outs[nd:]
+    received = list(packets)
+    for j in hop_order(nd, FORTH):
+        received[j] = lax.ppermute(packets[j], "dev", [(i, i ^ j) for i in range(nd)])
+    prepared = tile_indices(packets[0], blocks, orders, counts, nd, cap)
+    tiles, entries = margin_blocks.shape[3:]
+    *returns, images = render(received[1:], prepared, ids, swapped, nd, rows, tiles, entries)
+    back = list(returns)
+    for j in hop_order(nd, BACK):
+        back[j] = lax.ppermute(returns[j], "dev", [(i, i ^ j) for i in range(nd)])
+    share = params.shape[1] // LANES // (nv * nc)
+    sorted_own = owner_indices(returns[0], index, share, params.shape[1])
+    shares = owner_sums(back[1:], sorted_own, weights, nd, rows, nv, nc, share)
     arrived = []
     for dv in range(nv):
         for dc in range(nc):
@@ -585,8 +727,8 @@
             ]
             piece = shares[dv * nc + dc]
             arrived.append(piece if dv + dc == 0 else lax.ppermute(piece, ("view", "chip"), pairs))
-    grads = pull_back(at, params, arrived, nv, nc, view_basis.shape[1])
-    return (grads, images)
+    grads = pull_back(owned, arrived, nv, nc, view_basis.shape[1])
+    return (grads, jnp.swapaxes(images, 3, 4))
 
 
 def solution(mesh):

time: 41.9 us -> 41 us (0.979)
  waiting for transfers between devices: 9.44 us -> 8.07 us
  local copies, waits for them, and re-layouts: 3.33 us -> 4.22 us
  starting transfers between devices: 12.8 us -> 12 us
    pallas_call x3 -> x5, Pallas kernels: 12.5 us -> 14.9 us  [the longest x1 7.7 us: render(): pl.pallas_call(partial(render_kernel, nd=nd, rows=rows, tiles=tiles, entr...]
    pallas_call x1, Pallas kernels: 2.79 us -> 0.69 us  [owner_sums(): pl.pallas_call(partial(owner_kernel, nd=nd, rows=rows, parts=parts, nv=nv...]
    ppermute x6, waiting for transfers between devices: 6.86 us -> 4.84 us  [the longest x3 2.87 us: local(): back[j] = lax.ppermute(returns[j], 'dev', [(i, i ^ j) for i in range(nd)])]
    unnamed x20 -> x18, local copies, waits for them, and re-layouts: 3.33 us -> 4.22 us
    ppermute x6, starting transfers between devices: 10.9 us -> 10.1 us  [the longest x3 5.68 us: local(): lax.ppermute(packets[j], 'dev', [(i, i ^ j) for i in range(nd)])]
    ppermute x3, waiting for transfers between devices: 2.58 us -> 3.23 us  [local(): lax.ppermute(piece, ('view', 'chip'), pairs)]
  transfers between devices with their start and end apart: 9 -> 9, of which waited for: 7 -> 4; matrix products, arithmetic and copies ran while one was open for 4% -> 0% of each run, Pallas kernels for 0% -> 5%
where the time goes in v3:
time: 41 us; the launch traced here: 40.6 us
  Pallas kernels  15.6 us (38%)
  starting transfers between devices  12 us (29%)
  waiting for transfers between devices  8.07 us (20%)
  local copies, waits for them, and re-layouts  4.22 us (10%)
  between operations  0.72 us (2%)
    pallas_call x1, Pallas kernels, render(): pl.pallas_call(partial(render_kernel, nd=nd, rows=rows, tiles=tiles, entr...  7.7 us
    ppermute x3, starting transfers between devices, local(): lax.ppermute(packets[j], 'dev', [(i, i ^ j) for i in range(nd)])  5.68 us
    ppermute x3, starting transfers between devices, local(): back[j] = lax.ppermute(returns[j], 'dev', [(i, i ^ j) for i in range(nd)])  4.39 us
    unnamed x18, local copies, waits for them, and re-layouts  4.22 us
    pallas_call x1, Pallas kernels, send(): pl.pallas_call(partial(send_kernel, later=len(later), nd=nd, nc=nc, cap=c...  3.95 us
    ppermute x3, waiting for transfers between devices, local(): lax.ppermute(piece, ('view', 'chip'), pairs)  3.23 us
    ppermute x3, waiting for transfers between devices, local(): back[j] = lax.ppermute(returns[j], 'dev', [(i, i ^ j) for i in range(nd)])  2.87 us
    ppermute x3, waiting for transfers between devices, local(): lax.ppermute(packets[j], 'dev', [(i, i ^ j) for i in range(nd)])  1.96 us
  transfers between devices with their start and end apart: 9, of which 4 were waited for; matrix products, arithmetic and copies ran while one was open for 0% of the time, Pallas kernels for 5%

profile of v3, /device:TPU:0, one launch (start us, length us, event | category | flops | bytes accessed | tf_op | source)
XLA Modules:
  0.0 40.6 jit_solution(5084616098328147631)
XLA Ops:
  0.6 3.9 %project_gather.1 = (f32[9,8,128]{2,1,0:T(8,128)}, f32[9,8,128]{2,1,0:T(8,128)}, f32[9,8,128]{2,1,0:T(8,128)}, f32[9,8,128]{2,1,0:T(8,128)}, s32[32,128]{1,0:T(8...) custom-call(f32[1,2,4]{2,1,0:T(2,128)} %cam_hbm.1, ...), custom_call_target="tpu_custom_call" | custom-call | tf_op jit(solution)/shard_map/project_gather/pallas_call | solution.py:162
  4.6 0.0 copy-start.6
  4.6 3.1 %collective-permute-start = (f32[9,8,128]{2,1,0:T(8,128)}, f32[9,8,128]{2,1,0:T(8,128)S(1)}, u32[]{:S(2)}, u32[]{:S(2)}) collective-permute-start(f32[9,8,128]{2,1,0:T(8,128)} %get-tuple-element.33), channel_id=1, source_target_pairs={{0,4},{4,0},{8,12},{12,8},{1,5},{5,1},{9,13},{13,9},{2,6},{6,2},{1... | collective-permute-start | bytes 110600 | tf_op jit(solution)/shard_map/ppermute | solution.py:712
  7.7 2.6 %collective-permute-start.1 = (f32[9,8,128]{2,1,0:T(8,128)}, f32[9,8,128]{2,1,0:T(8,128)S(1)}, u32[]{:S(2)}, u32[]{:S(2)}) collective-permute-start(f32[9,8,128]{2,1,0:T(8,128)} %get-tuple-element.34), channel_id=1, source_target_pairs={{0,8},{4,12},{8,0},{12,4},{1,9},{5,13},{9,1},{13,5},{2,10},{6,14},... | collective-permute-start | bytes 110600 | tf_op jit(solution)/shard_map/ppermute | solution.py:712
  10.3 0.0 collective-permute-start.2
  10.3 0.0 copy-start.2
  10.3 0.8 %copy-done.2 = f32[9,8,128]{2,1,0:T(8,128)S(1)} copy-done((f32[9,8,128]{2,1,0:T(8,128)S(1)}, f32[9,8,128]{2,1,0:T(8,128)}, u32[]{:S(2)}) %copy-start.2) | copy-done | bytes 36888
  11.0 0.0 copy-start.3
  11.1 0.7 %copy-done.3 = s32[1,1,1,16,256]{4,3,2,1,0:T(8,128)S(1)} copy-done((s32[1,1,1,16,256]{4,3,2,1,0:T(8,128)S(1)}, s32[1,1,1,16,256]{4,3,2,1,0:T(8,128)}, u32[]{:S(2)}) %copy-start.3) | copy-done | bytes 16408
  11.8 0.0 copy-start.4
  11.8 0.7 %copy-done.4 = s32[1,1,1,16,256]{4,3,2,1,0:T(8,128)S(1)} copy-done((s32[1,1,1,16,256]{4,3,2,1,0:T(8,128)S(1)}, s32[1,1,1,16,256]{4,3,2,1,0:T(8,128)}, u32[]{:S(2)}) %copy-start.4) | copy-done | bytes 16408
  12.5 0.0 copy-start.7
  12.5 0.6 %copy-done.7 = s32[1,1,1,16]{3,2,1,0:T(1,128)S(1)} copy-done((s32[1,1,1,16]{3,2,1,0:T(1,128)S(1)}, s32[1,1,1,16]{3,2,1,0:T(1,128)}, u32[]{:S(2)}) %copy-start.7) | copy-done | bytes 88
  13.1 0.0 copy-start.5
  13.1 1.2 %prep_tiles.1 = (s32[16,256]{1,0:T(8,128)S(1)}, s32[16,256]{1,0:T(8,128)S(1)}, f32[16,256]{1,0:T(8,128)S(1)}, f32[9,16,256]{2,1,0:T(8,128)S(1)}, bf16[16,4096]{1...) custom-call(f32[9,8,128]{2,1,0:T(8,128)S(1)} %copy-done.2, s32[1,1,1,16,256]{4,3,2,1,0:T(8,128)S(1)} %copy-done.3, ...), custom_call_target="tpu_custom_call" | custom-call | tf_op jit(solution)/shard_map/prep_tiles/pallas_call | solution.py:278
  14.3 0.0 collective-permute-done.refs_0_
  14.3 0.0 collective-permute-done.1.refs_1_
  14.3 2.0 %collective-permute-done.2.refs_2_ = f32[9,8,128]{2,1,0:T(8,128)S(1)} collective-permute-done((f32[9,8,128]{2,1,0:T(8,128)}, f32[9,8,128]{2,1,0:T(8,128)S(1)}, u32[]{:S(2)}, u32[]{:S(2)}) %collective-permute-start.2) | collective-permute-done | bytes 36896 | tf_op jit(solution)/shard_map/ppermute | solution.py:712
  16.2 0.0 copy-start.1
  16.2 0.8 %copy-done.1 = f32[1,1,1,3,16,256]{5,4,3,2,1,0:T(8,128)S(1)} copy-done((f32[1,1,1,3,16,256]{5,4,3,2,1,0:T(8,128)S(1)}, f32[1,1,1,3,16,256]{5,4,3,2,1,0:T(8,128)}, u32[]{:S(2)}) %copy-start.1) | copy-done | bytes 49176
  17.0 0.0 copy-start.8
  17.0 0.6 %copy-done.8 = s32[1,1,1,16]{3,2,1,0:T(1,128)S(1)} copy-done((s32[1,1,1,16]{3,2,1,0:T(1,128)S(1)}, s32[1,1,1,16]{3,2,1,0:T(1,128)}, u32[]{:S(2)}) %copy-start.8) | copy-done | bytes 88
  17.7 0.0 copy-start
  17.7 7.7 %render_tiles.1 = (f32[9,8,128]{2,1,0:T(8,128)S(1)}, f32[9,8,128]{2,1,0:T(8,128)S(1)}, f32[9,8,128]{2,1,0:T(8,128)S(1)}, f32[9,8,128]{2,1,0:T(8,128)S(1)}, f32[1,1,1,3,16,256]{5,4,3,2,1,0:T(8,128)}) custom-call(f32[9,8,128]{2,1,0:T(8,128)S(1)} %collective-permute-done.refs_0_, f32[9,8,128]{2,1,0:T(8,128)S(1)} %collective-permute-done.1.refs_1_, ...), custom_call_target="tpu_custom_call" | custom-call | tf_op jit(solution)/shard_map/render_tiles/pallas_call | solution.py:503
  25.4 0.0 collective-permute-start.3
  25.4 2.4 %collective-permute-start.4 = (f32[9,8,128]{2,1,0:T(8,128)S(1)}, f32[9,8,128]{2,1,0:T(8,128)S(1)}, u32[]{:S(2)}, u32[]{:S(2)}) collective-permute-start(f32[9,8,128]{2,1,0:T(8,128)S(1)} %get-tuple-element.49), channel_id=1, source_target_pairs={{0,8},{4,12},{8,0},{12,4},{1,9},{5,13},{9,1},{13,5},{2,10},{6,14},... | collective-permute-start | bytes 110600 | tf_op jit(solution)/shard_map/ppermute | solution.py:718
  27.8 1.9 %collective-permute-start.5 = (f32[9,8,128]{2,1,0:T(8,128)S(1)}, f32[9,8,128]{2,1,0:T(8,128)S(1)}, u32[]{:S(2)}, u32[]{:S(2)}) collective-permute-start(f32[9,8,128]{2,1,0:T(8,128)S(1)} %get-tuple-element.50), channel_id=1, source_target_pairs={{0,12},{4,8},{8,4},{12,0},{1,13},{5,9},{9,5},{13,1},{2,14},{6,10},... | collective-permute-start | bytes 110600 | tf_op jit(solution)/shard_map/ppermute | solution.py:718
  29.8 0.0 copy-done.5
  29.8 0.9 %prep_owner.1 = (bf16[16,4096]{1,0:T(8,128)(2,1)S(1)}, bf16[4096,256]{1,0:T(8,128)(2,1)S(1)}, f32[288,256]{1,0:T(8,128)S(1)}) custom-call(f32[9,8,128]{2,1,0:T(8,128)S(1)} %get-tuple-element.51.own_ref, s32[32,128]{1,0:T(8,128)S(1)} %copy-done.5), custom_call_target="tpu_custom_call" | custom-call | tf_op jit(solution)/shard_map/prep_owner/pallas_call | solution.py:548
  30.7 0.0 collective-permute-done.3.refs_0_
  30.7 0.0 collective-permute-done.4.refs_1_
  30.7 2.9 %collective-permute-done.5.refs_2_ = f32[9,8,128]{2,1,0:T(8,128)S(1)} collective-permute-done((f32[9,8,128]{2,1,0:T(8,128)S(1)}, f32[9,8,128]{2,1,0:T(8,128)S(1)}, u32[]{:S(2)}, u32[]{:S(2)}) %collective-permute-start.5) | collective-permute-done | bytes 36896 | tf_op jit(solution)/shard_map/ppermute | solution.py:718
  33.6 0.0 copy-done.6
  33.6 0.7 %owner_sums.1 = (f32[10,8,128]{2,1,0:T(8,128)S(1)}, f32[10,8,128]{2,1,0:T(8,128)S(1)}, f32[10,8,128]{2,1,0:T(8,128)S(1)}, f32[10,8,128]{2,1,0:T(8,128)S(1)}) custom-call(f32[9,8,128]{2,1,0:T(8,128)S(1)} %collective-permute-done.3.refs_0_, f32[9,8,128]{2,1,0:T(8,128)S(1)} %collective-permute-done.4.refs_1_, f32[9,8,128]{2,1,0:T(8,128)S(1)} %collective-permute-done.5.refs_2_, ...), custom_call_target="tpu_custom_call" | custom-call | tf_op jit(solution)/shard_map/owner_sums/pallas_call | solution.py:599
  34.3 0.1 collective-permute-start.6
  34.3 1.6 %collective-permute-start.7 = (f32[10,8,128]{2,1,0:T(8,128)S(1)}, f32[10,8,128]{2,1,0:T(8,128)S(1)}, u32[]{:S(2)}, u32[]{:S(2)}) collective-permute-start(f32[10,8,128]{2,1,0:T(8,128)S(1)} %get-tuple-element.59), channel_id=1, source_target_pairs={{0,2},{1,3},{2,0},{3,1},{4,6},{5,7},{6,4},{7,5},{8,10},{9,11},{10,... | collective-permute-start | bytes 122888 | tf_op jit(solution)/shard_map/ppermute | solution.py:729
  35.9 0.3 collective-permute-start.8
  36.2 0.0 collective-permute-done.6.refs_1_
  36.2 2.2 %collective-permute-done.7.refs_2_ = f32[10,8,128]{2,1,0:T(8,128)S(1)} collective-permute-done((f32[10,8,128]{2,1,0:T(8,128)S(1)}, f32[10,8,128]{2,1,0:T(8,128)S(1)}, u32[]{:S(2)}, u32[]{:S(2)}) %collective-permute-start.7) | collective-permute-done | bytes 40992 | tf_op jit(solution)/shard_map/ppermute | solution.py:729
  38.4 1.0 %collective-permute-done.8.refs_3_ = f32[10,8,128]{2,1,0:T(8,128)S(1)} collective-permute-done((f32[10,8,128]{2,1,0:T(8,128)S(1)}, f32[10,8,128]{2,1,0:T(8,128)S(1)}, u32[]{:S(2)}, u32[]{:S(2)}) %collective-permute-start.8) | collective-permute-done | bytes 40992 | tf_op jit(solution)/shard_map/ppermute | solution.py:729
  39.4 0.0 copy-done
  39.4 1.2 %pull_back.1 = f32[58,1024]{1,0:T(8,128)} custom-call(f32[58,1024]{1,0:T(8,128)S(1)} %copy-done, f32[10,8,128]{2,1,0:T(8,128)S(1)} %get-tuple-element.57.refs_0_, f32[10,8,128]{2,1,0:T(8,128)S(1)} %collective-permute-done.6.refs_1_, f32[10,8,128]{2,1,0:T(8,128)S(1)} %collective-permute-done.7.refs_2_, f32[10,8,128]{2,1,0:T(8,128)S(1)} %collective-permute-done.8.refs_3_), custom_call_target="tpu_custom_call" | custom-call | tf_op jit(solution)/shard_map/pull_back/pallas_call | solution.py:674
Async XLA Ops:
  4.6 29.0 %copy-start.6 = (f32[8,128]{1,0:T(8,128)S(1)}, f32[8,128]{1,0:T(8,128)}, u32[]{:S(2)}) copy-start(f32[8,128]{1,0:T(8,128)} %get-tuple-element.56.refs_6_) | copy-start | bytes 12292
  4.6 9.7 %collective-permute-start = (f32[9,8,128]{2,1,0:T(8,128)}, f32[9,8,128]{2,1,0:T(8,128)S(1)}, u32[]{:S(2)}, u32[]{:S(2)}) collective-permute-start(f32[9,8,128]{2,1,0:T(8,128)} %get-tuple-element.33), channel_id=1, source_target_pairs={{0,4},{4,0},{8,12},{12,8},{1,5},{5,1},{9,13},{13,9},{2,6},{6,2},{1... | collective-permute-start | bytes 110600 | tf_op jit(solution)/shard_map/ppermute | solution.py:712
  7.7 6.6 %collective-permute-start.1 = (f32[9,8,128]{2,1,0:T(8,128)}, f32[9,8,128]{2,1,0:T(8,128)S(1)}, u32[]{:S(2)}, u32[]{:S(2)}) collective-permute-start(f32[9,8,128]{2,1,0:T(8,128)} %get-tuple-element.34), channel_id=1, source_target_pairs={{0,8},{4,12},{8,0},{12,4},{1,9},{5,13},{9,1},{13,5},{2,10},{6,14},... | collective-permute-start | bytes 110600 | tf_op jit(solution)/shard_map/ppermute | solution.py:712
  10.3 6.0 %collective-permute-start.2 = (f32[9,8,128]{2,1,0:T(8,128)}, f32[9,8,128]{2,1,0:T(8,128)S(1)}, u32[]{:S(2)}, u32[]{:S(2)}) collective-permute-start(f32[9,8,128]{2,1,0:T(8,128)} %get-tuple-element.35), channel_id=1, source_target_pairs={{0,12},{4,8},{8,4},{12,0},{1,13},{5,9},{9,5},{13,1},{2,14},{6,10},... | collective-permute-start | bytes 110600 | tf_op jit(solution)/shard_map/ppermute | solution.py:712
  10.3 0.8 %copy-start.2 = (f32[9,8,128]{2,1,0:T(8,128)S(1)}, f32[9,8,128]{2,1,0:T(8,128)}, u32[]{:S(2)}) copy-start(f32[9,8,128]{2,1,0:T(8,128)} %get-tuple-element.36.own_ref) | copy-start | bytes 110596
  11.0 0.7 %copy-start.3 = (s32[1,1,1,16,256]{4,3,2,1,0:T(8,128)S(1)}, s32[1,1,1,16,256]{4,3,2,1,0:T(8,128)}, u32[]{:S(2)}) copy-start(s32[1,1,1,16,256]{4,3,2,1,0:T(8,128)} %get-tuple-element.37.blocks_ref) | copy-start | bytes 49156
  11.8 0.7 %copy-start.4 = (s32[1,1,1,16,256]{4,3,2,1,0:T(8,128)S(1)}, s32[1,1,1,16,256]{4,3,2,1,0:T(8,128)}, u32[]{:S(2)}) copy-start(s32[1,1,1,16,256]{4,3,2,1,0:T(8,128)} %get-tuple-element.38.orders_ref) | copy-start | bytes 49156
  12.5 0.6 %copy-start.7 = (s32[1,1,1,16]{3,2,1,0:T(1,128)S(1)}, s32[1,1,1,16]{3,2,1,0:T(1,128)}, u32[]{:S(2)}) copy-start(s32[1,1,1,16]{3,2,1,0:T(1,128)} %get-tuple-element.39.counts_ref) | copy-start | bytes 196
  13.1 16.7 %copy-start.5 = (s32[32,128]{1,0:T(8,128)S(1)}, s32[32,128]{1,0:T(8,128)}, u32[]{:S(2)}) copy-start(s32[32,128]{1,0:T(8,128)} %get-tuple-element.52.idx_ref) | copy-start | bytes 49156
  16.2 0.8 %copy-start.1 = (f32[1,1,1,3,16,256]{5,4,3,2,1,0:T(8,128)S(1)}, f32[1,1,1,3,16,256]{5,4,3,2,1,0:T(8,128)}, u32[]{:S(2)}) copy-start(f32[1,1,1,3,16,256]{5,4,3,2,1,0:T(8,128)} %get-tuple-element.47.refs_10_) | copy-start | bytes 147460
  17.0 0.6 %copy-start.8 = (s32[1,1,1,16]{3,2,1,0:T(1,128)S(1)}, s32[1,1,1,16]{3,2,1,0:T(1,128)}, u32[]{:S(2)}) copy-start(s32[1,1,1,16]{3,2,1,0:T(1,128)} %get-tuple-element.46.refs_9_) | copy-start | bytes 196
  17.7 21.8 %copy-start = (f32[58,1024]{1,0:T(8,128)S(1)}, f32[58,1024]{1,0:T(8,128)}, u32[]{:S(2)}) copy-start(f32[58,1024]{1,0:T(8,128)} %get-tuple-element.32.params_ref) | copy-start | bytes 712708
  25.4 5.3 %collective-permute-start.3 = (f32[9,8,128]{2,1,0:T(8,128)S(1)}, f32[9,8,128]{2,1,0:T(8,128)S(1)}, u32[]{:S(2)}, u32[]{:S(2)}) collective-permute-start(f32[9,8,128]{2,1,0:T(8,128)S(1)} %get-tuple-element.48), channel_id=1, source_target_pairs={{0,4},{4,0},{8,12},{12,8},{1,5},{5,1},{9,13},{13,9},{2,6},{6,2},{1... | collective-permute-start | bytes 110600 | tf_op jit(solution)/shard_map/ppermute | solution.py:718
  25.4 5.3 %collective-permute-start.4 = (f32[9,8,128]{2,1,0:T(8,128)S(1)}, f32[9,8,128]{2,1,0:T(8,128)S(1)}, u32[]{:S(2)}, u32[]{:S(2)}) collective-permute-start(f32[9,8,128]{2,1,0:T(8,128)S(1)} %get-tuple-element.49), channel_id=1, source_target_pairs={{0,8},{4,12},{8,0},{12,4},{1,9},{5,13},{9,1},{13,5},{2,10},{6,14},... | collective-permute-start | bytes 110600 | tf_op jit(solution)/shard_map/ppermute | solution.py:718
  27.8 5.8 %collective-permute-start.5 = (f32[9,8,128]{2,1,0:T(8,128)S(1)}, f32[9,8,128]{2,1,0:T(8,128)S(1)}, u32[]{:S(2)}, u32[]{:S(2)}) collective-permute-start(f32[9,8,128]{2,1,0:T(8,128)S(1)} %get-tuple-element.50), channel_id=1, source_target_pairs={{0,12},{4,8},{8,4},{12,0},{1,13},{5,9},{9,5},{13,1},{2,14},{6,10},... | collective-permute-start | bytes 110600 | tf_op jit(solution)/shard_map/ppermute | solution.py:718
  34.3 1.9 %collective-permute-start.6 = (f32[10,8,128]{2,1,0:T(8,128)S(1)}, f32[10,8,128]{2,1,0:T(8,128)S(1)}, u32[]{:S(2)}, u32[]{:S(2)}) collective-permute-start(f32[10,8,128]{2,1,0:T(8,128)S(1)} %get-tuple-element.58), channel_id=1, source_target_pairs={{0,1},{1,0},{2,3},{3,2},{4,5},{5,4},{6,7},{7,6},{8,9},{9,8},{10,11... | collective-permute-start | bytes 122888 | tf_op jit(solution)/shard_map/ppermute | solution.py:729
  34.3 4.1 %collective-permute-start.7 = (f32[10,8,128]{2,1,0:T(8,128)S(1)}, f32[10,8,128]{2,1,0:T(8,128)S(1)}, u32[]{:S(2)}, u32[]{:S(2)}) collective-permute-start(f32[10,8,128]{2,1,0:T(8,128)S(1)} %get-tuple-element.59), channel_id=1, source_target_pairs={{0,2},{1,3},{2,0},{3,1},{4,6},{5,7},{6,4},{7,5},{8,10},{9,11},{10,... | collective-permute-start | bytes 122888 | tf_op jit(solution)/shard_map/ppermute | solution.py:729
  35.9 3.5 %collective-permute-start.8 = (f32[10,8,128]{2,1,0:T(8,128)S(1)}, f32[10,8,128]{2,1,0:T(8,128)S(1)}, u32[]{:S(2)}, u32[]{:S(2)}) collective-permute-start(f32[10,8,128]{2,1,0:T(8,128)S(1)} %get-tuple-element.60), channel_id=1, source_target_pairs={{0,3},{1,2},{2,1},{3,0},{4,7},{5,6},{6,5},{7,4},{8,11},{9,10},{10,... | collective-permute-start | bytes 122888 | tf_op jit(solution)/shard_map/ppermute | solution.py:729

commit v4 on v3

--- a/solution.py
+++ b/solution.py
@@ -35,37 +35,12 @@
     return lax.dot_general(a, b, (((ca,), (cb,)), ((), ())), preferred_element_type=F32)
 
 
-def send_kernel(cam_hbm, basis_hbm, params_hbm, req_hbm, *refs, later, nd, nc, cap, rows):
-    later_hbm = refs[:later]
-    outs = refs[later : later + nd]
-    idx_out, w_out, own_out = refs[later + nd : later + nd + 3]
-    later_out = refs[later + nd + 3 : 2 * later + nd + 3]
-    feat, w_scr, cam_ref, basis_ref, params_ref, req_ref, sems = refs[2 * later + nd + 3 :]
-    me = lax.axis_index("dev")
-    share = own_out.shape[1]
-    owned = pl.multiple_of((lax.axis_index("view") * nc + lax.axis_index("chip")) * share, LANES)
-    copies = [
-        (params_hbm, params_ref),
-        (cam_hbm, cam_ref),
-        (basis_hbm, basis_ref),
-        (req_hbm, req_ref),
-        (params_hbm.at[:, pl.ds(owned, share)], own_out),
-    ] + list(zip(later_hbm, later_out))
-    copies = [pltpu.make_async_copy(source, target, sems.at[i]) for i, (source, target) in enumerate(copies)]
-    for copy in copies:
-        copy.start()
-    for copy in copies[1:4]:
-        copy.wait()
+def send_kernel(me_ref, cam_ref, basis_ref, params_ref, req_ref, *refs, nd, cap, rows):
+    outs = refs[:nd]
+    idx_out, w_out, feat, w_scr = refs[nd:]
+    me = me_ref[0]
     width = params_ref.shape[1]
     coefs = basis_ref.shape[-1]
-    idx_out[...] = jnp.zeros_like(idx_out)
-    for j in range(nd):
-        dest = me ^ j
-        for i in range(rows):
-            size = min(LANES, cap - i * LANES)
-            idx_out[j * rows + i : j * rows + i + 1, 0:size] = req_ref[
-                0, dest, 0, 0:1, i * LANES : i * LANES + size
-            ]
     w_scr[...] = jnp.zeros_like(w_scr)
     w_scr[0:2, 0:4] = cam_ref[0]
     w_scr[2:3, 0:coefs] = basis_ref[...]
@@ -81,7 +56,6 @@
     weights = weights + jnp.where(row8 == 3, pltpu.roll(basis_row, 10 + coefs, 1), 0.0)
     weights = weights + jnp.where(row8 == 4, pltpu.roll(basis_row, 10 + 2 * coefs, 1), 0.0)
     w_scr[...] = weights
-    copies[0].wait()
     linear = lax.dot_general(
         w_scr[:, 0 : params_ref.shape[0]],
         params_ref[...],
@@ -116,6 +90,14 @@
     for c in range(3):
         feat[6 + c : 7 + c, :] = linear[2 + c : 3 + c, :] + 0.5
 
+    idx_out[...] = jnp.zeros_like(idx_out)
+    for j in range(nd):
+        dest = me ^ j
+        for i in range(rows):
+            size = min(LANES, cap - i * LANES)
+            idx_out[j * rows + i : j * rows + i + 1, 0:size] = req_ref[
+                0, dest, 0, 0:1, i * LANES : i * LANES + size
+            ]
     total = nd * rows
     step = 8 if total % 8 == 0 else total
     source_rows = width // LANES
@@ -137,8 +119,6 @@
                         outs[j][f, i : i + step, :] = acc[f]
                 else:
                     outs[j][f, i : i + 1, :] = acc[f][n : n + 1, :]
-    for copy in copies[4:]:
-        copy.wait()
 
 
 def vmem_spec():
@@ -149,27 +129,20 @@
     return pl.BlockSpec(memory_space=pltpu.SMEM)
 
 
-def send(cameras, basis, params, requests, later, nd, nv, nc, cap, rows):
-    count, width = params.shape
-    first = (cameras, basis, params, requests)
-    out_shape = [jax.ShapeDtypeStruct((FEATS, rows, LANES), F32)] * nd
-    out_shape += [
-        jax.ShapeDtypeStruct((nd * rows, LANES), jnp.int32),
-        jax.ShapeDtypeStruct((8, LANES), F32),
-        jax.ShapeDtypeStruct((count, width // (nv * nc)), F32),
-    ]
-    out_shape += [jax.ShapeDtypeStruct(x.shape, x.dtype) for x in later]
+def send(me, cameras, basis, params, requests, nd, cap, rows):
     return pl.pallas_call(
-        partial(send_kernel, later=len(later), nd=nd, nc=nc, cap=cap, rows=rows),
-        in_specs=[pl.BlockSpec(memory_space=pl.ANY)] * (4 + len(later)),
-        out_specs=[vmem_spec()] * len(out_shape),
-        out_shape=out_shape,
-        scratch_shapes=[pltpu.VMEM((16, width), F32), pltpu.VMEM((8, LANES), F32)]
-        + [pltpu.VMEM(x.shape, x.dtype) for x in first]
-        + [pltpu.SemaphoreType.DMA((5 + len(later),))],
-        compiler_params=pltpu.CompilerParams(vmem_limit_bytes=60 * 1024 * 1024),
+        partial(send_kernel, nd=nd, cap=cap, rows=rows),
+        in_specs=[smem_spec()] + [vmem_spec()] * 4,
+        out_specs=[vmem_spec()] * (nd + 2),
+        out_shape=[jax.ShapeDtypeStruct((FEATS, rows, LANES), F32)] * nd
+        + [
+            jax.ShapeDtypeStruct((nd * rows, LANES), jnp.int32),
+            jax.ShapeDtypeStruct((8, LANES), F32),
+        ],
+        scratch_shapes=[pltpu.VMEM((16, params.shape[1]), F32), pltpu.VMEM((8, LANES), F32)],
+        compiler_params=pltpu.CompilerParams(vmem_limit_bytes=40 * 1024 * 1024),
         name="project_gather",
-    )(*first, *later)
+    )(me, cameras, basis, params, requests)
 
 
 def fold_of(block):
@@ -220,9 +193,9 @@
 
 
 def index_kernel(
-    own_ref, blocks_ref, orders_ref, counts_ref, high_out, low_out, live_out, part_out, mask_out, hot_out, *, nd, cap
+    me_ref, own_ref, blocks_ref, orders_ref, counts_ref, ids_ref, high_out, low_out, live_out, centre_out, part_out, *, nd, cap
 ):
-    me = lax.axis_index("dev")
+    me = me_ref[0]
     rows = own_ref.shape[1]
     tiles, entries = blocks_ref.shape[3:]
     chunk = entries // 8
@@ -253,6 +226,9 @@
     slot_lane = offset & (LANES - 1)
     high_out[...] = slot_row
     low_out[...] = slot_lane
+    tile_id = column_of(ids_ref, tiles)
+    centre_out[0] = jnp.broadcast_to(((tile_id % TW) * SIDE).astype(F32) + 0.5 * SIDE, (tiles, LANES))
+    centre_out[1] = jnp.broadcast_to(((tile_id // TW) * SIDE).astype(F32) + 0.5 * SIDE, (tiles, LANES))
     live_out[...] = jnp.where(rank < column_of(counts_ref, tiles), 1.0, 0.0)
     for c in range(halves):
         columns = slice(c * LANES, (c + 1) * LANES)
@@ -263,33 +239,60 @@
             acc = take_rows(lambda f, n: own_ref[f, n : n + 1, :], high, low, 0, rows, start)
             for f in range(FEATS):
                 part_out[f, first : first + 8, columns] = acc[f]
-    wide = fold_of(rows)
-    key_high, key_low = fold(slot_row, slot_lane, rows)
-    key_columns = key_low.astype(F32).T.astype(jnp.int32)
-    for t in range(tiles):
-        place_mask(mask_out, t * entries, key_high[t : t + 1, :])
-        place_hot(hot_out, t * entries, key_columns[:, t : t + 1], wide)
-
-
-def tile_indices(own, blocks, orders, counts, nd, cap):
+
+
+def tile_indices(me, own, blocks, orders, counts, ids, nd, cap):
     rows = own.shape[1]
     tiles, entries = blocks.shape[3:]
     wide = fold_of(rows)
     return pl.pallas_call(
         partial(index_kernel, nd=nd, cap=cap),
-        in_specs=[vmem_spec()] * 4,
-        out_specs=[vmem_spec()] * 6,
+        in_specs=[smem_spec()] + [vmem_spec()] * 5,
+        out_specs=[vmem_spec()] * 5,
         out_shape=[
             jax.ShapeDtypeStruct((tiles, entries), jnp.int32),
             jax.ShapeDtypeStruct((tiles, entries), jnp.int32),
             jax.ShapeDtypeStruct((tiles, entries), F32),
+            jax.ShapeDtypeStruct((2, tiles, LANES), F32),
             jax.ShapeDtypeStruct((FEATS, tiles, entries), F32),
-            jax.ShapeDtypeStruct((nd * rows // wide, tiles * entries), BF16),
-            jax.ShapeDtypeStruct((tiles * entries, wide * LANES), BF16),
         ],
         compiler_params=pltpu.CompilerParams(vmem_limit_bytes=40 * 1024 * 1024),
         name="prep_tiles",
-    )(own, blocks, orders, counts)
+    )(me, own, blocks, orders, counts, ids)
+
+
+def gather_kernel(*refs, first_block):
+    recv = refs[:-4]
+    high_ref, low_ref, part_ref, part_out = refs[-4:]
+    rows = recv[0].shape[1]
+    tiles, entries = high_ref.shape
+    first_row = first_block * rows
+    for c in range(entries // LANES):
+        columns = slice(c * LANES, (c + 1) * LANES)
+        for first in range(0, tiles, 8):
+            block = slice(first, first + 8)
+            start = [part_ref[f, block, columns] for f in range(FEATS)]
+
+            def source(f, n):
+                n = n - first_row
+                return recv[n // rows][f, n % rows : n % rows + 1, :]
+
+            acc = take_rows(
+                source, high_ref[block, columns], low_ref[block, columns], first_row, len(recv) * rows, start
+            )
+            for f in range(FEATS):
+                part_out[f, block, columns] = acc[f]
+
+
+def gather_more(received, first_block, high, low, part):
+    return pl.pallas_call(
+        partial(gather_kernel, first_block=first_block),
+        in_specs=[vmem_spec()] * (len(received) + 3),
+        out_specs=vmem_spec(),
+        out_shape=jax.ShapeDtypeStruct(part.shape, F32),
+        compiler_params=pltpu.CompilerParams(vmem_limit_bytes=40 * 1024 * 1024),
+        name="prep_gather",
+    )(*received, high, low, part)
 
 
 def column_of(ref, tiles):
@@ -299,10 +302,9 @@
 
 
 def render_kernel(*refs, nd, rows, tiles, entries):
-    recv = refs[: nd - 1]
-    high_ref, low_ref, live_ref, part_ref, mask_ref, hot_ref, ids_ref, target_ref = refs[nd - 1 : nd + 7]
-    outs = refs[nd + 7 : 2 * nd + 7]
-    (images_ref, coef, a_scr, t_scr, q_scr, whi_scr, wlo_scr, ghi_scr, glo_scr, g_rows, mom, spread) = refs[2 * nd + 7 :]
+    last_ref, high_ref, low_ref, live_ref, centre_ref, part_ref, target_ref = refs[:7]
+    outs = refs[7 : nd + 7]
+    (images_ref, coef, a_scr, t_scr, q_scr, whi_scr, wlo_scr, ghi_scr, glo_scr, g_rows, mom, spread, mask_ref, hot_ref) = refs[nd + 7 :]
     pixels = SIDE * SIDE
     halves = entries // LANES
     table_rows = nd * rows
@@ -311,9 +313,8 @@
         for h in range(halves):
             ref[h, at : at + value.shape[0], :] = value[:, h * LANES : (h + 1) * LANES]
 
-    tile_id = column_of(ids_ref, tiles)
-    centre_x = ((tile_id % TW) * SIDE).astype(F32) + 0.5 * SIDE
-    centre_y = ((tile_id // TW) * SIDE).astype(F32) + 0.5 * SIDE
+    centre_x = centre_ref[0, :, 0:1]
+    centre_y = centre_ref[1, :, 0:1]
     live = live_ref[...] > 0.5
 
     pieces = [[[] for _ in range(halves)] for _ in range(FEATS)]
@@ -324,7 +325,7 @@
             high = high_ref[first : first + 8, columns]
             start = [part_ref[f, first : first + 8, columns] for f in range(FEATS)]
             acc = take_rows(
-                lambda f, n: recv[n // rows - 1][f, n % rows : n % rows + 1, :], high, low, rows, table_rows - rows, start
+                lambda f, n: last_ref[f, n % rows : n % rows + 1, :], high, low, table_rows - rows, rows, start
             )
             for f in range(FEATS):
                 pieces[f][c].append(acc[f])
@@ -480,6 +481,11 @@
         -0.5 * svv,
         m0,
     ] + [got(8 + i) for i in range(3)]
+    key_high, key_low = fold(high_ref[...], low_ref[...], rows)
+    key_columns = key_low.astype(F32).T.astype(jnp.int32)
+    for t in range(tiles):
+        place_mask(mask_ref, t * entries, key_high[t : t + 1, :])
+        place_hot(hot_ref, t * entries, key_columns[:, t : t + 1], fold_of(rows))
     parts = [exact_parts(g) for g in grads]
     for t in range(tiles):
         at = t * entries
@@ -498,11 +504,11 @@
                 ]
 
 
-def render(received, prepared, ids, target, nd, rows, tiles, entries):
+def render(last, prepared, target, nd, rows, tiles, entries):
     pixels = SIDE * SIDE
     return pl.pallas_call(
         partial(render_kernel, nd=nd, rows=rows, tiles=tiles, entries=entries),
-        in_specs=[vmem_spec()] * (nd + 7),
+        in_specs=[vmem_spec()] * 7,
         out_specs=[vmem_spec()] * (nd + 1),
         out_shape=[jax.ShapeDtypeStruct((FEATS, rows, LANES), F32)] * nd
         + [jax.ShapeDtypeStruct(target.shape, F32)],
@@ -518,13 +524,16 @@
             pltpu.VMEM((GROUP, 32, pixels), F32),
             pltpu.VMEM((entries // LANES, 11 * tiles, LANES), F32),
             pltpu.VMEM((2 * FEATS * nd * rows // fold_of(rows), tiles * entries), BF16),
+            pltpu.VMEM((nd * rows // fold_of(rows), tiles * entries), BF16),
+            pltpu.VMEM((tiles * entries, fold_of(rows) * LANES), BF16),
         ],
         compiler_params=pltpu.CompilerParams(vmem_limit_bytes=48 * 1024 * 1024),
         name="render_tiles",
-    )(*received, *prepared, ids, target)
-
-
-def owner_index_kernel(own_ref, idx_ref, mask_out, hot_out, sum_out, spread, *, share):
+    )(last, *prepared, target)
+
+
+def owner_index_kernel(own_ref, next_ref, idx_ref, mask_out, hot_low, hot_high, sum_out, spread, *, share):
+    middle = idx_ref.shape[0] // 2
     rows = own_ref.shape[1]
     index = idx_ref[...]
     key_high, key_low = fold(index >> 7, index & (LANES - 1), share)
@@ -532,49 +541,55 @@
     wide = fold_of(share)
     for n in range(idx_ref.shape[0]):
         place_mask(mask_out, n * LANES, key_high[n : n + 1, :])
-        place_hot(hot_out, n * LANES, key_columns[:, n : n + 1], wide)
-    parts = [exact_parts(own_ref[f]) for f in range(FEATS)]
-    for n in range(rows):
-        values = [[x[n : n + 1, :] for x in pair] for pair in parts]
-        place_values(spread, n * LANES, mask_out[:, n * LANES : (n + 1) * LANES], values)
-    sum_out[...] = dot(spread[...], hot_out[0 : rows * LANES, :], 1, 0)
-
-
-def owner_indices(own, index, share, width):
+        place_hot(hot_low if n < middle else hot_high, n % middle * LANES, key_columns[:, n : n + 1], wide)
+    for j, ref in enumerate((own_ref, next_ref)):
+        parts = [exact_parts(ref[f]) for f in range(FEATS)]
+        for i in range(rows):
+            at = (j * rows + i) * LANES
+            values = [[x[i : i + 1, :] for x in pair] for pair in parts]
+            place_values(spread, at, mask_out[:, at : at + LANES], values)
+    sum_out[...] = dot(spread[...], hot_low[0 : 2 * rows * LANES, :], 1, 0)
+
+
+def owner_indices(own, following, index, share, width):
     rows = own.shape[1]
     wide = fold_of(share)
     height = width // LANES // wide
     slots = index.shape[0] * LANES
     return pl.pallas_call(
         partial(owner_index_kernel, share=share),
-        in_specs=[vmem_spec()] * 2,
-        out_specs=[vmem_spec()] * 3,
+        in_specs=[vmem_spec()] * 3,
+        out_specs=[vmem_spec()] * 4,
         out_shape=[
             jax.ShapeDtypeStruct((height, slots), BF16),
-            jax.ShapeDtypeStruct((slots, wide * LANES), BF16),
+            jax.ShapeDtypeStruct((slots // 2, wide * LANES), BF16),
+            jax.ShapeDtypeStruct((slots // 2, wide * LANES), BF16),
             jax.ShapeDtypeStruct((2 * FEATS * height, wide * LANES), F32),
         ],
-        scratch_shapes=[pltpu.VMEM((2 * FEATS * height, rows * LANES), BF16)],
+        scratch_shapes=[pltpu.VMEM((2 * FEATS * height, 2 * rows * LANES), BF16)],
         compiler_params=pltpu.CompilerParams(vmem_limit_bytes=40 * 1024 * 1024),
         name="prep_owner",
-    )(own, index)
-
-
-def owner_kernel(*refs, nd, rows, parts, nv, nc, share):
-    recv = refs[: nd - 1]
-    mask_ref, hot_ref, sum_ref, w_ref = refs[nd - 1 : nd + 3]
+    )(own, following, index)
+
+
+def owner_kernel(me_ref, *refs, nd, rows, parts, nv, nc, share):
+    recv = refs[: nd - 2]
+    mask_ref, hot_low, hot_high, sum_ref, w_ref = refs[nd - 2 : nd + 3]
     outs = refs[nd + 3 : nd + 3 + parts]
     spread, summed = refs[nd + 3 + parts :]
-    my_view = lax.axis_index("view")
-    my_chip = lax.axis_index("chip")
-    skip = rows * LANES
-    for j in range(nd - 1):
+    my_view = me_ref[1]
+    my_chip = me_ref[2]
+    skip = 2 * rows * LANES
+    for j in range(nd - 2):
         pairs = [exact_parts(recv[j][f]) for f in range(FEATS)]
         for i in range(rows):
             at = (j * rows + i) * LANES
             values = [[x[i : i + 1, :] for x in pair] for pair in pairs]
             place_values(spread, at, mask_ref[:, skip + at : skip + at + LANES], values)
-    result = sum_ref[...] + dot(spread[...], hot_ref[skip:, :], 1, 0)
+    middle = hot_low.shape[0] - skip
+    result = sum_ref[...] + dot(spread[:, middle:], hot_high[...], 1, 0)
+    if middle > 0:
+        result = result + dot(spread[:, 0:middle], hot_low[skip:, :], 1, 0)
     wide = fold_of(share)
     height = share // wide
     total = parts * height
@@ -593,24 +608,24 @@
             outs[dv * nc + dc][...] = summed[where]
 
 
-def owner_sums(received, prepared, weights, nd, rows, nv, nc, share):
+def owner_sums(me, received, prepared, weights, nd, rows, nv, nc, share):
     parts = nv * nc
     height, slots = prepared[0].shape
     return pl.pallas_call(
         partial(owner_kernel, nd=nd, rows=rows, parts=parts, nv=nv, nc=nc, share=share),
-        in_specs=[vmem_spec()] * (nd + 3),
+        in_specs=[smem_spec()] + [vmem_spec()] * (nd + 3),
         out_specs=[vmem_spec()] * parts,
         out_shape=[jax.ShapeDtypeStruct((FEATS + 1, share, LANES), F32)] * parts,
         scratch_shapes=[
-            pltpu.VMEM((2 * FEATS * height, slots - rows * LANES), BF16),
+            pltpu.VMEM((2 * FEATS * height, slots - 2 * rows * LANES), BF16),
             pltpu.VMEM((parts, FEATS + 1, share, LANES), F32),
         ],
         compiler_params=pltpu.CompilerParams(vmem_limit_bytes=40 * 1024 * 1024),
         name="owner_sums",
-    )(*received, *prepared, weights)
-
-
-def pullback_kernel(params_ref, *refs, nv, nc, coefs):
+    )(me, *received, *prepared, weights)
+
+
+def pullback_kernel(at_ref, params_ref, *refs, nv, nc, coefs):
     recv = refs[: nv * nc]
     out_ref, flat = refs[nv * nc :]
     share = recv[0].shape[1]
@@ -670,16 +685,24 @@
         out_ref[10 + c * coefs : 10 + (c + 1) * coefs, :] = harmonics[c]
 
 
-def pull_back(params, received, nv, nc, coefs):
+def pull_back(at, params, received, nv, nc, coefs):
+    parts = nv * nc
+    columns = params.shape[1] // parts
+    block = received[0].shape
     return pl.pallas_call(
         partial(pullback_kernel, nv=nv, nc=nc, coefs=coefs),
-        in_specs=[vmem_spec()] * (1 + nv * nc),
-        out_specs=vmem_spec(),
-        out_shape=jax.ShapeDtypeStruct(params.shape, F32),
-        scratch_shapes=[pltpu.VMEM((16, params.shape[1]), F32)],
+        grid_spec=pltpu.PrefetchScalarGridSpec(
+            num_scalar_prefetch=1,
+            grid=(1,),
+            in_specs=[pl.BlockSpec((params.shape[0], columns), lambda i, at_ref: (0, at_ref[0]))]
+            + [pl.BlockSpec(block, lambda i, at_ref: (0, 0, 0))] * parts,
+            out_specs=pl.BlockSpec((params.shape[0], columns), lambda i, at_ref: (0, 0)),
+            scratch_shapes=[pltpu.VMEM((16, columns), F32)],
+        ),
+        out_shape=jax.ShapeDtypeStruct((params.shape[0], columns), F32),
         compiler_params=pltpu.CompilerParams(vmem_limit_bytes=40 * 1024 * 1024),
         name="pull_back",
-    )(params, *received)
+    )(at, params, *received)
 
 
 def hop_order(nd, first):
@@ -703,22 +726,29 @@
 ):
     cap = requests.shape[4]
     rows = -(-cap // LANES)
-    later = (margin_blocks, depth_orders, tile_counts, tile_lists, jnp.swapaxes(target, 3, 4))
-    outs = send(cameras, view_basis, params, requests, later, nd, nv, nc, cap, rows)
-    packets = outs[:nd]
-    index, weights, owned, blocks, orders, counts, ids, swapped = outs[nd:]
+    my_view = lax.axis_index("view")
+    my_chip = lax.axis_index("chip")
+    me = jnp.stack([lax.axis_index("dev"), my_view, my_chip]).astype(jnp.int32)
+    at = (my_view * nc + my_chip).astype(jnp.int32).reshape(1)
+
+    *packets, index, weights = send(me, cameras, view_basis, params, requests, nd, cap, rows)
     received = list(packets)
     for j in hop_order(nd, FORTH):
         received[j] = lax.ppermute(packets[j], "dev", [(i, i ^ j) for i in range(nd)])
-    prepared = tile_indices(packets[0], blocks, orders, counts, nd, cap)
+    prepared = tile_indices(
+        me, packets[0], margin_blocks, depth_orders, tile_counts, tile_lists, nd, cap
+    )
     tiles, entries = margin_blocks.shape[3:]
-    *returns, images = render(received[1:], prepared, ids, swapped, nd, rows, tiles, entries)
+    swapped = jnp.swapaxes(target, 3, 4)
+    *prepared, part = prepared
+    part = gather_more(received[1 : nd - 1], 1, prepared[0], prepared[1], part)
+    *returns, images = render(received[nd - 1], (*prepared, part), swapped, nd, rows, tiles, entries)
     back = list(returns)
     for j in hop_order(nd, BACK):
         back[j] = lax.ppermute(returns[j], "dev", [(i, i ^ j) for i in range(nd)])
     share = params.shape[1] // LANES // (nv * nc)
-    sorted_own = owner_indices(returns[0], index, share, params.shape[1])
-    shares = owner_sums(back[1:], sorted_own, weights, nd, rows, nv, nc, share)
+    sorted_own = owner_indices(returns[0], back[1], index, share, params.shape[1])
+    shares = owner_sums(me, back[2:], sorted_own, weights, nd, rows, nv, nc, share)
     arrived = []
     for dv in range(nv):
         for dc in range(nc):
@@ -727,7 +757,7 @@
             ]
             piece = shares[dv * nc + dc]
             arrived.append(piece if dv + dc == 0 else lax.ppermute(piece, ("view", "chip"), pairs))
-    grads = pull_back(owned, arrived, nv, nc, view_basis.shape[1])
+    grads = pull_back(at, params, arrived, nv, nc, view_basis.shape[1])
     return (grads, jnp.swapaxes(images, 3, 4))
 
 

time: 41 us -> 37.4 us (0.912)
  local copies, waits for them, and re-layouts: 4.22 us -> 2.51 us
  Pallas kernels: 15.6 us -> 13.9 us
    unnamed x18 -> x20, local copies, waits for them, and re-layouts: 4.22 us -> 2.51 us
    ppermute x3, waiting for transfers between devices: 2.87 us -> 1.37 us  [local(): back[j] = lax.ppermute(returns[j], 'dev', [(i, i ^ j) for i in range(nd)])]
    ppermute x3, waiting for transfers between devices: 1.96 us -> 3.3 us  [local(): lax.ppermute(packets[j], 'dev', [(i, i ^ j) for i in range(nd)])]
    pallas_call x1, Pallas kernels: 7.7 us -> 6.51 us  [render(): pl.pallas_call(partial(render_kernel, nd=nd, rows=rows, tiles=tiles, entr...]
    pallas_call x3 -> x4, Pallas kernels: 6.33 us -> 5.23 us  [the longest x1 2.25 us: send(): pl.pallas_call(partial(send_kernel, nd=nd, cap=cap, rows=rows), in_specs=...]
    pallas_call x1, Pallas kernels: 0.69 us -> 1.1 us  [owner_sums(): pl.pallas_call(partial(owner_kernel, nd=nd, rows=rows, parts=parts, nv=nv...]
  transfers between devices with their start and end apart: 9 -> 9, of which waited for: 4 -> 5; matrix products, arithmetic and copies ran while one was open for 0% -> 0% of each run, Pallas kernels for 5% -> 8%
where the time goes in v4:
time: 37.4 us; the launch traced here: 37.2 us
  Pallas kernels  13.9 us (37%)
  starting transfers between devices  12.1 us (32%)
  waiting for transfers between devices  7.87 us (21%)
  local copies, waits for them, and re-layouts  2.51 us (7%)
  between operations  0.75 us (2%)
    pallas_call x1, Pallas kernels, render(): pl.pallas_call(partial(render_kernel, nd=nd, rows=rows, tiles=tiles, entr...  6.51 us
    ppermute x3, starting transfers between devices, local(): lax.ppermute(packets[j], 'dev', [(i, i ^ j) for i in range(nd)])  5.68 us
    ppermute x3, starting transfers between devices, local(): back[j] = lax.ppermute(returns[j], 'dev', [(i, i ^ j) for i in range(nd)])  4.44 us
    ppermute x3, waiting for transfers between devices, local(): lax.ppermute(packets[j], 'dev', [(i, i ^ j) for i in range(nd)])  3.3 us
    ppermute x3, waiting for transfers between devices, local(): lax.ppermute(piece, ('view', 'chip'), pairs)  3.21 us
    unnamed x20, local copies, waits for them, and re-layouts  2.51 us
    pallas_call x1, Pallas kernels, send(): pl.pallas_call(partial(send_kernel, nd=nd, cap=cap, rows=rows), in_specs=...  2.25 us
    ppermute x3, starting transfers between devices, local(): lax.ppermute(piece, ('view', 'chip'), pairs)  1.93 us
  transfers between devices with their start and end apart: 9, of which 5 were waited for; matrix products, arithmetic and copies ran while one was open for 0% of the time, Pallas kernels for 8%

profile of v4, /device:TPU:0, one launch (start us, length us, event | category | flops | bytes accessed | tf_op | source)
XLA Modules:
  0.0 37.2 jit_solution(7902297794312363731)
XLA Ops:
  0.6 0.0 copy-start.3
  0.6 0.0 copy-start.6
  0.7 0.0 copy-start.7
  0.7 0.1 pad_add_fusion.me_ref
  0.7 0.6 %copy-done.3 = s32[1,4,1,1,960]{4,3,2,1,0:T(1,128)S(1)} copy-done((s32[1,4,1,1,960]{4,3,2,1,0:T(1,128)S(1)}, s32[1,4,1,1,960]{4,3,2,1,0:T(1,128)}, u32[]{:S(2)}) %copy-start.3) | copy-done | bytes 15384
  1.3 0.0 copy-done.6
  1.4 0.0 copy-done.7
  1.4 0.0 copy-start
  1.4 1.2 %copy-done = f32[58,4096]{1,0:T(8,128)S(1)} copy-done((f32[58,4096]{1,0:T(8,128)S(1)}, f32[58,4096]{1,0:T(8,128)}, u32[]{:S(2)}) %copy-start) | copy-done | bytes 950296
  2.6 0.0 copy-start.4
  2.6 0.0 copy-start.5
  2.6 2.3 %project_gather.1 = (f32[9,8,128]{2,1,0:T(8,128)S(1)}, f32[9,8,128]{2,1,0:T(8,128)S(1)}, f32[9,8,128]{2,1,0:T(8,128)S(1)}, f32[9,8,128]{2,1,0:T(8,128)S(1)}, s32...) custom-call(s32[3]{0:T(128)S(1)} %pad_add_fusion.me_ref, f32[1,2,4]{2,1,0:T(2,128)S(1)} %copy-done.6, f32[1,16]{1,0:T(1,128)S(1)} %copy-done.7, ...), custom_call_target="tpu_custom_call" | custom-call | tf_op jit(solution)/shard_map/project_gather/pallas_call | solution.py:133
  4.8 3.1 %collective-permute-start.1 = (f32[9,8,128]{2,1,0:T(8,128)S(1)}, f32[9,8,128]{2,1,0:T(8,128)S(1)}, u32[]{:S(2)}, u32[]{:S(2)}) collective-permute-start(f32[9,8,128]{2,1,0:T(8,128)S(1)} %get-tuple-element.32), channel_id=1, source_target_pairs={{0,4},{4,0},{8,12},{12,8},{1,5},{5,1},{9,13},{13,9},{2,6},{6,2},{1... | collective-permute-start | bytes 110600 | tf_op jit(solution)/shard_map/ppermute | solution.py:737
  7.9 2.6 %collective-permute-start.2 = (f32[9,8,128]{2,1,0:T(8,128)S(1)}, f32[9,8,128]{2,1,0:T(8,128)S(1)}, u32[]{:S(2)}, u32[]{:S(2)}) collective-permute-start(f32[9,8,128]{2,1,0:T(8,128)S(1)} %get-tuple-element.33), channel_id=1, source_target_pairs={{0,8},{4,12},{8,0},{12,4},{1,9},{5,13},{9,1},{13,5},{2,10},{6,14},... | collective-permute-start | bytes 110600 | tf_op jit(solution)/shard_map/ppermute | solution.py:737
  10.5 0.0 copy-start.8
  10.5 0.0 copy-start.9
  10.5 0.0 collective-permute-start
  10.5 0.0 copy-done.4
  10.5 0.0 copy-done.5
  10.5 0.6 %copy-done.8 = s32[1,1,1,16]{3,2,1,0:T(1,128)S(1)} copy-done((s32[1,1,1,16]{3,2,1,0:T(1,128)S(1)}, s32[1,1,1,16]{3,2,1,0:T(1,128)}, u32[]{:S(2)}) %copy-start.8) | copy-done | bytes 88
  11.2 0.0 copy-done.9
  11.2 1.1 %prep_tiles.1 = (s32[16,256]{1,0:T(8,128)S(1)}, s32[16,256]{1,0:T(8,128)S(1)}, f32[16,256]{1,0:T(8,128)S(1)}, f32[2,16,128]{2,1,0:T(8,128)S(1)}, f32[9,16,256]{2,1,0:T(8,128)S(1)}) custom-call(s32[3]{0:T(128)S(1)} %pad_add_fusion.me_ref, f32[9,8,128]{2,1,0:T(8,128)S(1)} %get-tuple-element.27.own_ref, s32[1,1,1,16,256]{4,3,2,1,0:T(8,128)S(1)} %copy-done.4, ...), custom_call_target="tpu_custom_call" | custom-call | tf_op jit(solution)/shard_map/prep_tiles/pallas_call | solution.py:248
  12.3 0.0 collective-permute-done.1.refs_0_
  12.3 1.2 %collective-permute-done.2.refs_1_ = f32[9,8,128]{2,1,0:T(8,128)S(1)} collective-permute-done((f32[9,8,128]{2,1,0:T(8,128)S(1)}, f32[9,8,128]{2,1,0:T(8,128)S(1)}, u32[]{:S(2)}, u32[]{:S(2)}) %collective-permute-start.2) | collective-permute-done | bytes 36896 | tf_op jit(solution)/shard_map/ppermute | solution.py:737
  13.5 0.0 copy-start.2
  13.5 0.7 %prep_gather.1.refs_5_ = f32[9,16,256]{2,1,0:T(8,128)S(1)} custom-call(f32[9,8,128]{2,1,0:T(8,128)S(1)} %collective-permute-done.1.refs_0_, f32[9,8,128]{2,1,0:T(8,128)S(1)} %collective-permute-done.2.refs_1_, s32[16,256]{1,0:T(8,128)S(1)} %get-tuple-element.28.refs_2_.refs_1_, s32[16,256]{1,0:T(8,128)S(1)} %get-tuple-element.29.refs_3_.refs_2_, ...), custom_call_target="tpu_custom_call" | custom-call | tf_op jit(solution)/shard_map/prep_gather/pallas_call | solution.py:288
  14.2 2.1 %collective-permute-done.refs_0_ = f32[9,8,128]{2,1,0:T(8,128)S(1)} collective-permute-done((f32[9,8,128]{2,1,0:T(8,128)S(1)}, f32[9,8,128]{2,1,0:T(8,128)S(1)}, u32[]{:S(2)}, u32[]{:S(2)}) %collective-permute-start) | collective-permute-done | bytes 36896 | tf_op jit(solution)/shard_map/ppermute | solution.py:737
  16.3 0.0 copy-done.2
  16.3 6.5 %render_tiles.1 = (f32[9,8,128]{2,1,0:T(8,128)S(1)}, f32[9,8,128]{2,1,0:T(8,128)S(1)}, f32[9,8,128]{2,1,0:T(8,128)S(1)}, f32[9,8,128]{2,1,0:T(8,128)S(1)}, f32[1,1,1,3,16,256]{5,4,3,2,1,0:T(8,128)}) custom-call(f32[9,8,128]{2,1,0:T(8,128)S(1)} %collective-permute-done.refs_0_, s32[16,256]{1,0:T(8,128)S(1)} %get-tuple-element.28.refs_2_.refs_1_, ...), custom_call_target="tpu_custom_call" | custom-call | tf_op jit(solution)/shard_map/render_tiles/pallas_call | solution.py:509
  22.8 0.1 collective-permute-start.5
  22.9 1.0 %collective-permute-start.3 = (f32[9,8,128]{2,1,0:T(8,128)S(1)}, f32[9,8,128]{2,1,0:T(8,128)S(1)}, u32[]{:S(2)}, u32[]{:S(2)}) collective-permute-start(f32[9,8,128]{2,1,0:T(8,128)S(1)} %get-tuple-element.35), channel_id=1, source_target_pairs={{0,8},{4,12},{8,0},{12,4},{1,9},{5,13},{9,1},{13,5},{2,10},{6,14},... | collective-permute-start | bytes 110600 | tf_op jit(solution)/shard_map/ppermute | solution.py:748
  23.9 3.3 %collective-permute-start.4 = (f32[9,8,128]{2,1,0:T(8,128)S(1)}, f32[9,8,128]{2,1,0:T(8,128)S(1)}, u32[]{:S(2)}, u32[]{:S(2)}) collective-permute-start(f32[9,8,128]{2,1,0:T(8,128)S(1)} %get-tuple-element.36), channel_id=1, source_target_pairs={{0,12},{4,8},{8,4},{12,0},{1,13},{5,9},{9,5},{13,1},{2,14},{6,10},... | collective-permute-start | bytes 110600 | tf_op jit(solution)/shard_map/ppermute | solution.py:748
  27.3 0.0 collective-permute-done.5.next_ref
  27.3 1.0 %prep_owner.1 = (bf16[16,4096]{1,0:T(8,128)(2,1)S(1)}, bf16[2048,256]{1,0:T(8,128)(2,1)S(1)}, bf16[2048,256]{1,0:T(8,128)(2,1)S(1)}, f32[288,256]{1,0:T(8,128)S(1)}) custom-call(f32[9,8,128]{2,1,0:T(8,128)S(1)} %get-tuple-element.37.own_ref, f32[9,8,128]{2,1,0:T(8,128)S(1)} %collective-permute-done.5.next_ref, s32[32,128]{1,0:T(8,128)S(1)} %get-tuple-element.39.idx_ref), custom_call_target="tpu_custom_call" | custom-call | tf_op jit(solution)/shard_map/prep_owner/pallas_call | solution.py:559
  28.3 0.0 collective-permute-done.3.refs_0_
  28.3 1.4 %collective-permute-done.4.refs_1_ = f32[9,8,128]{2,1,0:T(8,128)S(1)} collective-permute-done((f32[9,8,128]{2,1,0:T(8,128)S(1)}, f32[9,8,128]{2,1,0:T(8,128)S(1)}, u32[]{:S(2)}, u32[]{:S(2)}) %collective-permute-start.4) | collective-permute-done | bytes 36896 | tf_op jit(solution)/shard_map/ppermute | solution.py:748
  29.7 0.0 copy-start.1
  29.7 1.1 %owner_sums.1 = (f32[10,8,128]{2,1,0:T(8,128)S(1)}, f32[10,8,128]{2,1,0:T(8,128)S(1)}, f32[10,8,128]{2,1,0:T(8,128)S(1)}, f32[10,8,128]{2,1,0:T(8,128)S(1)}) custom-call(s32[3]{0:T(128)S(1)} %pad_add_fusion.me_ref, f32[9,8,128]{2,1,0:T(8,128)S(1)} %collective-permute-done.3.refs_0_, f32[9,8,128]{2,1,0:T(8,128)S(1)} %collective-permute-done.4.refs_1_, ...), custom_call_target="tpu_custom_call" | custom-call | tf_op jit(solution)/shard_map/owner_sums/pallas_call | solution.py:614
  30.8 0.1 collective-permute-start.6
  30.9 1.6 %collective-permute-start.7 = (f32[10,8,128]{2,1,0:T(8,128)S(1)}, f32[10,8,128]{2,1,0:T(8,128)S(1)}, u32[]{:S(2)}, u32[]{:S(2)}) collective-permute-start(f32[10,8,128]{2,1,0:T(8,128)S(1)} %get-tuple-element.47), channel_id=1, source_target_pairs={{0,2},{1,3},{2,0},{3,1},{4,6},{5,7},{6,4},{7,5},{8,10},{9,11},{10,... | collective-permute-start | bytes 122888 | tf_op jit(solution)/shard_map/ppermute | solution.py:759
  32.4 0.3 collective-permute-start.8
  32.7 0.0 collective-permute-done.6.refs_1_
  32.7 2.2 %collective-permute-done.7.refs_2_ = f32[10,8,128]{2,1,0:T(8,128)S(1)} collective-permute-done((f32[10,8,128]{2,1,0:T(8,128)S(1)}, f32[10,8,128]{2,1,0:T(8,128)S(1)}, u32[]{:S(2)}, u32[]{:S(2)}) %collective-permute-start.7) | collective-permute-done | bytes 40992 | tf_op jit(solution)/shard_map/ppermute | solution.py:759
  34.9 1.0 %collective-permute-done.8.refs_3_ = f32[10,8,128]{2,1,0:T(8,128)S(1)} collective-permute-done((f32[10,8,128]{2,1,0:T(8,128)S(1)}, f32[10,8,128]{2,1,0:T(8,128)S(1)}, u32[]{:S(2)}, u32[]{:S(2)}) %collective-permute-start.8) | collective-permute-done | bytes 40992 | tf_op jit(solution)/shard_map/ppermute | solution.py:759
  35.9 0.0 copy-done.1
  35.9 1.2 %pull_back.1 = f32[58,1024]{1,0:T(8,128)} custom-call(s32[1]{0:T(128)} %bitcast.at_ref, f32[58,4096]{1,0:T(8,128)S(1)} %copy-done.1, f32[10,8,128]{2,1,0:T(8,128)S(1)} %get-tuple-element.45.refs_0_, f32[10,8,128]{2,1,0:T(8,128)S(1)} %collective-permute-done.6.refs_1_, f32[10,8,128]{2,1,0:T(8,128)S(1)} %collective-permute-done.7.refs_2_, ...), custom_call_target="tpu_custom_call" | custom-call | tf_op jit(solution)/shard_map/pull_back/pallas_call | solution.py:692
Async XLA Ops:
  0.6 0.7 %copy-start.3 = (s32[1,4,1,1,960]{4,3,2,1,0:T(1,128)S(1)}, s32[1,4,1,1,960]{4,3,2,1,0:T(1,128)}, u32[]{:S(2)}) copy-start(s32[1,4,1,1,960]{4,3,2,1,0:T(1,128)} %req_ref.1) | copy-start | bytes 46084
  0.6 0.7 %copy-start.6 = (f32[1,2,4]{2,1,0:T(2,128)S(1)}, f32[1,2,4]{2,1,0:T(2,128)}, u32[]{:S(2)}) copy-start(f32[1,2,4]{2,1,0:T(2,128)} %cam_ref.1) | copy-start | bytes 100
  0.7 0.7 %copy-start.7 = (f32[1,16]{1,0:T(1,128)S(1)}, f32[1,16]{1,0:T(1,128)}, u32[]{:S(2)}) copy-start(f32[1,16]{1,0:T(1,128)} %basis_ref.1) | copy-start | bytes 196
  1.4 1.2 %copy-start = (f32[58,4096]{1,0:T(8,128)S(1)}, f32[58,4096]{1,0:T(8,128)}, u32[]{:S(2)}) copy-start(f32[58,4096]{1,0:T(8,128)} %params_ref.3) | copy-start | bytes 2850820
  2.6 8.0 %copy-start.4 = (s32[1,1,1,16,256]{4,3,2,1,0:T(8,128)S(1)}, s32[1,1,1,16,256]{4,3,2,1,0:T(8,128)}, u32[]{:S(2)}) copy-start(s32[1,1,1,16,256]{4,3,2,1,0:T(8,128)} %blocks_ref.1) | copy-start | bytes 49156
  2.6 8.0 %copy-start.5 = (s32[1,1,1,16,256]{4,3,2,1,0:T(8,128)S(1)}, s32[1,1,1,16,256]{4,3,2,1,0:T(8,128)}, u32[]{:S(2)}) copy-start(s32[1,1,1,16,256]{4,3,2,1,0:T(8,128)} %orders_ref.1) | copy-start | bytes 49156
  4.8 7.4 %collective-permute-start.1 = (f32[9,8,128]{2,1,0:T(8,128)S(1)}, f32[9,8,128]{2,1,0:T(8,128)S(1)}, u32[]{:S(2)}, u32[]{:S(2)}) collective-permute-start(f32[9,8,128]{2,1,0:T(8,128)S(1)} %get-tuple-element.32), channel_id=1, source_target_pairs={{0,4},{4,0},{8,12},{12,8},{1,5},{5,1},{9,13},{13,9},{2,6},{6,2},{1... | collective-permute-start | bytes 110600 | tf_op jit(solution)/shard_map/ppermute | solution.py:737
  7.9 5.5 %collective-permute-start.2 = (f32[9,8,128]{2,1,0:T(8,128)S(1)}, f32[9,8,128]{2,1,0:T(8,128)S(1)}, u32[]{:S(2)}, u32[]{:S(2)}) collective-permute-start(f32[9,8,128]{2,1,0:T(8,128)S(1)} %get-tuple-element.33), channel_id=1, source_target_pairs={{0,8},{4,12},{8,0},{12,4},{1,9},{5,13},{9,1},{13,5},{2,10},{6,14},... | collective-permute-start | bytes 110600 | tf_op jit(solution)/shard_map/ppermute | solution.py:737
  10.5 0.7 %copy-start.8 = (s32[1,1,1,16]{3,2,1,0:T(1,128)S(1)}, s32[1,1,1,16]{3,2,1,0:T(1,128)}, u32[]{:S(2)}) copy-start(s32[1,1,1,16]{3,2,1,0:T(1,128)} %counts_ref.1) | copy-start | bytes 196
  10.5 0.7 %copy-start.9 = (s32[1,1,1,16]{3,2,1,0:T(1,128)S(1)}, s32[1,1,1,16]{3,2,1,0:T(1,128)}, u32[]{:S(2)}) copy-start(s32[1,1,1,16]{3,2,1,0:T(1,128)} %ids_ref.1) | copy-start | bytes 196
  10.5 5.8 %collective-permute-start = (f32[9,8,128]{2,1,0:T(8,128)S(1)}, f32[9,8,128]{2,1,0:T(8,128)S(1)}, u32[]{:S(2)}, u32[]{:S(2)}) collective-permute-start(f32[9,8,128]{2,1,0:T(8,128)S(1)} %get-tuple-element.26), channel_id=1, source_target_pairs={{0,12},{4,8},{8,4},{12,0},{1,13},{5,9},{9,5},{13,1},{2,14},{6,10},... | collective-permute-start | bytes 110600 | tf_op jit(solution)/shard_map/ppermute | solution.py:737
  13.5 2.8 %copy-start.2 = (f32[1,1,1,16,3,256]{5,3,4,2,1,0:T(8,128)S(1)}, f32[1,1,1,16,3,256]{5,3,4,2,1,0:T(8,128)}, u32[]{:S(2)}) copy-start(f32[1,1,1,16,3,256]{5,3,4,2,1,0:T(8,128)} %param.17) | copy-start | bytes 147460
  22.8 4.5 %collective-permute-start.5 = (f32[9,8,128]{2,1,0:T(8,128)S(1)}, f32[9,8,128]{2,1,0:T(8,128)S(1)}, u32[]{:S(2)}, u32[]{:S(2)}) collective-permute-start(f32[9,8,128]{2,1,0:T(8,128)S(1)} %get-tuple-element.38), channel_id=1, source_target_pairs={{0,4},{4,0},{8,12},{12,8},{1,5},{5,1},{9,13},{13,9},{2,6},{6,2},{1... | collective-permute-start | bytes 110600 | tf_op jit(solution)/shard_map/ppermute | solution.py:748
  22.9 5.4 %collective-permute-start.3 = (f32[9,8,128]{2,1,0:T(8,128)S(1)}, f32[9,8,128]{2,1,0:T(8,128)S(1)}, u32[]{:S(2)}, u32[]{:S(2)}) collective-permute-start(f32[9,8,128]{2,1,0:T(8,128)S(1)} %get-tuple-element.35), channel_id=1, source_target_pairs={{0,8},{4,12},{8,0},{12,4},{1,9},{5,13},{9,1},{13,5},{2,10},{6,14},... | collective-permute-start | bytes 110600 | tf_op jit(solution)/shard_map/ppermute | solution.py:748
  23.9 5.8 %collective-permute-start.4 = (f32[9,8,128]{2,1,0:T(8,128)S(1)}, f32[9,8,128]{2,1,0:T(8,128)S(1)}, u32[]{:S(2)}, u32[]{:S(2)}) collective-permute-start(f32[9,8,128]{2,1,0:T(8,128)S(1)} %get-tuple-element.36), channel_id=1, source_target_pairs={{0,12},{4,8},{8,4},{12,0},{1,13},{5,9},{9,5},{13,1},{2,14},{6,10},... | collective-permute-start | bytes 110600 | tf_op jit(solution)/shard_map/ppermute | solution.py:748
  29.7 6.3 %copy-start.1 = (f32[58,4096]{1,0:T(8,128)S(1)}, f32[58,4096]{1,0:T(8,128)}, u32[]{:S(2)}) copy-start(f32[58,4096]{1,0:T(8,128)} %params_ref.3) | copy-start | bytes 2850820
  30.8 1.9 %collective-permute-start.6 = (f32[10,8,128]{2,1,0:T(8,128)S(1)}, f32[10,8,128]{2,1,0:T(8,128)S(1)}, u32[]{:S(2)}, u32[]{:S(2)}) collective-permute-start(f32[10,8,128]{2,1,0:T(8,128)S(1)} %get-tuple-element.46), channel_id=1, source_target_pairs={{0,1},{1,0},{2,3},{3,2},{4,5},{5,4},{6,7},{7,6},{8,9},{9,8},{10,11... | collective-permute-start | bytes 122888 | tf_op jit(solution)/shard_map/ppermute | solution.py:759
  30.9 4.1 %collective-permute-start.7 = (f32[10,8,128]{2,1,0:T(8,128)S(1)}, f32[10,8,128]{2,1,0:T(8,128)S(1)}, u32[]{:S(2)}, u32[]{:S(2)}) collective-permute-start(f32[10,8,128]{2,1,0:T(8,128)S(1)} %get-tuple-element.47), channel_id=1, source_target_pairs={{0,2},{1,3},{2,0},{3,1},{4,6},{5,7},{6,4},{7,5},{8,10},{9,11},{10,... | collective-permute-start | bytes 122888 | tf_op jit(solution)/shard_map/ppermute | solution.py:759
  32.4 3.5 %collective-permute-start.8 = (f32[10,8,128]{2,1,0:T(8,128)S(1)}, f32[10,8,128]{2,1,0:T(8,128)S(1)}, u32[]{:S(2)}, u32[]{:S(2)}) collective-permute-start(f32[10,8,128]{2,1,0:T(8,128)S(1)} %get-tuple-element.48), channel_id=1, source_target_pairs={{0,3},{1,2},{2,1},{3,0},{4,7},{5,6},{6,5},{7,4},{8,11},{9,10},{10,... | collective-permute-start | bytes 122888 | tf_op jit(solution)/shard_map/ppermute | solution.py:759

commit v5 on v4

--- a/solution.py
+++ b/solution.py
@@ -19,7 +19,7 @@
 FEATS = 9
 FORTH = (1, 2, 3)
 BACK = (1, 2, 3)
-GROUP = 16
+GROUP = 8
 
 
 def lane_take(row, index):
@@ -36,8 +36,8 @@
 
 
 def send_kernel(me_ref, cam_ref, basis_ref, params_ref, req_ref, *refs, nd, cap, rows):
-    outs = refs[:nd]
-    idx_out, w_out, feat, w_scr = refs[nd:]
+    outs = refs[: nd - 1]
+    idx_out, w_out, feat, w_scr = refs[nd - 1 :]
     me = me_ref[0]
     width = params_ref.shape[1]
     coefs = basis_ref.shape[-1]
@@ -55,14 +55,16 @@
     weights = weights + jnp.where(row8 == 2, at10, 0.0)
     weights = weights + jnp.where(row8 == 3, pltpu.roll(basis_row, 10 + coefs, 1), 0.0)
     weights = weights + jnp.where(row8 == 4, pltpu.roll(basis_row, 10 + 2 * coefs, 1), 0.0)
-    w_scr[...] = weights
-    linear = lax.dot_general(
-        w_scr[:, 0 : params_ref.shape[0]],
-        params_ref[...],
-        (((1,), (0,)), ((), ())),
-        precision=lax.Precision.HIGHEST,
-        preferred_element_type=F32,
-    )
+    columns = weights.T
+    last = params_ref.shape[0]
+
+    def weighted(c, low, high):
+        first, end = low // 8 * 8, min(-(-high // 8) * 8, last)
+        return jnp.sum(params_ref[first:end, :] * columns[first:end, c : c + 1], axis=0, keepdims=True)
+
+    linear = [weighted(0, 0, 3), weighted(1, 0, 3)]
+    for c in range(3):
+        linear.append(weighted(2 + c, 10 + c * coefs, 10 + (c + 1) * coefs))
 
     def cam(i, j):
         return cam_ref[0, i : i + 1, j : j + 1]
@@ -81,14 +83,14 @@
     inverse = 1.0 / (upper * lower - cross * cross)
     logit = row(9)
     log_opacity = jnp.minimum(logit, 0.0) * LOG2E - LOG2E * jnp.log(1.0 + jnp.exp(-jnp.abs(logit)))
-    feat[0:1, :] = linear[0:1, :] + cam(0, 3)
-    feat[1:2, :] = linear[1:2, :] + cam(1, 3)
+    feat[0:1, :] = linear[0] + cam(0, 3)
+    feat[1:2, :] = linear[1] + cam(1, 3)
     feat[2:3, :] = lower * inverse * (0.5 * LOG2E)
     feat[3:4, :] = -cross * inverse * LOG2E
     feat[4:5, :] = upper * inverse * (0.5 * LOG2E)
     feat[5:6, :] = log_opacity
     for c in range(3):
-        feat[6 + c : 7 + c, :] = linear[2 + c : 3 + c, :] + 0.5
+        feat[6 + c : 7 + c, :] = linear[2 + c] + 0.5
 
     idx_out[...] = jnp.zeros_like(idx_out)
     for j in range(nd):
@@ -99,26 +101,26 @@
                 0, dest, 0, 0:1, i * LANES : i * LANES + size
             ]
     total = nd * rows
-    step = 8 if total % 8 == 0 else total
-    source_rows = width // LANES
-    for first in range(0, total, step):
-        index = idx_out[first : first + step, :]
-        low = index & (LANES - 1)
-        high = index >> 7
-        acc = [jnp.zeros((step, LANES), F32) for _ in range(FEATS)]
-        for r in range(source_rows):
-            here = high == r
-            for f in range(FEATS):
-                source = jnp.broadcast_to(feat[f : f + 1, r * LANES : (r + 1) * LANES], (step, LANES))
-                acc[f] = jnp.where(here, lane_take(source, low), acc[f])
+    step = 8 if rows % 8 == 0 else total - rows
+    for first in range(rows, total, step):
+        gathered = gather_features(feat, idx_out[first : first + step, :])
         for f in range(FEATS):
-            for n in range(step):
+            for n in range(0, step, rows if step > rows else step):
                 j, i = divmod(first + n, rows)
-                if rows % step == 0:
-                    if n == 0:
-                        outs[j][f, i : i + step, :] = acc[f]
-                else:
-                    outs[j][f, i : i + 1, :] = acc[f][n : n + 1, :]
+                size = min(rows, step)
+                outs[j - 1][f, i : i + size, :] = gathered[f][n : n + size, :]
+
+
+def gather_features(feat, index):
+    low = index & (LANES - 1)
+    high = index >> 7
+    acc = [jnp.zeros(index.shape, F32) for _ in range(FEATS)]
+    for r in range(feat.shape[1] // LANES):
+        here = high == r
+        for f in range(FEATS):
+            source = jnp.broadcast_to(feat[f : f + 1, r * LANES : (r + 1) * LANES], index.shape)
+            acc[f] = jnp.where(here, lane_take(source, low), acc[f])
+    return acc
 
 
 def vmem_spec():
@@ -134,12 +136,13 @@
         partial(send_kernel, nd=nd, cap=cap, rows=rows),
         in_specs=[smem_spec()] + [vmem_spec()] * 4,
         out_specs=[vmem_spec()] * (nd + 2),
-        out_shape=[jax.ShapeDtypeStruct((FEATS, rows, LANES), F32)] * nd
+        out_shape=[jax.ShapeDtypeStruct((FEATS, rows, LANES), F32)] * (nd - 1)
         + [
             jax.ShapeDtypeStruct((nd * rows, LANES), jnp.int32),
             jax.ShapeDtypeStruct((8, LANES), F32),
+            jax.ShapeDtypeStruct((16, params.shape[1]), F32),
         ],
-        scratch_shapes=[pltpu.VMEM((16, params.shape[1]), F32), pltpu.VMEM((8, LANES), F32)],
+        scratch_shapes=[pltpu.VMEM((8, LANES), F32)],
         compiler_params=pltpu.CompilerParams(vmem_limit_bytes=40 * 1024 * 1024),
         name="project_gather",
     )(me, cameras, basis, params, requests)
@@ -193,10 +196,13 @@
 
 
 def index_kernel(
-    me_ref, own_ref, blocks_ref, orders_ref, counts_ref, ids_ref, high_out, low_out, live_out, centre_out, part_out, *, nd, cap
+    me_ref, feat_ref, idx_ref, blocks_ref, orders_ref, counts_ref, ids_ref, high_out, low_out, live_out, centre_out, part_out, own_ref, *, nd, cap
 ):
     me = me_ref[0]
     rows = own_ref.shape[1]
+    own = gather_features(feat_ref, idx_ref[0 : max(rows, 8), :])
+    for f in range(FEATS):
+        own_ref[f] = own[f][0:rows, :]
     tiles, entries = blocks_ref.shape[3:]
     chunk = entries // 8
     halves = entries // LANES
@@ -241,13 +247,13 @@
                 part_out[f, first : first + 8, columns] = acc[f]
 
 
-def tile_indices(me, own, blocks, orders, counts, ids, nd, cap):
-    rows = own.shape[1]
+def tile_indices(me, features, index, blocks, orders, counts, ids, nd, cap):
+    rows = index.shape[0] // nd
     tiles, entries = blocks.shape[3:]
     wide = fold_of(rows)
     return pl.pallas_call(
         partial(index_kernel, nd=nd, cap=cap),
-        in_specs=[smem_spec()] + [vmem_spec()] * 5,
+        in_specs=[smem_spec()] + [vmem_spec()] * 6,
         out_specs=[vmem_spec()] * 5,
         out_shape=[
             jax.ShapeDtypeStruct((tiles, entries), jnp.int32),
@@ -256,9 +262,10 @@
             jax.ShapeDtypeStruct((2, tiles, LANES), F32),
             jax.ShapeDtypeStruct((FEATS, tiles, entries), F32),
         ],
+        scratch_shapes=[pltpu.VMEM((FEATS, rows, LANES), F32)],
         compiler_params=pltpu.CompilerParams(vmem_limit_bytes=40 * 1024 * 1024),
         name="prep_tiles",
-    )(me, own, blocks, orders, counts, ids)
+    )(me, features, index, blocks, orders, counts, ids)
 
 
 def gather_kernel(*refs, first_block):
@@ -436,7 +443,7 @@
             befores.append(before)
         rows_out = []
         for u in lanes:
-            colour_grad = dot(tints[u], whi_scr[u], 1, 1) + dot(tints[u], wlo_scr[u], 1, 1)
+            colour_grad = (dot(whi_scr[u], tints[u], 1, 1) + dot(wlo_scr[u], tints[u], 1, 1)).T
             for i in range(3):
                 both = colour_grad[8 * i : 8 * i + 8, :] + colour_grad[24 + 8 * i : 32 + 8 * i, :]
                 rows_out.append(jnp.sum(own_chunk * both, axis=0, keepdims=True))
@@ -459,10 +466,8 @@
                     mom[h, pl.ds((8 + i) * tiles + ts[u], 1), :] = rows_out[3 * u + i][:, columns]
         return carry
 
-    if tiles == GROUP:
-        group(0, 0)
-    else:
-        lax.fori_loop(0, tiles // GROUP, group, 0)
+    for step in range(tiles // GROUP):
+        group(step, 0)
 
     def got(i):
         return jnp.concatenate([mom[h, i * tiles : (i + 1) * tiles, :] for h in range(halves)], axis=1)
@@ -625,9 +630,8 @@
     )(me, *received, *prepared, weights)
 
 
-def pullback_kernel(at_ref, params_ref, *refs, nv, nc, coefs):
-    recv = refs[: nv * nc]
-    out_ref, flat = refs[nv * nc :]
+def pulled(recv, params_ref, flat, out_ref, before_ref, *, nc, coefs):
+    nv = len(recv) // nc
     share = recv[0].shape[1]
     columns = share * LANES
 
@@ -680,29 +684,59 @@
     logit = row(9)
     total[9] = total[9] / (1.0 + jnp.exp(logit))
     for i in range(10):
-        out_ref[i : i + 1, :] = total[i]
+        out_ref[i : i + 1, :] = total[i] if before_ref is None else total[i] + before_ref[i : i + 1, :]
     for c in range(3):
-        out_ref[10 + c * coefs : 10 + (c + 1) * coefs, :] = harmonics[c]
-
-
-def pull_back(at, params, received, nv, nc, coefs):
-    parts = nv * nc
+        at = slice(10 + c * coefs, 10 + (c + 1) * coefs)
+        out_ref[at, :] = harmonics[c] if before_ref is None else harmonics[c] + before_ref[at, :]
+
+
+def pull_own_kernel(at_ref, params_ref, *refs, nc, coefs):
+    out_ref, geometry_out, flat = refs[nc:]
+    geometry_out[...] = params_ref[0:16, :]
+    pulled(refs[:nc], params_ref, flat, out_ref, None, nc=nc, coefs=coefs)
+
+
+def pull_own(at, params, received, parts, coefs):
     columns = params.shape[1] // parts
     block = received[0].shape
+    count = params.shape[0]
     return pl.pallas_call(
-        partial(pullback_kernel, nv=nv, nc=nc, coefs=coefs),
+        partial(pull_own_kernel, nc=len(received), coefs=coefs),
         grid_spec=pltpu.PrefetchScalarGridSpec(
             num_scalar_prefetch=1,
             grid=(1,),
-            in_specs=[pl.BlockSpec((params.shape[0], columns), lambda i, at_ref: (0, at_ref[0]))]
-            + [pl.BlockSpec(block, lambda i, at_ref: (0, 0, 0))] * parts,
-            out_specs=pl.BlockSpec((params.shape[0], columns), lambda i, at_ref: (0, 0)),
+            in_specs=[pl.BlockSpec((count, columns), lambda i, at_ref: (0, at_ref[0]))]
+            + [pl.BlockSpec(block, lambda i, at_ref: (0, 0, 0))] * len(received),
+            out_specs=[
+                pl.BlockSpec((count, columns), lambda i, at_ref: (0, 0)),
+                pl.BlockSpec((16, columns), lambda i, at_ref: (0, 0)),
+            ],
             scratch_shapes=[pltpu.VMEM((16, columns), F32)],
         ),
-        out_shape=jax.ShapeDtypeStruct((params.shape[0], columns), F32),
+        out_shape=[
+            jax.ShapeDtypeStruct((count, columns), F32),
+            jax.ShapeDtypeStruct((16, columns), F32),
+        ],
+        compiler_params=pltpu.CompilerParams(vmem_limit_bytes=40 * 1024 * 1024),
+        name="prep_pull",
+    )(at, params, *received)
+
+
+def pull_rest_kernel(before_ref, geometry_ref, *refs, nc, coefs):
+    out_ref, flat = refs[-2:]
+    pulled(refs[:-2], geometry_ref, flat, out_ref, before_ref, nc=nc, coefs=coefs)
+
+
+def pull_rest(before, geometry, received, nc, coefs):
+    return pl.pallas_call(
+        partial(pull_rest_kernel, nc=nc, coefs=coefs),
+        in_specs=[vmem_spec()] * (2 + len(received)),
+        out_specs=vmem_spec(),
+        out_shape=jax.ShapeDtypeStruct(before.shape, F32),
+        scratch_shapes=[pltpu.VMEM((16, before.shape[1]), F32)],
         compiler_params=pltpu.CompilerParams(vmem_limit_bytes=40 * 1024 * 1024),
         name="pull_back",
-    )(at, params, *received)
+    )(before, geometry, *received)
 
 
 def hop_order(nd, first):
@@ -731,12 +765,12 @@
     me = jnp.stack([lax.axis_index("dev"), my_view, my_chip]).astype(jnp.int32)
     at = (my_view * nc + my_chip).astype(jnp.int32).reshape(1)
 
-    *packets, index, weights = send(me, cameras, view_basis, params, requests, nd, cap, rows)
-    received = list(packets)
+    *packets, index, weights, features = send(me, cameras, view_basis, params, requests, nd, cap, rows)
+    received = [None, *packets]
     for j in hop_order(nd, FORTH):
-        received[j] = lax.ppermute(packets[j], "dev", [(i, i ^ j) for i in range(nd)])
+        received[j] = lax.ppermute(packets[j - 1], "dev", [(i, i ^ j) for i in range(nd)])
     prepared = tile_indices(
-        me, packets[0], margin_blocks, depth_orders, tile_counts, tile_lists, nd, cap
+        me, features, index, margin_blocks, depth_orders, tile_counts, tile_lists, nd, cap
     )
     tiles, entries = margin_blocks.shape[3:]
     swapped = jnp.swapaxes(target, 3, 4)
@@ -757,7 +791,9 @@
             ]
             piece = shares[dv * nc + dc]
             arrived.append(piece if dv + dc == 0 else lax.ppermute(piece, ("view", "chip"), pairs))
-    grads = pull_back(at, params, arrived, nv, nc, view_basis.shape[1])
+    coefs = view_basis.shape[1]
+    before, geometry = pull_own(at, params, arrived[:nc], nv * nc, coefs)
+    grads = pull_rest(before, geometry, arrived[nc:], nc, coefs)
     return (grads, jnp.swapaxes(images, 3, 4))
 
 

time: 37.4 us -> 37.3 us (level)
    ppermute x3, waiting for transfers between devices: 1.37 us -> 1.83 us  [local(): back[j] = lax.ppermute(returns[j], 'dev', [(i, i ^ j) for i in range(nd)])]
    pallas_call x1 -> x2, Pallas kernels: 1.21 us -> 1.3 us  [the longest x1 1.02 us: pull_rest(): pl.pallas_call(partial(pull_rest_kernel, nc=nc, coefs=coefs), in_specs=[v...]
  transfers between devices with their start and end apart: 9 -> 9, of which waited for: 5 -> 5; matrix products, arithmetic and copies ran while one was open for 0% -> 0% of each run, Pallas kernels for 8% -> 9%
where the time goes in v5:
time: 37.3 us; the launch traced here: 37 us
  Pallas kernels  13.9 us (37%)
  starting transfers between devices  12.1 us (32%)
  waiting for transfers between devices  7.75 us (21%)
  local copies, waits for them, and re-layouts  2.51 us (7%)
  between operations  0.76 us (2%)
    pallas_call x1, Pallas kernels, render(): pl.pallas_call(partial(render_kernel, nd=nd, rows=rows, tiles=tiles, entr...  6.32 us
    ppermute x3, starting transfers between devices, local(): lax.ppermute(packets[j - 1], 'dev', [(i, i ^ j) for i in range(nd)])  5.68 us
    ppermute x3, starting transfers between devices, local(): back[j] = lax.ppermute(returns[j], 'dev', [(i, i ^ j) for i in range(nd)])  4.44 us
    ppermute x3, waiting for transfers between devices, local(): lax.ppermute(packets[j - 1], 'dev', [(i, i ^ j) for i in range(nd)])  2.99 us
    ppermute x3, waiting for transfers between devices, local(): lax.ppermute(piece, ('view', 'chip'), pairs)  2.94 us
    unnamed x20, local copies, waits for them, and re-layouts  2.51 us
    pallas_call x1, Pallas kernels, send(): pl.pallas_call(partial(send_kernel, nd=nd, cap=cap, rows=rows), in_specs=...  2.03 us
    ppermute x3, starting transfers between devices, local(): lax.ppermute(piece, ('view', 'chip'), pairs)  1.93 us
  transfers between devices with their start and end apart: 9, of which 5 were waited for; matrix products, arithmetic and copies ran while one was open for 0% of the time, Pallas kernels for 9%

profile of v5, /device:TPU:0, one launch (start us, length us, event | category | flops | bytes accessed | tf_op | source)
XLA Modules:
  0.0 37.0 jit_solution(13715040775782003824)
XLA Ops:
  0.6 0.0 copy-start.3
  0.6 0.0 copy-start.6
  0.7 0.0 copy-start.7
  0.7 0.1 pad_add_fusion.me_ref
  0.7 0.6 %copy-done.3 = s32[1,4,1,1,960]{4,3,2,1,0:T(1,128)S(1)} copy-done((s32[1,4,1,1,960]{4,3,2,1,0:T(1,128)S(1)}, s32[1,4,1,1,960]{4,3,2,1,0:T(1,128)}, u32[]{:S(2)}) %copy-start.3) | copy-done | bytes 15384
  1.3 0.0 copy-done.6
  1.4 0.0 copy-done.7
  1.4 0.0 copy-start
  1.4 1.2 %copy-done = f32[58,4096]{1,0:T(8,128)S(1)} copy-done((f32[58,4096]{1,0:T(8,128)S(1)}, f32[58,4096]{1,0:T(8,128)}, u32[]{:S(2)}) %copy-start) | copy-done | bytes 950296
  2.6 0.0 copy-start.4
  2.6 0.0 copy-start.5
  2.6 2.0 %project_gather.1 = (f32[9,8,128]{2,1,0:T(8,128)S(1)}, f32[9,8,128]{2,1,0:T(8,128)S(1)}, f32[9,8,128]{2,1,0:T(8,128)S(1)}, s32[32,128]{1,0:T(8,128)S(1)}, f32[8,128]{1,0:T(8,128)S(1)}, /*index=5*/f32[16,4096]{1,0:T(8,128)S(1)}) custom-call(s32[3]{0:T(128)S(1)} %pad_add_fusion.me_ref, f32[1,2,4]{2,1,0:T(2,128)S(1)} %copy-done.6, f32[1,16]{1,0:T(1,128)S(1)} %copy-done.7, ...), custom_call_target="tpu_custom_call" | custom-call | tf_op jit(solution)/shard_map/project_gather/pallas_call | solution.py:135
  4.6 3.1 %collective-permute-start.1 = (f32[9,8,128]{2,1,0:T(8,128)S(1)}, f32[9,8,128]{2,1,0:T(8,128)S(1)}, u32[]{:S(2)}, u32[]{:S(2)}) collective-permute-start(f32[9,8,128]{2,1,0:T(8,128)S(1)} %get-tuple-element.35), channel_id=1, source_target_pairs={{0,4},{4,0},{8,12},{12,8},{1,5},{5,1},{9,13},{13,9},{2,6},{6,2},{1... | collective-permute-start | bytes 110600 | tf_op jit(solution)/shard_map/ppermute | solution.py:771
  7.7 2.6 %collective-permute-start.2 = (f32[9,8,128]{2,1,0:T(8,128)S(1)}, f32[9,8,128]{2,1,0:T(8,128)S(1)}, u32[]{:S(2)}, u32[]{:S(2)}) collective-permute-start(f32[9,8,128]{2,1,0:T(8,128)S(1)} %get-tuple-element.36), channel_id=1, source_target_pairs={{0,8},{4,12},{8,0},{12,4},{1,9},{5,13},{9,1},{13,5},{2,10},{6,14},... | collective-permute-start | bytes 110600 | tf_op jit(solution)/shard_map/ppermute | solution.py:771
  10.3 0.0 collective-permute-start
  10.3 0.0 copy-start.8
  10.3 0.0 copy-start.9
  10.3 0.0 copy-done.4
  10.3 0.0 copy-done.5
  10.3 0.6 %copy-done.8 = s32[1,1,1,16]{3,2,1,0:T(1,128)S(1)} copy-done((s32[1,1,1,16]{3,2,1,0:T(1,128)S(1)}, s32[1,1,1,16]{3,2,1,0:T(1,128)}, u32[]{:S(2)}) %copy-start.8) | copy-done | bytes 88
  11.0 0.0 copy-done.9
  11.0 1.4 %prep_tiles.1 = (s32[16,256]{1,0:T(8,128)S(1)}, s32[16,256]{1,0:T(8,128)S(1)}, f32[16,256]{1,0:T(8,128)S(1)}, f32[2,16,128]{2,1,0:T(8,128)S(1)}, f32[9,16,256]{2,1,0:T(8,128)S(1)}) custom-call(s32[3]{0:T(128)S(1)} %pad_add_fusion.me_ref, f32[16,4096]{1,0:T(8,128)S(1)} %get-tuple-element.29.feat_ref, s32[32,128]{1,0:T(8,128)S(1)} %get-tuple-element.30.idx_ref, ...), custom_call_target="tpu_custom_call" | custom-call | tf_op jit(solution)/shard_map/prep_tiles/pallas_call | solution.py:254
  12.4 0.0 collective-permute-done.1.refs_0_
  12.4 0.9 %collective-permute-done.2.refs_1_ = f32[9,8,128]{2,1,0:T(8,128)S(1)} collective-permute-done((f32[9,8,128]{2,1,0:T(8,128)S(1)}, f32[9,8,128]{2,1,0:T(8,128)S(1)}, u32[]{:S(2)}, u32[]{:S(2)}) %collective-permute-start.2) | collective-permute-done | bytes 36896 | tf_op jit(solution)/shard_map/ppermute | solution.py:771
  13.2 0.0 copy-start.2
  13.2 0.7 %prep_gather.1.refs_5_ = f32[9,16,256]{2,1,0:T(8,128)S(1)} custom-call(f32[9,8,128]{2,1,0:T(8,128)S(1)} %collective-permute-done.1.refs_0_, f32[9,8,128]{2,1,0:T(8,128)S(1)} %collective-permute-done.2.refs_1_, s32[16,256]{1,0:T(8,128)S(1)} %get-tuple-element.31.refs_2_.refs_1_, s32[16,256]{1,0:T(8,128)S(1)} %get-tuple-element.32.refs_3_.refs_2_, ...), custom_call_target="tpu_custom_call" | custom-call | tf_op jit(solution)/shard_map/prep_gather/pallas_call | solution.py:295
  13.9 2.1 %collective-permute-done.refs_0_ = f32[9,8,128]{2,1,0:T(8,128)S(1)} collective-permute-done((f32[9,8,128]{2,1,0:T(8,128)S(1)}, f32[9,8,128]{2,1,0:T(8,128)S(1)}, u32[]{:S(2)}, u32[]{:S(2)}) %collective-permute-start) | collective-permute-done | bytes 36896 | tf_op jit(solution)/shard_map/ppermute | solution.py:771
  16.1 0.0 copy-done.2
  16.1 6.3 %render_tiles.1 = (f32[9,8,128]{2,1,0:T(8,128)S(1)}, f32[9,8,128]{2,1,0:T(8,128)S(1)}, f32[9,8,128]{2,1,0:T(8,128)S(1)}, f32[9,8,128]{2,1,0:T(8,128)S(1)}, f32[1,1,1,3,16,256]{5,4,3,2,1,0:T(8,128)}) custom-call(f32[9,8,128]{2,1,0:T(8,128)S(1)} %collective-permute-done.refs_0_, s32[16,256]{1,0:T(8,128)S(1)} %get-tuple-element.31.refs_2_.refs_1_, ...), custom_call_target="tpu_custom_call" | custom-call | tf_op jit(solution)/shard_map/render_tiles/pallas_call | solution.py:514
  22.4 0.1 collective-permute-start.5
  22.5 1.5 %collective-permute-start.3 = (f32[9,8,128]{2,1,0:T(8,128)S(1)}, f32[9,8,128]{2,1,0:T(8,128)S(1)}, u32[]{:S(2)}, u32[]{:S(2)}) collective-permute-start(f32[9,8,128]{2,1,0:T(8,128)S(1)} %get-tuple-element.38), channel_id=1, source_target_pairs={{0,8},{4,12},{8,0},{12,4},{1,9},{5,13},{9,1},{13,5},{2,10},{6,14},... | collective-permute-start | bytes 110600 | tf_op jit(solution)/shard_map/ppermute | solution.py:782
  24.0 2.9 %collective-permute-start.4 = (f32[9,8,128]{2,1,0:T(8,128)S(1)}, f32[9,8,128]{2,1,0:T(8,128)S(1)}, u32[]{:S(2)}, u32[]{:S(2)}) collective-permute-start(f32[9,8,128]{2,1,0:T(8,128)S(1)} %get-tuple-element.39), channel_id=1, source_target_pairs={{0,12},{4,8},{8,4},{12,0},{1,13},{5,9},{9,5},{13,1},{2,14},{6,10},... | collective-permute-start | bytes 110600 | tf_op jit(solution)/shard_map/ppermute | solution.py:782
  26.8 0.0 collective-permute-done.5.next_ref
  26.8 1.0 %prep_owner.1 = (bf16[16,4096]{1,0:T(8,128)(2,1)S(1)}, bf16[2048,256]{1,0:T(8,128)(2,1)S(1)}, bf16[2048,256]{1,0:T(8,128)(2,1)S(1)}, f32[288,256]{1,0:T(8,128)S(1)}) custom-call(f32[9,8,128]{2,1,0:T(8,128)S(1)} %get-tuple-element.40.own_ref, f32[9,8,128]{2,1,0:T(8,128)S(1)} %collective-permute-done.5.next_ref, s32[32,128]{1,0:T(8,128)S(1)} %get-tuple-element.30.idx_ref), custom_call_target="tpu_custom_call" | custom-call | tf_op jit(solution)/shard_map/prep_owner/pallas_call | solution.py:564
  27.9 0.0 collective-permute-done.3.refs_0_
  27.9 1.8 %collective-permute-done.4.refs_1_ = f32[9,8,128]{2,1,0:T(8,128)S(1)} collective-permute-done((f32[9,8,128]{2,1,0:T(8,128)S(1)}, f32[9,8,128]{2,1,0:T(8,128)S(1)}, u32[]{:S(2)}, u32[]{:S(2)}) %collective-permute-start.4) | collective-permute-done | bytes 36896 | tf_op jit(solution)/shard_map/ppermute | solution.py:782
  29.7 0.0 copy-start.1
  29.7 1.1 %owner_sums.1 = (f32[10,8,128]{2,1,0:T(8,128)S(1)}, f32[10,8,128]{2,1,0:T(8,128)S(1)}, f32[10,8,128]{2,1,0:T(8,128)S(1)}, f32[10,8,128]{2,1,0:T(8,128)S(1)}) custom-call(s32[3]{0:T(128)S(1)} %pad_add_fusion.me_ref, f32[9,8,128]{2,1,0:T(8,128)S(1)} %collective-permute-done.3.refs_0_, f32[9,8,128]{2,1,0:T(8,128)S(1)} %collective-permute-done.4.refs_1_, ...), custom_call_target="tpu_custom_call" | custom-call | tf_op jit(solution)/shard_map/owner_sums/pallas_call | solution.py:619
  30.8 0.1 collective-permute-start.6
  30.9 1.6 %collective-permute-start.7 = (f32[10,8,128]{2,1,0:T(8,128)S(1)}, f32[10,8,128]{2,1,0:T(8,128)S(1)}, u32[]{:S(2)}, u32[]{:S(2)}) collective-permute-start(f32[10,8,128]{2,1,0:T(8,128)S(1)} %get-tuple-element.51), channel_id=1, source_target_pairs={{0,2},{1,3},{2,0},{3,1},{4,6},{5,7},{6,4},{7,5},{8,10},{9,11},{10,... | collective-permute-start | bytes 122888 | tf_op jit(solution)/shard_map/ppermute | solution.py:793
  32.5 0.3 collective-permute-start.8
  32.8 0.0 collective-permute-done.6.refs_1_
  32.8 0.0 copy-done.1
  32.8 0.3 prep_pull.1
  33.1 1.9 %collective-permute-done.7.refs_0_ = f32[10,8,128]{2,1,0:T(8,128)S(1)} collective-permute-done((f32[10,8,128]{2,1,0:T(8,128)S(1)}, f32[10,8,128]{2,1,0:T(8,128)S(1)}, u32[]{:S(2)}, u32[]{:S(2)}) %collective-permute-start.7) | collective-permute-done | bytes 40992 | tf_op jit(solution)/shard_map/ppermute | solution.py:793
  35.0 1.0 %collective-permute-done.8.refs_1_ = f32[10,8,128]{2,1,0:T(8,128)S(1)} collective-permute-done((f32[10,8,128]{2,1,0:T(8,128)S(1)}, f32[10,8,128]{2,1,0:T(8,128)S(1)}, u32[]{:S(2)}, u32[]{:S(2)}) %collective-permute-start.8) | collective-permute-done | bytes 40992 | tf_op jit(solution)/shard_map/ppermute | solution.py:793
  36.0 1.0 %pull_back.1 = f32[58,1024]{1,0:T(8,128)} custom-call(f32[58,1024]{1,0:T(8,128)S(1)} %get-tuple-element.49.before_ref, f32[16,1024]{1,0:T(8,128)S(1)} %get-tuple-element.50.geometry_ref, f32[10,8,128]{2,1,0:T(8,128)S(1)} %collective-permute-done.7.refs_0_, f32[10,8,128]{2,1,0:T(8,128)S(1)} %collective-permute-done.8.refs_1_), custom_call_target="tpu_custom_call" | custom-call | tf_op jit(solution)/shard_map/pull_back/pallas_call | solution.py:731
Async XLA Ops:
  0.6 0.7 %copy-start.3 = (s32[1,4,1,1,960]{4,3,2,1,0:T(1,128)S(1)}, s32[1,4,1,1,960]{4,3,2,1,0:T(1,128)}, u32[]{:S(2)}) copy-start(s32[1,4,1,1,960]{4,3,2,1,0:T(1,128)} %req_ref.1) | copy-start | bytes 46084
  0.6 0.7 %copy-start.6 = (f32[1,2,4]{2,1,0:T(2,128)S(1)}, f32[1,2,4]{2,1,0:T(2,128)}, u32[]{:S(2)}) copy-start(f32[1,2,4]{2,1,0:T(2,128)} %cam_ref.1) | copy-start | bytes 100
  0.7 0.7 %copy-start.7 = (f32[1,16]{1,0:T(1,128)S(1)}, f32[1,16]{1,0:T(1,128)}, u32[]{:S(2)}) copy-start(f32[1,16]{1,0:T(1,128)} %basis_ref.1) | copy-start | bytes 196
  1.4 1.2 %copy-start = (f32[58,4096]{1,0:T(8,128)S(1)}, f32[58,4096]{1,0:T(8,128)}, u32[]{:S(2)}) copy-start(f32[58,4096]{1,0:T(8,128)} %params_ref.3) | copy-start | bytes 2850820
  2.6 7.7 %copy-start.4 = (s32[1,1,1,16,256]{4,3,2,1,0:T(8,128)S(1)}, s32[1,1,1,16,256]{4,3,2,1,0:T(8,128)}, u32[]{:S(2)}) copy-start(s32[1,1,1,16,256]{4,3,2,1,0:T(8,128)} %blocks_ref.1) | copy-start | bytes 49156
  2.6 7.7 %copy-start.5 = (s32[1,1,1,16,256]{4,3,2,1,0:T(8,128)S(1)}, s32[1,1,1,16,256]{4,3,2,1,0:T(8,128)}, u32[]{:S(2)}) copy-start(s32[1,1,1,16,256]{4,3,2,1,0:T(8,128)} %orders_ref.1) | copy-start | bytes 49156
  4.6 7.8 %collective-permute-start.1 = (f32[9,8,128]{2,1,0:T(8,128)S(1)}, f32[9,8,128]{2,1,0:T(8,128)S(1)}, u32[]{:S(2)}, u32[]{:S(2)}) collective-permute-start(f32[9,8,128]{2,1,0:T(8,128)S(1)} %get-tuple-element.35), channel_id=1, source_target_pairs={{0,4},{4,0},{8,12},{12,8},{1,5},{5,1},{9,13},{13,9},{2,6},{6,2},{1... | collective-permute-start | bytes 110600 | tf_op jit(solution)/shard_map/ppermute | solution.py:771
  7.7 5.5 %collective-permute-start.2 = (f32[9,8,128]{2,1,0:T(8,128)S(1)}, f32[9,8,128]{2,1,0:T(8,128)S(1)}, u32[]{:S(2)}, u32[]{:S(2)}) collective-permute-start(f32[9,8,128]{2,1,0:T(8,128)S(1)} %get-tuple-element.36), channel_id=1, source_target_pairs={{0,8},{4,12},{8,0},{12,4},{1,9},{5,13},{9,1},{13,5},{2,10},{6,14},... | collective-permute-start | bytes 110600 | tf_op jit(solution)/shard_map/ppermute | solution.py:771
  10.3 5.8 %collective-permute-start = (f32[9,8,128]{2,1,0:T(8,128)S(1)}, f32[9,8,128]{2,1,0:T(8,128)S(1)}, u32[]{:S(2)}, u32[]{:S(2)}) collective-permute-start(f32[9,8,128]{2,1,0:T(8,128)S(1)} %get-tuple-element.28), channel_id=1, source_target_pairs={{0,12},{4,8},{8,4},{12,0},{1,13},{5,9},{9,5},{13,1},{2,14},{6,10},... | collective-permute-start | bytes 110600 | tf_op jit(solution)/shard_map/ppermute | solution.py:771
  10.3 0.7 %copy-start.8 = (s32[1,1,1,16]{3,2,1,0:T(1,128)S(1)}, s32[1,1,1,16]{3,2,1,0:T(1,128)}, u32[]{:S(2)}) copy-start(s32[1,1,1,16]{3,2,1,0:T(1,128)} %counts_ref.1) | copy-start | bytes 196
  10.3 0.7 %copy-start.9 = (s32[1,1,1,16]{3,2,1,0:T(1,128)S(1)}, s32[1,1,1,16]{3,2,1,0:T(1,128)}, u32[]{:S(2)}) copy-start(s32[1,1,1,16]{3,2,1,0:T(1,128)} %ids_ref.1) | copy-start | bytes 196
  13.2 2.8 %copy-start.2 = (f32[1,1,1,16,3,256]{5,3,4,2,1,0:T(8,128)S(1)}, f32[1,1,1,16,3,256]{5,3,4,2,1,0:T(8,128)}, u32[]{:S(2)}) copy-start(f32[1,1,1,16,3,256]{5,3,4,2,1,0:T(8,128)} %param.17) | copy-start | bytes 147460
  22.4 4.5 %collective-permute-start.5 = (f32[9,8,128]{2,1,0:T(8,128)S(1)}, f32[9,8,128]{2,1,0:T(8,128)S(1)}, u32[]{:S(2)}, u32[]{:S(2)}) collective-permute-start(f32[9,8,128]{2,1,0:T(8,128)S(1)} %get-tuple-element.41), channel_id=1, source_target_pairs={{0,4},{4,0},{8,12},{12,8},{1,5},{5,1},{9,13},{13,9},{2,6},{6,2},{1... | collective-permute-start | bytes 110600 | tf_op jit(solution)/shard_map/ppermute | solution.py:782
  22.5 5.4 %collective-permute-start.3 = (f32[9,8,128]{2,1,0:T(8,128)S(1)}, f32[9,8,128]{2,1,0:T(8,128)S(1)}, u32[]{:S(2)}, u32[]{:S(2)}) collective-permute-start(f32[9,8,128]{2,1,0:T(8,128)S(1)} %get-tuple-element.38), channel_id=1, source_target_pairs={{0,8},{4,12},{8,0},{12,4},{1,9},{5,13},{9,1},{13,5},{2,10},{6,14},... | collective-permute-start | bytes 110600 | tf_op jit(solution)/shard_map/ppermute | solution.py:782
  24.0 5.8 %collective-permute-start.4 = (f32[9,8,128]{2,1,0:T(8,128)S(1)}, f32[9,8,128]{2,1,0:T(8,128)S(1)}, u32[]{:S(2)}, u32[]{:S(2)}) collective-permute-start(f32[9,8,128]{2,1,0:T(8,128)S(1)} %get-tuple-element.39), channel_id=1, source_target_pairs={{0,12},{4,8},{8,4},{12,0},{1,13},{5,9},{9,5},{13,1},{2,14},{6,10},... | collective-permute-start | bytes 110600 | tf_op jit(solution)/shard_map/ppermute | solution.py:782
  29.7 3.0 %copy-start.1 = (f32[58,4096]{1,0:T(8,128)S(1)}, f32[58,4096]{1,0:T(8,128)}, u32[]{:S(2)}) copy-start(f32[58,4096]{1,0:T(8,128)} %params_ref.3) | copy-start | bytes 2850820
  30.8 1.9 %collective-permute-start.6 = (f32[10,8,128]{2,1,0:T(8,128)S(1)}, f32[10,8,128]{2,1,0:T(8,128)S(1)}, u32[]{:S(2)}, u32[]{:S(2)}) collective-permute-start(f32[10,8,128]{2,1,0:T(8,128)S(1)} %get-tuple-element.48), channel_id=1, source_target_pairs={{0,1},{1,0},{2,3},{3,2},{4,5},{5,4},{6,7},{7,6},{8,9},{9,8},{10,11... | collective-permute-start | bytes 122888 | tf_op jit(solution)/shard_map/ppermute | solution.py:793
  30.9 4.1 %collective-permute-start.7 = (f32[10,8,128]{2,1,0:T(8,128)S(1)}, f32[10,8,128]{2,1,0:T(8,128)S(1)}, u32[]{:S(2)}, u32[]{:S(2)}) collective-permute-start(f32[10,8,128]{2,1,0:T(8,128)S(1)} %get-tuple-element.51), channel_id=1, source_target_pairs={{0,2},{1,3},{2,0},{3,1},{4,6},{5,7},{6,4},{7,5},{8,10},{9,11},{10,... | collective-permute-start | bytes 122888 | tf_op jit(solution)/shard_map/ppermute | solution.py:793
  32.5 3.5 %collective-permute-start.8 = (f32[10,8,128]{2,1,0:T(8,128)S(1)}, f32[10,8,128]{2,1,0:T(8,128)S(1)}, u32[]{:S(2)}, u32[]{:S(2)}) collective-permute-start(f32[10,8,128]{2,1,0:T(8,128)S(1)} %get-tuple-element.52), channel_id=1, source_target_pairs={{0,3},{1,2},{2,1},{3,0},{4,7},{5,6},{6,5},{7,4},{8,11},{9,10},{10,... | collective-permute-start | bytes 122888 | tf_op jit(solution)/shard_map/ppermute | solution.py:793

commit v6 on v5

--- a/solution.py
+++ b/solution.py
@@ -17,7 +17,7 @@
 F32 = jnp.float32
 BF16 = jnp.bfloat16
 FEATS = 9
-FORTH = (1, 2, 3)
+FORTH = (3, 2, 1)
 BACK = (1, 2, 3)
 GROUP = 8
 
@@ -36,8 +36,7 @@
 
 
 def send_kernel(me_ref, cam_ref, basis_ref, params_ref, req_ref, *refs, nd, cap, rows):
-    outs = refs[: nd - 1]
-    idx_out, w_out, feat, w_scr = refs[nd - 1 :]
+    far_out, idx_out, w_out, feat, w_scr = refs
     me = me_ref[0]
     width = params_ref.shape[1]
     coefs = basis_ref.shape[-1]
@@ -100,15 +99,35 @@
             idx_out[j * rows + i : j * rows + i + 1, 0:size] = req_ref[
                 0, dest, 0, 0:1, i * LANES : i * LANES + size
             ]
-    total = nd * rows
-    step = 8 if rows % 8 == 0 else total - rows
-    for first in range(rows, total, step):
-        gathered = gather_features(feat, idx_out[first : first + step, :])
+    far = (nd - 1) * rows
+    size = max(rows, 8)
+    gathered = gather_features(feat, idx_out[nd * rows - size :, :])
+    for f in range(FEATS):
+        far_out[f] = gathered[f][far - nd * rows + size :, :]
+
+
+def near_kernel(feat_ref, idx_ref, *outs):
+    rows = outs[0].shape[1]
+    total = len(outs) * rows
+    step = 8 if rows % 8 == 0 else total
+    for first in range(0, total, step):
+        gathered = gather_features(feat_ref, idx_ref[rows + first : rows + first + step, :])
+        size = min(rows, step)
         for f in range(FEATS):
-            for n in range(0, step, rows if step > rows else step):
+            for n in range(0, step, size):
                 j, i = divmod(first + n, rows)
-                size = min(rows, step)
-                outs[j - 1][f, i : i + size, :] = gathered[f][n : n + size, :]
+                outs[j][f, i : i + size, :] = gathered[f][n : n + size, :]
+
+
+def gather_near(features, index, nd, rows):
+    return pl.pallas_call(
+        near_kernel,
+        in_specs=[vmem_spec()] * 2,
+        out_specs=[vmem_spec()] * (nd - 2),
+        out_shape=[jax.ShapeDtypeStruct((FEATS, rows, LANES), F32)] * (nd - 2),
+        compiler_params=pltpu.CompilerParams(vmem_limit_bytes=40 * 1024 * 1024),
+        name="prep_near",
+    )(features, index)
 
 
 def gather_features(feat, index):
@@ -135,9 +154,9 @@
     return pl.pallas_call(
         partial(send_kernel, nd=nd, cap=cap, rows=rows),
         in_specs=[smem_spec()] + [vmem_spec()] * 4,
-        out_specs=[vmem_spec()] * (nd + 2),
-        out_shape=[jax.ShapeDtypeStruct((FEATS, rows, LANES), F32)] * (nd - 1)
-        + [
+        out_specs=[vmem_spec()] * 4,
+        out_shape=[
+            jax.ShapeDtypeStruct((FEATS, rows, LANES), F32),
             jax.ShapeDtypeStruct((nd * rows, LANES), jnp.int32),
             jax.ShapeDtypeStruct((8, LANES), F32),
             jax.ShapeDtypeStruct((16, params.shape[1]), F32),
@@ -765,7 +784,8 @@
     me = jnp.stack([lax.axis_index("dev"), my_view, my_chip]).astype(jnp.int32)
     at = (my_view * nc + my_chip).astype(jnp.int32).reshape(1)
 
-    *packets, index, weights, features = send(me, cameras, view_basis, params, requests, nd, cap, rows)
+    far, index, weights, features = send(me, cameras, view_basis, params, requests, nd, cap, rows)
+    packets = [*gather_near(features, index, nd, rows), far]
     received = [None, *packets]
     for j in hop_order(nd, FORTH):
         received[j] = lax.ppermute(packets[j - 1], "dev", [(i, i ^ j) for i in range(nd)])

time: 37.3 us -> 36.9 us (0.989)
  local copies, waits for them, and re-layouts: 2.51 us -> 1.87 us
    pallas_call x0 -> x1, Pallas kernels: none -> 0.69 us  [gather_near(): pl.pallas_call(near_kernel, in_specs=[vmem_spec()] * 2, out_specs=[vmem_s...]
    pallas_call x1, Pallas kernels: 2.03 us -> 1.38 us  [send(): pl.pallas_call(partial(send_kernel, nd=nd, cap=cap, rows=rows), in_specs=...]
    unnamed x20, local copies, waits for them, and re-layouts: 2.51 us -> 1.87 us
    ppermute x3, waiting for transfers between devices: 2.99 us -> 3.63 us  [local(): lax.ppermute(packets[j - 1], 'dev', [(i, i ^ j) for i in range(nd)])]
    ppermute x3, waiting for transfers between devices: 1.83 us -> 1.37 us  [local(): back[j] = lax.ppermute(returns[j], 'dev', [(i, i ^ j) for i in range(nd)])]
where the time goes in v6:
time: 36.9 us; the launch traced here: 36.6 us
  Pallas kernels  13.9 us (38%)
  starting transfers between devices  12.1 us (33%)
  waiting for transfers between devices  7.93 us (21%)
  local copies, waits for them, and re-layouts  1.87 us (5%)
  between operations  0.79 us (2%)
    pallas_call x1, Pallas kernels, render(): pl.pallas_call(partial(render_kernel, nd=nd, rows=rows, tiles=tiles, entr...  6.32 us
    ppermute x3, starting transfers between devices, local(): lax.ppermute(packets[j - 1], 'dev', [(i, i ^ j) for i in range(nd)])  5.68 us
    ppermute x3, starting transfers between devices, local(): back[j] = lax.ppermute(returns[j], 'dev', [(i, i ^ j) for i in range(nd)])  4.44 us
    ppermute x3, waiting for transfers between devices, local(): lax.ppermute(packets[j - 1], 'dev', [(i, i ^ j) for i in range(nd)])  3.63 us
    ppermute x3, waiting for transfers between devices, local(): lax.ppermute(piece, ('view', 'chip'), pairs)  2.94 us
    ppermute x3, starting transfers between devices, local(): lax.ppermute(piece, ('view', 'chip'), pairs)  1.93 us
    unnamed x20, local copies, waits for them, and re-layouts  1.87 us
    pallas_call x1, Pallas kernels, tile_indices(): pl.pallas_call(partial(index_kernel, nd=nd, cap=cap), in_specs=[smem_spec...  1.4 us
  transfers between devices with their start and end apart: 9, of which 5 were waited for; matrix products, arithmetic and copies ran while one was open for 0% of the time, Pallas kernels for 9%

profile of v6, /device:TPU:0, one launch (start us, length us, event | category | flops | bytes accessed | tf_op | source)
XLA Modules:
  0.0 36.6 jit_solution(4803626451100250636)
XLA Ops:
  0.6 0.0 copy-start.3
  0.6 0.0 copy-start.6
  0.7 0.0 copy-start.7
  0.7 0.1 pad_add_fusion.me_ref
  0.7 0.6 %copy-done.3 = s32[1,4,1,1,960]{4,3,2,1,0:T(1,128)S(1)} copy-done((s32[1,4,1,1,960]{4,3,2,1,0:T(1,128)S(1)}, s32[1,4,1,1,960]{4,3,2,1,0:T(1,128)}, u32[]{:S(2)}) %copy-start.3) | copy-done | bytes 15384
  1.3 0.0 copy-done.6
  1.4 0.0 copy-done.7
  1.4 0.0 copy-start
  1.4 1.2 %copy-done = f32[58,4096]{1,0:T(8,128)S(1)} copy-done((f32[58,4096]{1,0:T(8,128)S(1)}, f32[58,4096]{1,0:T(8,128)}, u32[]{:S(2)}) %copy-start) | copy-done | bytes 950296
  2.6 1.4 %project_gather.1 = (f32[9,8,128]{2,1,0:T(8,128)S(1)}, s32[32,128]{1,0:T(8,128)S(1)}, f32[8,128]{1,0:T(8,128)S(1)}, f32[16,4096]{1,0:T(8,128)S(1)}) custom-call(s32[3]{0:T(128)S(1)} %pad_add_fusion.me_ref, f32[1,2,4]{2,1,0:T(2,128)S(1)} %copy-done.6, f32[1,16]{1,0:T(1,128)S(1)} %copy-done.7, f32[58,4096]{1,0:T(8,128)S(1)} %copy-done, ...), custom_call_target="tpu_custom_call" | custom-call | tf_op jit(solution)/shard_map/project_gather/pallas_call | solution.py:154
  4.0 0.0 copy-start.4
  4.0 0.0 copy-start.5
  4.0 0.7 %prep_near.1 = (f32[9,8,128]{2,1,0:T(8,128)S(1)}, f32[9,8,128]{2,1,0:T(8,128)S(1)}) custom-call(f32[16,4096]{1,0:T(8,128)S(1)} %get-tuple-element.29.feat_ref, s32[32,128]{1,0:T(8,128)S(1)} %get-tuple-element.30.idx_ref), custom_call_target="tpu_custom_call" | custom-call | tf_op jit(solution)/shard_map/prep_near/pallas_call | solution.py:123
  4.7 3.1 %collective-permute-start.1 = (f32[9,8,128]{2,1,0:T(8,128)S(1)}, f32[9,8,128]{2,1,0:T(8,128)S(1)}, u32[]{:S(2)}, u32[]{:S(2)}) collective-permute-start(f32[9,8,128]{2,1,0:T(8,128)S(1)} %get-tuple-element.35), channel_id=1, source_target_pairs={{0,4},{4,0},{8,12},{12,8},{1,5},{5,1},{9,13},{13,9},{2,6},{6,2},{1... | collective-permute-start | bytes 110600 | tf_op jit(solution)/shard_map/ppermute | solution.py:791
  7.8 0.0 copy-start.8
  7.8 0.0 copy-start.9
  7.8 2.6 %collective-permute-start.2 = (f32[9,8,128]{2,1,0:T(8,128)S(1)}, f32[9,8,128]{2,1,0:T(8,128)S(1)}, u32[]{:S(2)}, u32[]{:S(2)}) collective-permute-start(f32[9,8,128]{2,1,0:T(8,128)S(1)} %get-tuple-element.36), channel_id=1, source_target_pairs={{0,8},{4,12},{8,0},{12,4},{1,9},{5,13},{9,1},{13,5},{2,10},{6,14},... | collective-permute-start | bytes 110600 | tf_op jit(solution)/shard_map/ppermute | solution.py:791
  10.4 0.0 collective-permute-start
  10.4 0.0 copy-done.4
  10.4 0.0 copy-done.5
  10.4 0.0 copy-done.8
  10.4 0.0 copy-done.9
  10.4 1.4 %prep_tiles.1 = (s32[16,256]{1,0:T(8,128)S(1)}, s32[16,256]{1,0:T(8,128)S(1)}, f32[16,256]{1,0:T(8,128)S(1)}, f32[2,16,128]{2,1,0:T(8,128)S(1)}, f32[9,16,256]{2,1,0:T(8,128)S(1)}) custom-call(s32[3]{0:T(128)S(1)} %pad_add_fusion.me_ref, f32[16,4096]{1,0:T(8,128)S(1)} %get-tuple-element.29.feat_ref, s32[32,128]{1,0:T(8,128)S(1)} %get-tuple-element.30.idx_ref, ...), custom_call_target="tpu_custom_call" | custom-call | tf_op jit(solution)/shard_map/prep_tiles/pallas_call | solution.py:273
  11.8 0.0 collective-permute-done.1.refs_0_
  11.8 1.5 %collective-permute-done.2.refs_1_ = f32[9,8,128]{2,1,0:T(8,128)S(1)} collective-permute-done((f32[9,8,128]{2,1,0:T(8,128)S(1)}, f32[9,8,128]{2,1,0:T(8,128)S(1)}, u32[]{:S(2)}, u32[]{:S(2)}) %collective-permute-start.2) | collective-permute-done | bytes 36896 | tf_op jit(solution)/shard_map/ppermute | solution.py:791
  13.3 0.0 copy-start.2
  13.3 0.7 %prep_gather.1.refs_5_ = f32[9,16,256]{2,1,0:T(8,128)S(1)} custom-call(f32[9,8,128]{2,1,0:T(8,128)S(1)} %collective-permute-done.1.refs_0_, f32[9,8,128]{2,1,0:T(8,128)S(1)} %collective-permute-done.2.refs_1_, s32[16,256]{1,0:T(8,128)S(1)} %get-tuple-element.31.refs_2_.refs_1_, s32[16,256]{1,0:T(8,128)S(1)} %get-tuple-element.32.refs_3_.refs_2_, ...), custom_call_target="tpu_custom_call" | custom-call | tf_op jit(solution)/shard_map/prep_gather/pallas_call | solution.py:314
  14.0 2.1 %collective-permute-done.refs_0_ = f32[9,8,128]{2,1,0:T(8,128)S(1)} collective-permute-done((f32[9,8,128]{2,1,0:T(8,128)S(1)}, f32[9,8,128]{2,1,0:T(8,128)S(1)}, u32[]{:S(2)}, u32[]{:S(2)}) %collective-permute-start) | collective-permute-done | bytes 36896 | tf_op jit(solution)/shard_map/ppermute | solution.py:791
  16.1 0.0 copy-done.2
  16.1 6.3 %render_tiles.1 = (f32[9,8,128]{2,1,0:T(8,128)S(1)}, f32[9,8,128]{2,1,0:T(8,128)S(1)}, f32[9,8,128]{2,1,0:T(8,128)S(1)}, f32[9,8,128]{2,1,0:T(8,128)S(1)}, f32[1,1,1,3,16,256]{5,4,3,2,1,0:T(8,128)}) custom-call(f32[9,8,128]{2,1,0:T(8,128)S(1)} %collective-permute-done.refs_0_, s32[16,256]{1,0:T(8,128)S(1)} %get-tuple-element.31.refs_2_.refs_1_, ...), custom_call_target="tpu_custom_call" | custom-call | tf_op jit(solution)/shard_map/render_tiles/pallas_call | solution.py:533
  22.5 0.1 collective-permute-start.5
  22.5 1.0 %collective-permute-start.3 = (f32[9,8,128]{2,1,0:T(8,128)S(1)}, f32[9,8,128]{2,1,0:T(8,128)S(1)}, u32[]{:S(2)}, u32[]{:S(2)}) collective-permute-start(f32[9,8,128]{2,1,0:T(8,128)S(1)} %get-tuple-element.38), channel_id=1, source_target_pairs={{0,8},{4,12},{8,0},{12,4},{1,9},{5,13},{9,1},{13,5},{2,10},{6,14},... | collective-permute-start | bytes 110600 | tf_op jit(solution)/shard_map/ppermute | solution.py:802
  23.6 3.3 %collective-permute-start.4 = (f32[9,8,128]{2,1,0:T(8,128)S(1)}, f32[9,8,128]{2,1,0:T(8,128)S(1)}, u32[]{:S(2)}, u32[]{:S(2)}) collective-permute-start(f32[9,8,128]{2,1,0:T(8,128)S(1)} %get-tuple-element.39), channel_id=1, source_target_pairs={{0,12},{4,8},{8,4},{12,0},{1,13},{5,9},{9,5},{13,1},{2,14},{6,10},... | collective-permute-start | bytes 110600 | tf_op jit(solution)/shard_map/ppermute | solution.py:802
  26.9 0.0 collective-permute-done.5.next_ref
  26.9 1.0 %prep_owner.1 = (bf16[16,4096]{1,0:T(8,128)(2,1)S(1)}, bf16[2048,256]{1,0:T(8,128)(2,1)S(1)}, bf16[2048,256]{1,0:T(8,128)(2,1)S(1)}, f32[288,256]{1,0:T(8,128)S(1)}) custom-call(f32[9,8,128]{2,1,0:T(8,128)S(1)} %get-tuple-element.40.own_ref, f32[9,8,128]{2,1,0:T(8,128)S(1)} %collective-permute-done.5.next_ref, s32[32,128]{1,0:T(8,128)S(1)} %get-tuple-element.30.idx_ref), custom_call_target="tpu_custom_call" | custom-call | tf_op jit(solution)/shard_map/prep_owner/pallas_call | solution.py:583
  28.0 0.0 collective-permute-done.3.refs_0_
  28.0 1.4 %collective-permute-done.4.refs_1_ = f32[9,8,128]{2,1,0:T(8,128)S(1)} collective-permute-done((f32[9,8,128]{2,1,0:T(8,128)S(1)}, f32[9,8,128]{2,1,0:T(8,128)S(1)}, u32[]{:S(2)}, u32[]{:S(2)}) %collective-permute-start.4) | collective-permute-done | bytes 36896 | tf_op jit(solution)/shard_map/ppermute | solution.py:802
  29.4 0.0 copy-start.1
  29.4 1.1 %owner_sums.1 = (f32[10,8,128]{2,1,0:T(8,128)S(1)}, f32[10,8,128]{2,1,0:T(8,128)S(1)}, f32[10,8,128]{2,1,0:T(8,128)S(1)}, f32[10,8,128]{2,1,0:T(8,128)S(1)}) custom-call(s32[3]{0:T(128)S(1)} %pad_add_fusion.me_ref, f32[9,8,128]{2,1,0:T(8,128)S(1)} %collective-permute-done.3.refs_0_, f32[9,8,128]{2,1,0:T(8,128)S(1)} %collective-permute-done.4.refs_1_, ...), custom_call_target="tpu_custom_call" | custom-call | tf_op jit(solution)/shard_map/owner_sums/pallas_call | solution.py:638
  30.5 0.1 collective-permute-start.6
  30.5 1.6 %collective-permute-start.7 = (f32[10,8,128]{2,1,0:T(8,128)S(1)}, f32[10,8,128]{2,1,0:T(8,128)S(1)}, u32[]{:S(2)}, u32[]{:S(2)}) collective-permute-start(f32[10,8,128]{2,1,0:T(8,128)S(1)} %get-tuple-element.51), channel_id=1, source_target_pairs={{0,2},{1,3},{2,0},{3,1},{4,6},{5,7},{6,4},{7,5},{8,10},{9,11},{10,... | collective-permute-start | bytes 122888 | tf_op jit(solution)/shard_map/ppermute | solution.py:813
  32.1 0.3 collective-permute-start.8
  32.4 0.0 collective-permute-done.6.refs_1_
  32.4 0.0 copy-done.1
  32.4 0.3 prep_pull.1
  32.7 1.9 %collective-permute-done.7.refs_0_ = f32[10,8,128]{2,1,0:T(8,128)S(1)} collective-permute-done((f32[10,8,128]{2,1,0:T(8,128)S(1)}, f32[10,8,128]{2,1,0:T(8,128)S(1)}, u32[]{:S(2)}, u32[]{:S(2)}) %collective-permute-start.7) | collective-permute-done | bytes 40992 | tf_op jit(solution)/shard_map/ppermute | solution.py:813
  34.6 1.0 %collective-permute-done.8.refs_1_ = f32[10,8,128]{2,1,0:T(8,128)S(1)} collective-permute-done((f32[10,8,128]{2,1,0:T(8,128)S(1)}, f32[10,8,128]{2,1,0:T(8,128)S(1)}, u32[]{:S(2)}, u32[]{:S(2)}) %collective-permute-start.8) | collective-permute-done | bytes 40992 | tf_op jit(solution)/shard_map/ppermute | solution.py:813
  35.6 1.0 %pull_back.1 = f32[58,1024]{1,0:T(8,128)} custom-call(f32[58,1024]{1,0:T(8,128)S(1)} %get-tuple-element.49.before_ref, f32[16,1024]{1,0:T(8,128)S(1)} %get-tuple-element.50.geometry_ref, f32[10,8,128]{2,1,0:T(8,128)S(1)} %collective-permute-done.7.refs_0_, f32[10,8,128]{2,1,0:T(8,128)S(1)} %collective-permute-done.8.refs_1_), custom_call_target="tpu_custom_call" | custom-call | tf_op jit(solution)/shard_map/pull_back/pallas_call | solution.py:750
Async XLA Ops:
  0.6 0.7 %copy-start.3 = (s32[1,4,1,1,960]{4,3,2,1,0:T(1,128)S(1)}, s32[1,4,1,1,960]{4,3,2,1,0:T(1,128)}, u32[]{:S(2)}) copy-start(s32[1,4,1,1,960]{4,3,2,1,0:T(1,128)} %req_ref.1) | copy-start | bytes 46084
  0.6 0.7 %copy-start.6 = (f32[1,2,4]{2,1,0:T(2,128)S(1)}, f32[1,2,4]{2,1,0:T(2,128)}, u32[]{:S(2)}) copy-start(f32[1,2,4]{2,1,0:T(2,128)} %cam_ref.1) | copy-start | bytes 100
  0.7 0.7 %copy-start.7 = (f32[1,16]{1,0:T(1,128)S(1)}, f32[1,16]{1,0:T(1,128)}, u32[]{:S(2)}) copy-start(f32[1,16]{1,0:T(1,128)} %basis_ref.1) | copy-start | bytes 196
  1.4 1.2 %copy-start = (f32[58,4096]{1,0:T(8,128)S(1)}, f32[58,4096]{1,0:T(8,128)}, u32[]{:S(2)}) copy-start(f32[58,4096]{1,0:T(8,128)} %params_ref.3) | copy-start | bytes 2850820
  4.0 6.4 %copy-start.4 = (s32[1,1,1,16,256]{4,3,2,1,0:T(8,128)S(1)}, s32[1,1,1,16,256]{4,3,2,1,0:T(8,128)}, u32[]{:S(2)}) copy-start(s32[1,1,1,16,256]{4,3,2,1,0:T(8,128)} %blocks_ref.1) | copy-start | bytes 49156
  4.0 6.4 %copy-start.5 = (s32[1,1,1,16,256]{4,3,2,1,0:T(8,128)S(1)}, s32[1,1,1,16,256]{4,3,2,1,0:T(8,128)}, u32[]{:S(2)}) copy-start(s32[1,1,1,16,256]{4,3,2,1,0:T(8,128)} %orders_ref.1) | copy-start | bytes 49156
  4.7 7.1 %collective-permute-start.1 = (f32[9,8,128]{2,1,0:T(8,128)S(1)}, f32[9,8,128]{2,1,0:T(8,128)S(1)}, u32[]{:S(2)}, u32[]{:S(2)}) collective-permute-start(f32[9,8,128]{2,1,0:T(8,128)S(1)} %get-tuple-element.35), channel_id=1, source_target_pairs={{0,4},{4,0},{8,12},{12,8},{1,5},{5,1},{9,13},{13,9},{2,6},{6,2},{1... | collective-permute-start | bytes 110600 | tf_op jit(solution)/shard_map/ppermute | solution.py:791
  7.8 2.6 %copy-start.8 = (s32[1,1,1,16]{3,2,1,0:T(1,128)S(1)}, s32[1,1,1,16]{3,2,1,0:T(1,128)}, u32[]{:S(2)}) copy-start(s32[1,1,1,16]{3,2,1,0:T(1,128)} %counts_ref.1) | copy-start | bytes 196
  7.8 2.6 %copy-start.9 = (s32[1,1,1,16]{3,2,1,0:T(1,128)S(1)}, s32[1,1,1,16]{3,2,1,0:T(1,128)}, u32[]{:S(2)}) copy-start(s32[1,1,1,16]{3,2,1,0:T(1,128)} %ids_ref.1) | copy-start | bytes 196
  7.8 5.5 %collective-permute-start.2 = (f32[9,8,128]{2,1,0:T(8,128)S(1)}, f32[9,8,128]{2,1,0:T(8,128)S(1)}, u32[]{:S(2)}, u32[]{:S(2)}) collective-permute-start(f32[9,8,128]{2,1,0:T(8,128)S(1)} %get-tuple-element.36), channel_id=1, source_target_pairs={{0,8},{4,12},{8,0},{12,4},{1,9},{5,13},{9,1},{13,5},{2,10},{6,14},... | collective-permute-start | bytes 110600 | tf_op jit(solution)/shard_map/ppermute | solution.py:791
  10.4 5.8 %collective-permute-start = (f32[9,8,128]{2,1,0:T(8,128)S(1)}, f32[9,8,128]{2,1,0:T(8,128)S(1)}, u32[]{:S(2)}, u32[]{:S(2)}) collective-permute-start(f32[9,8,128]{2,1,0:T(8,128)S(1)} %get-tuple-element.28), channel_id=1, source_target_pairs={{0,12},{4,8},{8,4},{12,0},{1,13},{5,9},{9,5},{13,1},{2,14},{6,10},... | collective-permute-start | bytes 110600 | tf_op jit(solution)/shard_map/ppermute | solution.py:791
  13.3 2.8 %copy-start.2 = (f32[1,1,1,16,3,256]{5,3,4,2,1,0:T(8,128)S(1)}, f32[1,1,1,16,3,256]{5,3,4,2,1,0:T(8,128)}, u32[]{:S(2)}) copy-start(f32[1,1,1,16,3,256]{5,3,4,2,1,0:T(8,128)} %param.17) | copy-start | bytes 147460
  22.5 4.5 %collective-permute-start.5 = (f32[9,8,128]{2,1,0:T(8,128)S(1)}, f32[9,8,128]{2,1,0:T(8,128)S(1)}, u32[]{:S(2)}, u32[]{:S(2)}) collective-permute-start(f32[9,8,128]{2,1,0:T(8,128)S(1)} %get-tuple-element.41), channel_id=1, source_target_pairs={{0,4},{4,0},{8,12},{12,8},{1,5},{5,1},{9,13},{13,9},{2,6},{6,2},{1... | collective-permute-start | bytes 110600 | tf_op jit(solution)/shard_map/ppermute | solution.py:802
  22.5 5.4 %collective-permute-start.3 = (f32[9,8,128]{2,1,0:T(8,128)S(1)}, f32[9,8,128]{2,1,0:T(8,128)S(1)}, u32[]{:S(2)}, u32[]{:S(2)}) collective-permute-start(f32[9,8,128]{2,1,0:T(8,128)S(1)} %get-tuple-element.38), channel_id=1, source_target_pairs={{0,8},{4,12},{8,0},{12,4},{1,9},{5,13},{9,1},{13,5},{2,10},{6,14},... | collective-permute-start | bytes 110600 | tf_op jit(solution)/shard_map/ppermute | solution.py:802
  23.6 5.8 %collective-permute-start.4 = (f32[9,8,128]{2,1,0:T(8,128)S(1)}, f32[9,8,128]{2,1,0:T(8,128)S(1)}, u32[]{:S(2)}, u32[]{:S(2)}) collective-permute-start(f32[9,8,128]{2,1,0:T(8,128)S(1)} %get-tuple-element.39), channel_id=1, source_target_pairs={{0,12},{4,8},{8,4},{12,0},{1,13},{5,9},{9,5},{13,1},{2,14},{6,10},... | collective-permute-start | bytes 110600 | tf_op jit(solution)/shard_map/ppermute | solution.py:802
  29.4 3.0 %copy-start.1 = (f32[58,4096]{1,0:T(8,128)S(1)}, f32[58,4096]{1,0:T(8,128)}, u32[]{:S(2)}) copy-start(f32[58,4096]{1,0:T(8,128)} %params_ref.3) | copy-start | bytes 2850820
  30.5 1.9 %collective-permute-start.6 = (f32[10,8,128]{2,1,0:T(8,128)S(1)}, f32[10,8,128]{2,1,0:T(8,128)S(1)}, u32[]{:S(2)}, u32[]{:S(2)}) collective-permute-start(f32[10,8,128]{2,1,0:T(8,128)S(1)} %get-tuple-element.48), channel_id=1, source_target_pairs={{0,1},{1,0},{2,3},{3,2},{4,5},{5,4},{6,7},{7,6},{8,9},{9,8},{10,11... | collective-permute-start | bytes 122888 | tf_op jit(solution)/shard_map/ppermute | solution.py:813
  30.5 4.1 %collective-permute-start.7 = (f32[10,8,128]{2,1,0:T(8,128)S(1)}, f32[10,8,128]{2,1,0:T(8,128)S(1)}, u32[]{:S(2)}, u32[]{:S(2)}) collective-permute-start(f32[10,8,128]{2,1,0:T(8,128)S(1)} %get-tuple-element.51), channel_id=1, source_target_pairs={{0,2},{1,3},{2,0},{3,1},{4,6},{5,7},{6,4},{7,5},{8,10},{9,11},{10,... | collective-permute-start | bytes 122888 | tf_op jit(solution)/shard_map/ppermute | solution.py:813
  32.1 3.5 %collective-permute-start.8 = (f32[10,8,128]{2,1,0:T(8,128)S(1)}, f32[10,8,128]{2,1,0:T(8,128)S(1)}, u32[]{:S(2)}, u32[]{:S(2)}) collective-permute-start(f32[10,8,128]{2,1,0:T(8,128)S(1)} %get-tuple-element.52), channel_id=1, source_target_pairs={{0,3},{1,2},{2,1},{3,0},{4,7},{5,6},{6,5},{7,4},{8,11},{9,10},{10,... | collective-permute-start | bytes 122888 | tf_op jit(solution)/shard_map/ppermute | solution.py:813
